TPU v7x, 128 devices: a whole 4x4x4 slice. The times are simulated.
128 devices in a mesh: gx: 8 (over z, core), gy: 16 (over x, y).
Axes of the slice: x: 4, y: 4, z: 4, core: 2. Of those that a mesh axis runs over, the one named last changes fastest.
Arguments:
- residual: float32 [256, 8192], P('gy', 'gx'), may hold values from -60 to 60
- norm_gain: float32 [8192], P('gx'), may hold values from 0.1 to 1.9
- w_gate: bfloat16 [8192, 32768], P('gx', 'gy'), may hold values from -0.0625 to 0.0625
- w_up: bfloat16 [8192, 32768], P('gx', 'gy'), may hold values from -0.0625 to 0.0625
- w_query: bfloat16 [8192, 8192], P('gx', 'gy'), may hold values from -0.0625 to 0.0625
- w_keyval: bfloat16 [8192, 512], P('gx', 'gy'), may hold values from -0.19824219 to 0.19824219
- w_down: bfloat16 [32768, 8192], P('gy', 'gx'), may hold values from -0.03125 to 0.03125
- w_out: bfloat16 [8192, 8192], P('gy', 'gx'), may hold values from -0.0625 to 0.0625
- cache_keys: bfloat16 [256, 2048, 256], P(('gx', 'gy')), may hold values from -500 to 500
- cache_values: bfloat16 [256, 2048, 256], P(('gx', 'gy')), may hold values from -6 to 6
- lengths: int32 [256], P(('gx', 'gy')), may hold values from 1 to 2048, as said below
Outputs:
- final_stream: float32 [256, 8192], P('gy', 'gx')
Inputs may be any that keep to these rules, and one draw needn't show every extreme that they name: `lengths`: row 0 uses all 2048 positions.
All inputs are finite; a program needn't handle non-finite values.
Results may differ from a plain program's by a relative error of at most 0.008.
Values may be sent and summed in bfloat16 or wider, within the bound.
No kernel may reach another device: no remote copies, remote signals or barrier semaphores. Data moves between devices by JAX's collectives and lax.ppermute only.
A program may use at most 64 MiB of HBM per device.

v0:
```python
import math

import jax
import jax.numpy as jnp
from jax import lax
from jax.sharding import PartitionSpec as P

D = 8192
HEADS = 32
DH = 256
STEPS = 2


EPS = 1e-06


def attend(query_rows, key_list, value_list, cache_keys, cache_values, lengths):
    count = query_rows.shape[0]
    heads = query_rows.reshape(count, HEADS, DH)
    scale = 1.0 / math.sqrt(DH)
    old_s = (
        jnp.einsum("rhd,rpd->rhp", heads, cache_keys, preferred_element_type=jnp.float32) * scale
    )
    places = lax.broadcasted_iota(jnp.int32, (count, 1, cache_keys.shape[1]), 2)
    old_s = jnp.where(places < lengths[:, None, None], old_s, -jnp.inf)
    new_k = jnp.stack(key_list, 1)
    new_v = jnp.stack(value_list, 1)
    new_s = jnp.einsum("rhd,rtd->rht", heads, new_k, preferred_element_type=jnp.float32) * scale
    top = jnp.maximum(jnp.max(old_s, axis=2), jnp.max(new_s, axis=2))
    old_e = jnp.exp(old_s - top[..., None])
    new_e = jnp.exp(new_s - top[..., None])
    total = jnp.sum(old_e, axis=2) + jnp.sum(new_e, axis=2)
    old_w = (old_e / total[..., None]).astype(jnp.bfloat16)
    new_w = (new_e / total[..., None]).astype(jnp.bfloat16)
    result = jnp.einsum("rhp,rpd->rhd", old_w, cache_values, preferred_element_type=jnp.float32)
    result = result + jnp.einsum("rht,rtd->rhd", new_w, new_v, preferred_element_type=jnp.float32)
    return result.astype(jnp.bfloat16).reshape(count, HEADS * DH)


def body(
    residual,
    norm_gain,
    w_gate,
    w_up,
    w_query,
    w_keyval,
    w_down,
    w_out,
    cache_keys,
    cache_values,
    lengths,
):
    stream = residual
    ff_cols = w_gate.shape[1]
    q_cols = w_query.shape[1]
    key_list = []
    value_list = []
    for step in range(STEPS):
        squares = lax.psum(jnp.sum(stream * stream, axis=1), "gx")
        normed = (stream * lax.rsqrt(squares / D + EPS)[:, None] * norm_gain[None, :]).astype(
            jnp.bfloat16
        )
        gathered = lax.all_gather(normed, "gy", axis=0, tiled=True)
        summed = lax.psum_scatter(
            jnp.concatenate(
                [
                    jnp.concatenate(
                        [
                            jnp.dot(gathered, w_gate, preferred_element_type=jnp.float32),
                            jnp.dot(gathered, w_up, preferred_element_type=jnp.float32),
                        ],
                        1,
                    ),
                    jnp.concatenate(
                        [
                            jnp.dot(gathered, w_query, preferred_element_type=jnp.float32),
                            jnp.dot(gathered, w_keyval, preferred_element_type=jnp.float32),
                        ],
                        1,
                    ),
                ],
                1,
            ),
            "gx",
            scatter_dimension=0,
            tiled=True,
        )
        hidden = (jax.nn.silu(summed[:, :ff_cols]) * summed[:, ff_cols : 2 * ff_cols]).astype(
            jnp.bfloat16
        )
        mine = summed[:, 2 * ff_cols :]
        query = mine[:, :q_cols].astype(jnp.bfloat16)
        keyval = mine[:, q_cols:].astype(jnp.bfloat16)
        query_rows, keyval_rows = (
            lax.all_to_all(query, "gy", split_axis=0, concat_axis=1, tiled=True),
            lax.all_to_all(keyval, "gy", split_axis=0, concat_axis=1, tiled=True),
        )
        key_list.append(keyval_rows[:, :DH])
        value_list.append(keyval_rows[:, DH:])
        attended = attend(query_rows, key_list, value_list, cache_keys, cache_values, lengths)
        head_block = lax.all_to_all(attended, "gy", split_axis=1, concat_axis=0, tiled=True)
        hidden_all, heads_all = (
            lax.all_gather(hidden, "gx", axis=0, tiled=True),
            lax.all_gather(head_block, "gx", axis=0, tiled=True),
        )
        stream = stream + lax.psum_scatter(
            jnp.dot(hidden_all, w_down, preferred_element_type=jnp.float32)
            + jnp.dot(heads_all, w_out, preferred_element_type=jnp.float32),
            "gy",
            scatter_dimension=0,
            tiled=True,
        )
    return stream


def solution(mesh):
    in_specs = (
        P("gy", "gx"),
        P("gx"),
        P("gx", "gy"),
        P("gx", "gy"),
        P("gx", "gy"),
        P("gx", "gy"),
        P("gy", "gx"),
        P("gy", "gx"),
        P(("gx", "gy"), None, None),
        P(("gx", "gy"), None, None),
        P(("gx", "gy")),
    )
    out_specs = P("gy", "gx")
    return jax.shard_map(body, mesh=mesh, in_specs=in_specs, out_specs=out_specs, check_vma=False)
```

profile of v0, /device:TPU:0, one launch (start us, length us, event | category | flops | bytes accessed | tf_op | source)
XLA Modules:
  0.0 442.3 jit_solution(11265895847960648058)
XLA Ops:
  6.5 1.1 multiply_reduce_fusion.1
  7.6 16.0 %psum.14 = f32[16]{0:T(128)S(1)} all-reduce(f32[16]{0:T(128)S(1)} %multiply_reduce_fusion.1), channel_id=1, replica_groups=mesh['gx'=8,'gy'=16] {'gx'}, use_global_device_ids=true, to_apply=%region_1.0 | all-reduce | flops 16 | bytes 128 | tf_op jit(solution)/shard_map/psum | solution.py:59
  23.6 1.1 multiply_convert_fusion.1
  24.7 24.4 %all_gather.18 = bf16[256,1024]{1,0:T(8,128)(2,1)S(1)} all-gather(bf16[16,1024]{1,0:T(8,128)(2,1)S(1)} %multiply_convert_fusion.1), channel_id=1, replica_groups=mesh['gx'=8,'gy'=16] {'gy'}, dimensions={0}, use_global_device_ids=true | all-gather | bytes 557056 | tf_op jit(solution)/shard_map/all_gather | solution.py:63
  49.1 3.5 fusion.31
  52.6 1.3 fusion.32
  53.9 0.5 fusion.33
  54.3 0.3 fusion.34
  54.6 2.5 pad_maximum_fusion
  57.2 36.4 %reduce-scatter.5.cloned.1.call-done = f32[32,4640]{1,0:T(8,128)} async-done(((f32[256,4640]{1,0:T(8,128)}), f32[32,4640]{1,0:T(8,128)}) %reduce-scatter.5.cloned.1.call-update) | async-done | bytes 593936 | tf_op jit(solution)/shard_map/reduce_scatter | solution.py:64
  93.5 1.1 convert.14
  94.7 0.6 slice.61
  95.2 6.8 %all-to-all-start.1 = ((bf16[16,2,32]{2,1,0:T(2,128)(2,1)}), bf16[16,2,32]{2,1,0:T(2,128)(2,1)S(1)}, u32[]{:S(2)}, u32[]{:S(2)}) async-start(bf16[16,2,32]{2,1,0:T(2,128)(2,1)} %bitcast.1), calls=%async_computation.2 | async-start | bytes 16384 | tf_op jit(solution)/shard_map/all_to_all | solution.py:96
  102.0 0.0 all-gather.3.cloned.1.call-start
  102.1 1.8 fusion.8
  103.9 0.1 iota_compare_fusion
  104.0 0.6 all_to_all.80
  104.6 5.0 %all-to-all-done.1 = bf16[16,2,32]{2,1,0:T(2,128)(2,1)S(1)} async-done(((bf16[16,2,32]{2,1,0:T(2,128)(2,1)}), bf16[16,2,32]{2,1,0:T(2,128)(2,1)S(1)}, u32[]{:S(2)}, u32[]{:S(2)}) %all-to-all-start.1) | async-done | bytes 2080 | tf_op jit(solution)/shard_map/all_to_all | solution.py:96
  109.6 3.5 all-to-all-start
  113.1 0.0 reduce-scatter.7.cloned.1.call-start
  113.1 0.1 all_to_all.86
  113.2 0.6 slice_bitcast_fusion.2
  113.8 6.8 %all-to-all-done = bf16[16,2,512]{2,1,0:T(2,128)(2,1)S(1)} async-done(((bf16[16,2,512]{2,1,0:T(2,128)(2,1)}), bf16[16,2,512]{2,1,0:T(2,128)(2,1)S(1)}, u32[]{:S(2)}, u32[]{:S(2)}) %all-to-all-start) | async-done | bytes 32800 | tf_op jit(solution)/shard_map/all_to_all | solution.py:95
  120.7 0.1 fusion.19
  120.8 0.8 fusion.28
  121.6 0.2 fusion.4
  121.9 2.2 fusion.2
  124.1 10.7 %all_to_all.108 = bf16[2,16,512]{2,0,1:T(2,128)(2,1)S(1)} all-to-all(bf16[2,16,512]{2,0,1:T(2,128)(2,1)S(1)} %copy.43), channel_id=1, replica_groups=mesh['gx'=8,'gy'=16] {'gy'}, dimensions={1} | all-to-all | bytes 65536 | tf_op jit(solution)/shard_map/all_to_all | solution.py:101
  134.9 12.8 %all_gather.20 = bf16[256,512]{1,0:T(8,128)(2,1)S(1)} all-gather(bf16[32,512]{1,0:T(8,128)(2,1)S(1)} %all_to_all.90), channel_id=1, replica_groups=mesh['gx'=8,'gy'=16] {'gx'}, dimensions={0}, use_global_device_ids=true | all-gather | bytes 294912 | tf_op jit(solution)/shard_map/all_gather | solution.py:104
  147.7 3.8 fusion.35
  151.6 1.4 convolution_add_fusion.1
  153.1 0.0 reduce-scatter.9.cloned.1.call-start
  153.1 69.0 %reduce-scatter.7.cloned.1.call-done = f32[16,1024]{1,0:T(8,128)} async-done(((f32[256,1024]{1,0:T(8,128)}), f32[16,1024]{1,0:T(8,128)}) %reduce-scatter.7.cloned.1.call-update) | async-done | bytes 65552 | tf_op jit(solution)/shard_map/reduce_scatter | solution.py:106
  222.1 1.0 multiply_reduce_fusion
  223.0 13.2 %psum.15 = f32[16]{0:T(128)S(1)} all-reduce(f32[16]{0:T(128)S(1)} %get-tuple-element.5), channel_id=1, replica_groups=mesh['gx'=8,'gy'=16] {'gx'}, use_global_device_ids=true, to_apply=%region_7.8 | all-reduce | flops 16 | bytes 128 | tf_op jit(solution)/shard_map/psum | solution.py:59
  236.3 0.1 multiply_convert_fusion
  236.4 22.9 %all_gather.21 = bf16[256,1024]{1,0:T(8,128)(2,1)S(1)} all-gather(bf16[16,1024]{1,0:T(8,128)(2,1)S(1)} %multiply_convert_fusion), channel_id=1, replica_groups=mesh['gx'=8,'gy'=16] {'gy'}, dimensions={0}, use_global_device_ids=true | all-gather | bytes 557056 | tf_op jit(solution)/shard_map/all_gather | solution.py:63
  259.3 3.5 fusion.36
  262.8 1.3 fusion.37
  264.1 0.4 fusion.38
  264.5 0.3 fusion.39
  264.8 2.5 pad_maximum_fusion.1
  267.4 36.0 %reduce-scatter.9.cloned.1.call-done = f32[32,4640]{1,0:T(8,128)} async-done(((f32[256,4640]{1,0:T(8,128)}), f32[32,4640]{1,0:T(8,128)}) %reduce-scatter.9.cloned.1.call-update) | async-done | bytes 593936 | tf_op jit(solution)/shard_map/reduce_scatter | solution.py:64
  303.4 1.8 fusion.7
  305.1 1.1 convert.17
  306.3 0.6 slice.67
  306.8 6.8 %all-to-all-start.4 = ((bf16[16,2,32]{2,1,0:T(2,128)(2,1)}), bf16[16,2,32]{2,1,0:T(2,128)(2,1)S(1)}, u32[]{:S(2)}, u32[]{:S(2)}) async-start(bf16[16,2,32]{2,1,0:T(2,128)(2,1)} %bitcast.9), calls=%async_computation.7 | async-start | bytes 16384 | tf_op jit(solution)/shard_map/all_to_all | solution.py:96
  313.7 0.6 all_to_all.91
  314.3 6.9 %all-to-all-done.4 = bf16[16,2,32]{2,1,0:T(2,128)(2,1)S(1)} async-done(((bf16[16,2,32]{2,1,0:T(2,128)(2,1)}), bf16[16,2,32]{2,1,0:T(2,128)(2,1)S(1)}, u32[]{:S(2)}, u32[]{:S(2)}) %all-to-all-start.4) | async-done | bytes 2080 | tf_op jit(solution)/shard_map/all_to_all | solution.py:96
  321.2 3.5 all-to-all-start.3
  324.7 0.2 reduce-scatter.11.cloned.1.call-start
  324.9 0.1 all_to_all.97
  325.1 7.2 %all-to-all-done.3 = bf16[16,2,512]{2,1,0:T(2,128)(2,1)S(1)} async-done(((bf16[16,2,512]{2,1,0:T(2,128)(2,1)}), bf16[16,2,512]{2,1,0:T(2,128)(2,1)S(1)}, u32[]{:S(2)}, u32[]{:S(2)}) %all-to-all-start.3) | async-done | bytes 32800 | tf_op jit(solution)/shard_map/all_to_all | solution.py:95
  332.3 0.1 fusion.30
  332.4 0.8 fusion.29
  333.3 0.2 fusion.5
  333.5 2.1 fusion.6
  335.6 0.2 fusion.3
  335.9 10.9 %all_to_all.109 = bf16[2,16,512]{2,0,1:T(2,128)(2,1)S(1)} all-to-all(bf16[2,16,512]{2,0,1:T(2,128)(2,1)S(1)} %copy.51), channel_id=1, replica_groups=mesh['gx'=8,'gy'=16] {'gy'}, dimensions={1} | all-to-all | bytes 65536 | tf_op jit(solution)/shard_map/all_to_all | solution.py:101
  346.8 12.8 %all_gather.23 = bf16[256,512]{1,0:T(8,128)(2,1)S(1)} all-gather(bf16[32,512]{1,0:T(8,128)(2,1)S(1)} %all_to_all.101), channel_id=1, replica_groups=mesh['gx'=8,'gy'=16] {'gx'}, dimensions={0}, use_global_device_ids=true | all-gather | bytes 294912 | tf_op jit(solution)/shard_map/all_gather | solution.py:104
  359.7 3.8 fusion.40
  363.4 1.4 convolution_add_fusion
  364.9 69.0 %reduce-scatter.11.cloned.1.call-done = f32[16,1024]{1,0:T(8,128)} async-done(((f32[256,1024]{1,0:T(8,128)}), f32[16,1024]{1,0:T(8,128)}) %reduce-scatter.11.cloned.1.call-update) | async-done | bytes 65552 | tf_op jit(solution)/shard_map/reduce_scatter | solution.py:106
  433.9 1.5 add.66
  (60 shorter events, 0.5 us)
Async XLA Ops:
  6.5 114.3 %copy-start = (bf16[2,2048,256]{2,1,0:T(8,128)(2,1)S(1)}, bf16[2,2048,256]{2,1,0:T(8,128)(2,1)}, u32[]{:S(2)}) copy-start(bf16[2,2048,256]{2,1,0:T(8,128)(2,1)} %param.19) | copy-start | bytes 6291460
  6.5 87.0 %reduce-scatter.5.cloned.1.call-start = ((), (), s32[]{:S(2)}) async-start(), calls=%async_computation.10 | async-start | bytes 5455872 | tf_op jit(solution)/shard_map/reduce_scatter | solution.py:64
  23.6 28.9 %copy-start.10 = (bf16[1024,2048]{1,0:T(8,128)(2,1)S(1)}, bf16[1024,2048]{1,0:T(8,128)(2,1)}, u32[]{:S(2)}) copy-start(bf16[1024,2048]{1,0:T(8,128)(2,1)} %param.14) | copy-start | bytes 12582916
  52.6 1.3 copy-start.1
  52.6 1.8 copy-start.5
  57.2 46.7 %copy-start.9 = (s32[2]{0:T(128)S(1)}, s32[2]{0:T(128)}, u32[]{:S(2)}) copy-start(s32[2]{0:T(128)} %param.21) | copy-start | bytes 28
  95.2 14.3 %all-to-all-start.1 = ((bf16[16,2,32]{2,1,0:T(2,128)(2,1)}), bf16[16,2,32]{2,1,0:T(2,128)(2,1)S(1)}, u32[]{:S(2)}, u32[]{:S(2)}) async-start(bf16[16,2,32]{2,1,0:T(2,128)(2,1)} %bitcast.1), calls=%async_computation.2 | async-start | bytes 16384 | tf_op jit(solution)/shard_map/all_to_all | solution.py:96
  102.0 45.7 %all-gather.3.cloned.1.call-start = ((), (), s32[]{:S(2)}) async-start(), calls=%async_computation.11 | async-start | bytes 1179648 | tf_op jit(solution)/shard_map/all_gather | solution.py:103
  109.6 11.1 %all-to-all-start = ((bf16[16,2,512]{2,1,0:T(2,128)(2,1)}), bf16[16,2,512]{2,1,0:T(2,128)(2,1)S(1)}, u32[]{:S(2)}, u32[]{:S(2)}) async-start(bf16[16,2,512]{2,1,0:T(2,128)(2,1)} %all_to_all.80), calls=%async_computation.1 | async-start | bytes 65536 | tf_op jit(solution)/shard_map/all_to_all | solution.py:95
  113.1 109.0 %reduce-scatter.7.cloned.1.call-start = ((), (), s32[]{:S(2)}) async-start(), calls=%async_computation.12 | async-start | bytes 1114112 | tf_op jit(solution)/shard_map/reduce_scatter | solution.py:106
  147.7 74.4 %copy-start.4 = (f32[16,1024]{1,0:T(8,128)S(1)}, f32[16,1024]{1,0:T(8,128)}, u32[]{:S(2)}) copy-start(f32[16,1024]{1,0:T(8,128)} %param.11) | copy-start | bytes 196612
  147.7 3.8 copy-start.2
  151.6 84.7 %copy-start.7 = (f32[1024]{0:T(1024)S(1)}, f32[1024]{0:T(1024)}, u32[]{:S(2)}) copy-start(f32[1024]{0:T(1024)} %param.12) | copy-start | bytes 12292
  153.1 150.3 %reduce-scatter.9.cloned.1.call-start = ((), (), s32[]{:S(2)}) async-start(), calls=%async_computation.13 | async-start | bytes 5455872 | tf_op jit(solution)/shard_map/reduce_scatter | solution.py:64
  236.3 26.5 %copy-start.11 = (bf16[1024,2048]{1,0:T(8,128)(2,1)S(1)}, bf16[1024,2048]{1,0:T(8,128)(2,1)}, u32[]{:S(2)}) copy-start(bf16[1024,2048]{1,0:T(8,128)(2,1)} %param.14) | copy-start | bytes 12582916
  262.8 1.7 copy-start.6
  267.3 46.3 %copy-start.8 = (bf16[2,1,256]{2,0,1:T(2,128)(2,1)S(1)}, bf16[2,1,256]{2,0,1:T(2,128)(2,1)}, u32[]{:S(2)}) copy-start(bf16[2,1,256]{2,0,1:T(2,128)(2,1)} %get-tuple-element.10) | copy-start | bytes 3076
  267.4 92.3 %all-gather.5.cloned.1.call-start = ((), (), s32[]{:S(2)}) async-start(), calls=%async_computation.14 | async-start | bytes 1179648 | tf_op jit(solution)/shard_map/all_gather | solution.py:103
  306.8 14.4 %all-to-all-start.4 = ((bf16[16,2,32]{2,1,0:T(2,128)(2,1)}), bf16[16,2,32]{2,1,0:T(2,128)(2,1)S(1)}, u32[]{:S(2)}, u32[]{:S(2)}) async-start(bf16[16,2,32]{2,1,0:T(2,128)(2,1)} %bitcast.9), calls=%async_computation.7 | async-start | bytes 16384 | tf_op jit(solution)/shard_map/all_to_all | solution.py:96
  321.2 11.1 %all-to-all-start.3 = ((bf16[16,2,512]{2,1,0:T(2,128)(2,1)}), bf16[16,2,512]{2,1,0:T(2,128)(2,1)S(1)}, u32[]{:S(2)}, u32[]{:S(2)}) async-start(bf16[16,2,512]{2,1,0:T(2,128)(2,1)} %all_to_all.91), calls=%async_computation.6 | async-start | bytes 65536 | tf_op jit(solution)/shard_map/all_to_all | solution.py:95
  324.7 109.2 %reduce-scatter.11.cloned.1.call-start = ((), (), s32[]{:S(2)}) async-start(), calls=%async_computation.15 | async-start | bytes 1114112 | tf_op jit(solution)/shard_map/reduce_scatter | solution.py:106
  335.6 27.8 %copy-start.3 = (bf16[512,1024]{1,0:T(8,128)(2,1)S(1)}, bf16[512,1024]{1,0:T(8,128)(2,1)}, u32[]{:S(2)}) copy-start(bf16[512,1024]{1,0:T(8,128)(2,1)} %param.18) | copy-start | bytes 3145732
Sparse Core Ops, SparseCore 0:
  57.3 36.1 reduce-scatter.4
  104.7 22.6 all-gather.2
  153.2 68.8 reduce-scatter.6
  267.5 35.8 reduce-scatter.8
  305.3 22.6 all-gather.4
  365.0 68.8 reduce-scatter.10
where the time goes:
time: 443 us; the launch traced here: 442 us
  waiting for transfers between devices  236 us (53%)
  blocking collectives  124 us (28%)
  matrix products  27.8 us (6%)
  starting transfers between devices  20.9 us (5%)
  other arithmetic  16.7 us (4%)
  between operations  13.8 us (3%)
    reduce_scatter x2, waiting for transfers between devices, body(): lax.psum_scatter(jnp.dot(hidden_all, w_down, preferred_element_type=jnp.f...  138 us
    reduce_scatter x2, waiting for transfers between devices, body(): lax.psum_scatter(jnp.concatenate([jnp.concatenate([jnp.dot(gathered, w_ga...  72.3 us
    all_gather x2, blocking collectives, body(): gathered = lax.all_gather(normed, 'gy', axis=0, tiled=True)  47.3 us
    psum x2, blocking collectives, body(): squares = lax.psum(jnp.sum(stream * stream, axis=1), 'gx')  29.2 us
    all_gather x2, blocking collectives, body(): lax.all_gather(head_block, 'gx', axis=0, tiled=True)  25.7 us
    all_to_all x2, blocking collectives, body(): lax.all_to_all(attended, 'gy', split_axis=1, concat_axis=0, tiled=True)  21.6 us
    all_to_all x2, waiting for transfers between devices, body(): lax.all_to_all(query, 'gy', split_axis=0, concat_axis=1, tiled=True)  14 us
    all_to_all x2, starting transfers between devices, body(): lax.all_to_all(keyval, 'gy', split_axis=0, concat_axis=1, tiled=True)  13.6 us
  transfers between devices with their start and end apart: 10, of which 8 were waited for; matrix products, arithmetic and copies ran while one was open for 3% of the time, Pallas kernels for 0%

commit v1 on v0

v1 whole, which is shorter than its diff:
```python
import jax
import jax.numpy as jnp
from jax import lax
from jax.sharding import PartitionSpec as P

D = 8192
HEADS = 32
DH = 256
STEPS = 2
EPS = 1e-06
F32 = jnp.float32
BF16 = jnp.bfloat16


def dot32(a, b):
    return jnp.dot(a, b, preferred_element_type=F32)


def square_columns(squares, width):
    high = lax.reduce_precision(squares, 8, 7)
    low = squares - high
    pair = jnp.stack([high, low], axis=1)
    return jnp.pad(pair, ((0, 0), (0, width - 2))).astype(BF16)


def row_scale(columns):
    return lax.rsqrt((columns[..., 0:1] + columns[..., 1:2]) / D + EPS)


def attend(heads, key_list, value_list, cache_keys, cache_values, lengths):
    count = heads.shape[0]
    old_s = jnp.einsum("rhd,rpd->rhp", heads, cache_keys, preferred_element_type=F32)
    places = lax.broadcasted_iota(jnp.int32, (count, 1, cache_keys.shape[1]), 2)
    old_s = jnp.where(places < lengths[:, None, None], old_s, -jnp.inf)
    new_k = jnp.stack(key_list, 1)
    new_v = jnp.stack(value_list, 1)
    new_s = jnp.einsum("rhd,rtd->rht", heads, new_k, preferred_element_type=F32)
    top = jnp.maximum(jnp.max(old_s, axis=2), jnp.max(new_s, axis=2))
    old_e = jnp.exp(old_s - top[..., None])
    new_e = jnp.exp(new_s - top[..., None])
    total = jnp.sum(old_e, axis=2) + jnp.sum(new_e, axis=2)
    old_w = (old_e / total[..., None]).astype(BF16)
    new_w = (new_e / total[..., None]).astype(BF16)
    result = jnp.einsum("rhp,rpd->rhd", old_w, cache_values, preferred_element_type=F32)
    result = result + jnp.einsum("rht,rtd->rhd", new_w, new_v, preferred_element_type=F32)
    return result.astype(BF16)


def make_body(gx, gy):
    gz = gx // 2
    core_swap = [(n, n ^ 1) for n in range(gx)]
    z_groups = [[2 * z + c for z in range(gz)] for c in range(2)]

    def exchange(parts, axis, groups=None):
        return lax.all_to_all(
            parts, axis, split_axis=0, concat_axis=0, tiled=False, axis_index_groups=groups
        )

    def body(
        residual,
        norm_gain,
        w_gate,
        w_up,
        w_query,
        w_keyval,
        w_down,
        w_out,
        cache_keys,
        cache_values,
        lengths,
    ):
        stream = residual
        own_rows, width = residual.shape
        rows = own_rows * gy
        ff_cols = w_gate.shape[1]
        half = ff_cols // 2
        q_cols = w_query.shape[1]
        kv_cols = w_keyval.shape[1]
        cache_rows = cache_keys.shape[0]
        first = lax.axis_index("gx") % 2 == 0
        inverse_gain = 1.0 / norm_gain
        key_list = []
        value_list = []
        for step in range(STEPS):
            scaled = (stream * norm_gain[None, :]).astype(BF16)
            gathered = exchange(jnp.broadcast_to(scaled[None], (gy, own_rows, width)), "gy")
            gathered = gathered.reshape(rows, width)

            plain = gathered.astype(F32) * inverse_gain[None, :]
            squares = square_columns(jnp.sum(plain * plain, axis=1), 128)
            query_part = dot32(gathered, w_query).astype(BF16)
            keyval_part = dot32(gathered, w_keyval).astype(BF16)
            packed = jnp.concatenate(
                [query_part, keyval_part, squares[:, : 128 - kv_cols]], axis=1
            )
            packed = exchange(packed.reshape(gx * gy, cache_rows, q_cols + 128), ("gx", "gy"))

            gate_part = dot32(gathered, w_gate).astype(BF16)
            up_part = dot32(gathered, w_up).astype(BF16)
            keep = jnp.concatenate(
                [
                    jnp.where(first, gate_part[:, :half], gate_part[:, half:]),
                    jnp.where(first, up_part[:, :half], up_part[:, half:]),
                    squares,
                ],
                axis=1,
            )
            give = jnp.concatenate(
                [
                    jnp.where(first, gate_part[:, half:], gate_part[:, :half]),
                    jnp.where(first, up_part[:, half:], up_part[:, :half]),
                    squares,
                ],
                axis=1,
            )
            other = lax.ppermute(give, "gx", core_swap)
            pair = (keep.astype(F32) + other.astype(F32)).astype(BF16)
            pair = exchange(pair.reshape(gz, rows // gz, 2 * half + 128), "gx", z_groups)

            mine = jnp.sum(
                packed.reshape(gx, gy, cache_rows, q_cols + 128).astype(F32), axis=0
            )
            mine = mine * row_scale(mine[0, :, q_cols + kv_cols :])[None]
            query = mine[:, :, :q_cols].astype(BF16).transpose(1, 0, 2)
            query = query.reshape(cache_rows, HEADS, DH) * BF16(DH**-0.5)
            keyval = mine[:, :, q_cols : q_cols + kv_cols].astype(BF16).transpose(1, 0, 2)
            keyval = keyval.reshape(cache_rows, 2 * DH)
            key_list.append(keyval[:, :DH])
            value_list.append(keyval[:, DH:])
            attended = attend(query, key_list, value_list, cache_keys, cache_values, lengths)
            blocks = attended.reshape(cache_rows, gy, q_cols).transpose(1, 0, 2)
            blocks = jnp.broadcast_to(blocks[None], (gx, gy, cache_rows, q_cols))
            heads_all = exchange(blocks.reshape(gx * gy, cache_rows, q_cols), ("gx", "gy"))
            heads_all = heads_all.reshape(rows, q_cols)

            summed = jnp.sum(pair.astype(F32), axis=0)
            scale = row_scale(summed[:, 2 * half :])
            gate = summed[:, :half] * scale
            up = summed[:, half : 2 * half] * scale
            hidden = (jax.nn.silu(gate) * up).astype(BF16)
            hidden = exchange(
                jnp.broadcast_to(hidden[None], (gz,) + hidden.shape), "gx", z_groups
            ).reshape(rows, half)
            hidden_other = lax.ppermute(hidden, "gx", core_swap)
            hidden_all = jnp.concatenate(
                [
                    jnp.where(first, hidden, hidden_other),
                    jnp.where(first, hidden_other, hidden),
                ],
                axis=1,
            )
            delta = (dot32(hidden_all, w_down) + dot32(heads_all, w_out)).astype(BF16)
            delta = exchange(delta.reshape(gy, own_rows, width), "gy")
            stream = stream + jnp.sum(delta.astype(F32), axis=0)
        return stream

    return body


def solution(mesh):
    in_specs = (
        P("gy", "gx"),
        P("gx"),
        P("gx", "gy"),
        P("gx", "gy"),
        P("gx", "gy"),
        P("gx", "gy"),
        P("gy", "gx"),
        P("gy", "gx"),
        P(("gx", "gy"), None, None),
        P(("gx", "gy"), None, None),
        P(("gx", "gy")),
    )
    return jax.shard_map(
        make_body(mesh.shape["gx"], mesh.shape["gy"]),
        mesh=mesh,
        in_specs=in_specs,
        out_specs=P("gy", "gx"),
        check_vma=False,
    )
```

time: 443 us -> 241 us (0.54)
  waiting for transfers between devices: 236 us -> 96.9 us
  blocking collectives: 124 us -> 28.5 us
  starting transfers between devices: 20.9 us -> 51.2 us
  between operations: 13.8 us -> 0.66 us
  local copies, waits for them, and re-layouts: 2.93 us -> 13.9 us
  other arithmetic: 16.7 us -> 23.3 us
    reduce_scatter x4 -> x0, waiting for transfers between devices: 210 us -> none  [the longest x2 138 us: body(): lax.psum_scatter(jnp.dot(hidden_all, w_down, preferred_element_type=jnp.f...]
    all_gather x4 -> x0, blocking collectives: 73 us -> none  [the longest x2 47.3 us: body(): gathered = lax.all_gather(normed, 'gy', axis=0, tiled=True)]
    all_to_all x4 -> x10, waiting for transfers between devices: 25.9 us -> 96.9 us  [exchange(): lax.all_to_all(parts, axis, split_axis=0, concat_axis=0, tiled=False, axi...]
    all_to_all x4 -> x10, starting transfers between devices: 20.6 us -> 51 us  [exchange(): lax.all_to_all(parts, axis, split_axis=0, concat_axis=0, tiled=False, axi...]
    psum x2 -> x0, blocking collectives: 29.2 us -> none  [body(): squares = lax.psum(jnp.sum(stream * stream, axis=1), 'gx')]
    all_to_all x2, blocking collectives: 21.6 us -> 28.5 us  [exchange(): lax.all_to_all(parts, axis, split_axis=0, concat_axis=0, tiled=False, axi...]
    select_n x0 -> x5, other arithmetic: none -> 6.61 us  [the longest x2 3.01 us: body(): jnp.where(first, hidden, hidden_other)]
    broadcast_in_dim x0 -> x6, local copies, waits for them, and re-layouts: none -> 5.11 us  [the longest x2 1.72 us: body(): jnp.broadcast_to(hidden[None], (gz,) + hidden.shape)]
  transfers between devices with their start and end apart: 10 -> 14, of which waited for: 8 -> 10; matrix products, arithmetic and copies ran while one was open for 3% -> 8% of each run, Pallas kernels for 0% -> 0%
where the time goes in v1:
time: 241 us; the launch traced here: 240 us
  waiting for transfers between devices  96.9 us (40%)
  starting transfers between devices  51.2 us (21%)
  blocking collectives  28.5 us (12%)
  matrix products  25.2 us (10%)
  other arithmetic  23.3 us (10%)
  local copies, waits for them, and re-layouts  13.9 us (6%)
    all_to_all x10, waiting for transfers between devices, exchange(): lax.all_to_all(parts, axis, split_axis=0, concat_axis=0, tiled=False, axi...  96.9 us
    all_to_all x10, starting transfers between devices, exchange(): lax.all_to_all(parts, axis, split_axis=0, concat_axis=0, tiled=False, axi...  51 us
    all_to_all x2, blocking collectives, exchange(): lax.all_to_all(parts, axis, split_axis=0, concat_axis=0, tiled=False, axi...  28.5 us
    dot_general x12, matrix products, dot32(): return jnp.dot(a, b, preferred_element_type=F32)  18.5 us
    convert_element_type x2, other arithmetic, body(): pair = (keep.astype(F32) + other.astype(F32)).astype(BF16)  5.09 us
  transfers between devices with their start and end apart: 14, of which 10 were waited for; matrix products, arithmetic and copies ran while one was open for 8% of the time, Pallas kernels for 0%

profile of v1, /device:TPU:0, one launch (start us, length us, event | category | flops | bytes accessed | tf_op | source)
XLA Modules:
  0.0 239.7 jit_solution(11974303476770754492)
XLA Ops:
  0.0 1.0 multiply_convert_fusion.3
  1.0 0.8 broadcast_in_dim.28
  1.8 7.1 %all-to-all-start = ((bf16[16,16,1024]{2,1,0:T(8,128)(2,1)}), bf16[16,16,1024]{2,1,0:T(8,128)(2,1)S(1)}, u32[]{:S(2)}, u32[]{:S(2)}) async-start(bf16[16,16,1024]{2,1,0:T(8,128)(2,1)} %broadcast_in_dim.28), calls=%async_computation | async-start | bytes 1048576 | tf_op jit(solution)/shard_map/all_to_all | solution.py:55
  9.0 0.7 broadcast_divide_fusion
  9.7 0.7 iota_compare_fusion
  10.4 10.1 %all-to-all-done = bf16[16,16,1024]{2,1,0:T(8,128)(2,1)S(1)} async-done(((bf16[16,16,1024]{2,1,0:T(8,128)(2,1)}), bf16[16,16,1024]{2,1,0:T(8,128)(2,1)S(1)}, u32[]{:S(2)}, u32[]{:S(2)}) %all-to-all-start) | async-done | bytes 524320 | tf_op jit(solution)/shard_map/all_to_all | solution.py:55
  20.5 3.6 %convolution_convert_fusion.3 = bf16[256,2048]{1,0:T(8,128)(2,1)S(1)} fusion(bf16[256,1024]{1,0:T(8,128)(2,1)S(1)} %bitcast.74, bf16[1024,2048]{1,0:T(8,128)(2,1)} %param.13), kind=kOutput, calls=%fused_computation.3 | convolution fusion | flops 1074266112 | bytes 5767168 | tf_op jit(solution)/shard_map/dot_general | solution.py:16
  24.1 1.3 convolution_convert_fusion.2
  25.4 0.9 broadcast_select_fusion.11
  26.2 1.1 broadcast_select_fusion.10
  27.8 0.7 pad_slice_fusion.1
  28.4 2.4 convolution_convert_fusion.5
  31.2 1.1 pad_maximum_fusion.4
  32.3 0.9 reshape.189
  33.1 7.5 %all-to-all-start.3 = ((bf16[128,2,640]{2,1,0:T(2,128)(2,1)}), bf16[128,2,640]{2,1,0:T(2,128)(2,1)S(1)}, u32[]{:S(2)}, u32[]{:S(2)}) async-start(bf16[128,2,640]{2,1,0:T(2,128)(2,1)} %reshape.189), calls=%async_computation.3 | async-start | bytes 655360 | tf_op jit(solution)/shard_map/all_to_all | solution.py:55
  40.7 2.3 pad_maximum_fusion
  42.9 9.3 %all-to-all-done.3 = bf16[128,2,640]{2,1,0:T(2,128)(2,1)S(1)} async-done(((bf16[128,2,640]{2,1,0:T(2,128)(2,1)}), bf16[128,2,640]{2,1,0:T(2,128)(2,1)S(1)}, u32[]{:S(2)}, u32[]{:S(2)}) %all-to-all-start.3) | async-done | bytes 327712 | tf_op jit(solution)/shard_map/all_to_all | solution.py:55
  53.1 2.5 %add_convert_fusion.1 = bf16[256,2176]{1,0:T(8,128)(2,1)} fusion(bf16[256,2176]{1,0:T(8,128)(2,1)} %collective-permute-done, bf16[256,128]{1,0:T(8,128)(2,1)S(1)} %pad.9, bf16[256,1024]{1,0:T(8,128)(2,1)S(1)} %copy-done.4, bf16[256,1024]{1,0:T(8,128)(2,1)S(1)} %get-tuple-element.15), kind=kLoop, calls=%fused_computation.9 | loop fusion | flops 5013504 | bytes 3342336 | tf_op jit(solution)/shard_map/convert_element_type | solution.py:117
  55.6 3.5 %all-to-all-start.1 = ((bf16[4,64,2176]{2,1,0:T(8,128)(2,1)}), bf16[4,64,2176]{2,1,0:T(8,128)(2,1)S(1)}, u32[]{:S(2)}, u32[]{:S(2)}) async-start(bf16[4,64,2176]{2,1,0:T(8,128)(2,1)} %bitcast.83), calls=%async_computation.1 | async-start | bytes 2228224 | tf_op jit(solution)/shard_map/all_to_all | solution.py:55
  59.3 0.8 fusion.51
  60.1 0.8 copy-done.5
  61.1 13.5 %all-to-all-done.1 = bf16[4,64,2176]{2,1,0:T(8,128)(2,1)S(1)} async-done(((bf16[4,64,2176]{2,1,0:T(8,128)(2,1)}), bf16[4,64,2176]{2,1,0:T(8,128)(2,1)S(1)}, u32[]{:S(2)}, u32[]{:S(2)}) %all-to-all-start.1) | async-done | bytes 1114144 | tf_op jit(solution)/shard_map/all_to_all | solution.py:55
  75.1 0.9 broadcast_in_dim.29
  76.0 4.1 %all-to-all-start.2 = ((bf16[4,64,1024]{2,1,0:T(8,128)(2,1)}), bf16[4,64,1024]{2,1,0:T(8,128)(2,1)}, u32[]{:S(2)}, u32[]{:S(2)}) async-start(bf16[4,64,1024]{2,1,0:T(8,128)(2,1)} %broadcast_in_dim.29), calls=%async_computation.2 | async-start | bytes 1048576 | tf_op jit(solution)/shard_map/all_to_all | solution.py:55
  80.1 2.3 fusion.2
  82.5 5.9 %all-to-all-done.2 = bf16[4,64,1024]{2,1,0:T(8,128)(2,1)} async-done(((bf16[4,64,1024]{2,1,0:T(8,128)(2,1)}), bf16[4,64,1024]{2,1,0:T(8,128)(2,1)}, u32[]{:S(2)}, u32[]{:S(2)}) %all-to-all-start.2) | async-done | bytes 524320 | tf_op jit(solution)/shard_map/all_to_all | solution.py:55
  88.4 0.9 broadcast_in_dim.32
  89.2 6.3 %all-to-all-start.4 = ((bf16[128,2,512]{2,1,0:T(2,128)(2,1)}), bf16[128,2,512]{2,1,0:T(2,128)(2,1)}, u32[]{:S(2)}, u32[]{:S(2)}) async-start(bf16[128,2,512]{2,1,0:T(2,128)(2,1)} %bitcast.11), calls=%async_computation.4 | async-start | bytes 524288 | tf_op jit(solution)/shard_map/all_to_all | solution.py:55
  95.6 10.4 %all-to-all-done.4 = bf16[128,2,512]{2,1,0:T(2,128)(2,1)} async-done(((bf16[128,2,512]{2,1,0:T(2,128)(2,1)}), bf16[128,2,512]{2,1,0:T(2,128)(2,1)}, u32[]{:S(2)}, u32[]{:S(2)}) %all-to-all-start.4) | async-done | bytes 262176 | tf_op jit(solution)/shard_map/all_to_all | solution.py:55
  106.0 1.1 reshape.193
  107.5 1.5 broadcast_select_fusion.7
  109.0 0.5 copy-done.15
  109.6 1.3 fusion
  110.9 14.3 %all_to_all.60 = bf16[16,16,1024]{2,1,0:T(8,128)(2,1)S(1)} all-to-all(bf16[16,16,1024]{2,1,0:T(8,128)(2,1)S(1)} %bitcast.86), channel_id=1, replica_groups=mesh['gx'=8,'gy'=16] {'gy'}, dimensions={0} | all-to-all | bytes 1048576 | tf_op jit(solution)/shard_map/all_to_all | solution.py:55
  125.2 0.6 multiply_convert_fusion.2
  125.9 0.8 broadcast_in_dim.33
  126.7 3.8 %all-to-all-start.6 = ((bf16[16,16,1024]{2,1,0:T(8,128)(2,1)}), bf16[16,16,1024]{2,1,0:T(8,128)(2,1)S(1)}, u32[]{:S(2)}, u32[]{:S(2)}) async-start(bf16[16,16,1024]{2,1,0:T(8,128)(2,1)} %broadcast_in_dim.33), calls=%async_computation.6 | async-start | bytes 1048576 | tf_op jit(solution)/shard_map/all_to_all | solution.py:55
  130.5 0.6 copy.125
  131.1 9.5 %all-to-all-done.6 = bf16[16,16,1024]{2,1,0:T(8,128)(2,1)S(1)} async-done(((bf16[16,16,1024]{2,1,0:T(8,128)(2,1)}), bf16[16,16,1024]{2,1,0:T(8,128)(2,1)S(1)}, u32[]{:S(2)}, u32[]{:S(2)}) %all-to-all-start.6) | async-done | bytes 524320 | tf_op jit(solution)/shard_map/all_to_all | solution.py:55
  140.6 4.6 %convolution_convert_fusion = bf16[256,2048]{1,0:T(8,128)(2,1)} fusion(bf16[256,1024]{1,0:T(8,128)(2,1)S(1)} %bitcast.78, bf16[1024,2048]{1,0:T(8,128)(2,1)} %param.14), kind=kOutput, calls=%fused_computation | convolution fusion | flops 1074266112 | bytes 5767168 | tf_op jit(solution)/shard_map/dot_general | solution.py:16
  145.1 2.3 convolution_convert_fusion.1
  148.9 0.8 reshape.198
  149.8 4.6 %all-to-all-start.9 = ((bf16[128,2,640]{2,1,0:T(2,128)(2,1)}), bf16[128,2,640]{2,1,0:T(2,128)(2,1)S(1)}, u32[]{:S(2)}, u32[]{:S(2)}) async-start(bf16[128,2,640]{2,1,0:T(2,128)(2,1)} %reshape.198), calls=%async_computation.9 | async-start | bytes 655360 | tf_op jit(solution)/shard_map/all_to_all | solution.py:55
  154.4 1.7 broadcast_select_fusion.4
  156.0 1.1 pad_maximum_fusion.2
  157.2 8.8 %all-to-all-done.9 = bf16[128,2,640]{2,1,0:T(2,128)(2,1)S(1)} async-done(((bf16[128,2,640]{2,1,0:T(2,128)(2,1)}), bf16[128,2,640]{2,1,0:T(2,128)(2,1)S(1)}, u32[]{:S(2)}, u32[]{:S(2)}) %all-to-all-start.9) | async-done | bytes 327712 | tf_op jit(solution)/shard_map/all_to_all | solution.py:55
  166.8 2.6 %add_convert_fusion = bf16[256,2176]{1,0:T(8,128)(2,1)} fusion(bf16[256,2176]{1,0:T(8,128)(2,1)} %collective-permute-done.2, bf16[256,128]{1,0:T(8,128)(2,1)S(1)} %pad.10, bf16[256,1024]{1,0:T(8,128)(2,1)S(1)} %get-tuple-element.11, bf16[256,1024]{1,0:T(8,128)(2,1)S(1)} %get-tuple-element.38), kind=kLoop, calls=%fused_computation.7 | loop fusion | flops 5013504 | bytes 3342336 | tf_op jit(solution)/shard_map/convert_element_type | solution.py:117
  169.3 3.5 %all-to-all-start.7 = ((bf16[4,64,2176]{2,1,0:T(8,128)(2,1)}), bf16[4,64,2176]{2,1,0:T(8,128)(2,1)S(1)}, u32[]{:S(2)}, u32[]{:S(2)}) async-start(bf16[4,64,2176]{2,1,0:T(8,128)(2,1)} %bitcast.82), calls=%async_computation.7 | async-start | bytes 2228224 | tf_op jit(solution)/shard_map/all_to_all | solution.py:55
  173.1 0.8 fusion.52
  174.2 0.5 copy-done.6
  174.7 13.6 %all-to-all-done.7 = bf16[4,64,2176]{2,1,0:T(8,128)(2,1)S(1)} async-done(((bf16[4,64,2176]{2,1,0:T(8,128)(2,1)}), bf16[4,64,2176]{2,1,0:T(8,128)(2,1)S(1)}, u32[]{:S(2)}, u32[]{:S(2)}) %all-to-all-start.7) | async-done | bytes 1114144 | tf_op jit(solution)/shard_map/all_to_all | solution.py:55
  188.8 0.9 broadcast_in_dim.34
  189.7 4.3 %all-to-all-start.8 = ((bf16[4,64,1024]{2,1,0:T(8,128)(2,1)}), bf16[4,64,1024]{2,1,0:T(8,128)(2,1)}, u32[]{:S(2)}, u32[]{:S(2)}) async-start(bf16[4,64,1024]{2,1,0:T(8,128)(2,1)} %broadcast_in_dim.34), calls=%async_computation.8 | async-start | bytes 1048576 | tf_op jit(solution)/shard_map/all_to_all | solution.py:55
  194.0 2.3 fusion.12
  196.6 5.7 %all-to-all-done.8 = bf16[4,64,1024]{2,1,0:T(8,128)(2,1)} async-done(((bf16[4,64,1024]{2,1,0:T(8,128)(2,1)}), bf16[4,64,1024]{2,1,0:T(8,128)(2,1)}, u32[]{:S(2)}, u32[]{:S(2)}) %all-to-all-start.8) | async-done | bytes 524320 | tf_op jit(solution)/shard_map/all_to_all | solution.py:55
  202.3 0.9 broadcast_in_dim.35
  203.1 6.3 %all-to-all-start.10 = ((bf16[128,2,512]{2,1,0:T(2,128)(2,1)}), bf16[128,2,512]{2,1,0:T(2,128)(2,1)}, u32[]{:S(2)}, u32[]{:S(2)}) async-start(bf16[128,2,512]{2,1,0:T(2,128)(2,1)} %bitcast.25), calls=%async_computation.10 | async-start | bytes 524288 | tf_op jit(solution)/shard_map/all_to_all | solution.py:55
  209.5 10.4 %all-to-all-done.10 = bf16[128,2,512]{2,1,0:T(2,128)(2,1)} async-done(((bf16[128,2,512]{2,1,0:T(2,128)(2,1)}), bf16[128,2,512]{2,1,0:T(2,128)(2,1)}, u32[]{:S(2)}, u32[]{:S(2)}) %all-to-all-start.10) | async-done | bytes 262176 | tf_op jit(solution)/shard_map/all_to_all | solution.py:55
  219.9 1.1 reshape.202
  221.4 1.5 broadcast_select_fusion.1
  222.9 0.5 copy-done.16
  223.4 1.3 fusion.1
  224.7 14.3 %all_to_all.61 = bf16[16,16,1024]{2,1,0:T(8,128)(2,1)S(1)} all-to-all(bf16[16,16,1024]{2,1,0:T(8,128)(2,1)S(1)} %bitcast.87), channel_id=1, replica_groups=mesh['gx'=8,'gy'=16] {'gy'}, dimensions={0} | all-to-all | bytes 1048576 | tf_op jit(solution)/shard_map/all_to_all | solution.py:55
  239.1 0.6 add.95
  (106 shorter events, 7.2 us)
Async XLA Ops:
  0.0 59.3 %copy-start = (bf16[2,2048,256]{2,1,0:T(8,128)(2,1)S(1)}, bf16[2,2048,256]{2,1,0:T(8,128)(2,1)}, u32[]{:S(2)}) copy-start(bf16[2,2048,256]{2,1,0:T(8,128)(2,1)} %param.19) | copy-start | bytes 6291460
  1.8 18.6 %all-to-all-start = ((bf16[16,16,1024]{2,1,0:T(8,128)(2,1)}), bf16[16,16,1024]{2,1,0:T(8,128)(2,1)S(1)}, u32[]{:S(2)}, u32[]{:S(2)}) async-start(bf16[16,16,1024]{2,1,0:T(8,128)(2,1)} %broadcast_in_dim.28), calls=%async_computation | async-start | bytes 1048576 | tf_op jit(solution)/shard_map/all_to_all | solution.py:55
  20.5 3.6 %copy-start.13 = (bf16[1024,2048]{1,0:T(8,128)(2,1)S(1)}, bf16[1024,2048]{1,0:T(8,128)(2,1)}, u32[]{:S(2)}) copy-start(bf16[1024,2048]{1,0:T(8,128)(2,1)} %param.14) | copy-start | bytes 12582916
  26.2 4.6 %copy-start.7 = (bf16[1024,32]{0,1:T(8,128)(2,1)S(1)}, bf16[1024,32]{0,1:T(8,128)(2,1)}, u32[]{:S(2)}) copy-start(bf16[1024,32]{0,1:T(8,128)(2,1)} %param.16) | copy-start | bytes 196612
  32.3 20.8 %copy-start.4 = (bf16[256,1024]{1,0:T(8,128)(2,1)S(1)}, bf16[256,1024]{1,0:T(8,128)(2,1)}, u32[]{:S(2)}) copy-start(bf16[256,1024]{1,0:T(8,128)(2,1)} %get-tuple-element.17) | copy-start | bytes 1572868
  33.1 19.1 %all-to-all-start.3 = ((bf16[128,2,640]{2,1,0:T(2,128)(2,1)}), bf16[128,2,640]{2,1,0:T(2,128)(2,1)S(1)}, u32[]{:S(2)}, u32[]{:S(2)}) async-start(bf16[128,2,640]{2,1,0:T(2,128)(2,1)} %reshape.189), calls=%async_computation.3 | async-start | bytes 655360 | tf_op jit(solution)/shard_map/all_to_all | solution.py:55
  42.9 10.1 %collective-permute-start = (bf16[256,2176]{1,0:T(8,128)(2,1)}, bf16[256,2176]{1,0:T(8,128)(2,1)}, u32[]{:S(2)}, u32[]{:S(2)}) collective-permute-start(bf16[256,2176]{1,0:T(8,128)(2,1)} %pad_maximum_fusion), channel_id=1, source_target_pairs={{0,16},{16,0},{32,48},{48,32},{64,80},{80,64},{96,112},{112,96},{1... | collective-permute-start | bytes 3342344 | tf_op jit(solution)/shard_map/ppermute | solution.py:116
  55.6 19.0 %all-to-all-start.1 = ((bf16[4,64,2176]{2,1,0:T(8,128)(2,1)}), bf16[4,64,2176]{2,1,0:T(8,128)(2,1)S(1)}, u32[]{:S(2)}, u32[]{:S(2)}) async-start(bf16[4,64,2176]{2,1,0:T(8,128)(2,1)} %bitcast.83), calls=%async_computation.1 | async-start | bytes 2228224 | tf_op jit(solution)/shard_map/all_to_all | solution.py:55
  60.1 0.8 copy-start.5
  76.0 12.4 %all-to-all-start.2 = ((bf16[4,64,1024]{2,1,0:T(8,128)(2,1)}), bf16[4,64,1024]{2,1,0:T(8,128)(2,1)}, u32[]{:S(2)}, u32[]{:S(2)}) async-start(bf16[4,64,1024]{2,1,0:T(8,128)(2,1)} %broadcast_in_dim.29), calls=%async_computation.2 | async-start | bytes 1048576 | tf_op jit(solution)/shard_map/all_to_all | solution.py:55
  80.1 26.9 %copy-start.2 = (bf16[512,1024]{1,0:T(8,128)(2,1)S(1)}, bf16[512,1024]{1,0:T(8,128)(2,1)}, u32[]{:S(2)}) copy-start(bf16[512,1024]{1,0:T(8,128)(2,1)} %param.18) | copy-start | bytes 3145732
  89.2 16.7 %all-to-all-start.4 = ((bf16[128,2,512]{2,1,0:T(2,128)(2,1)}), bf16[128,2,512]{2,1,0:T(2,128)(2,1)}, u32[]{:S(2)}, u32[]{:S(2)}) async-start(bf16[128,2,512]{2,1,0:T(2,128)(2,1)} %bitcast.11), calls=%async_computation.4 | async-start | bytes 524288 | tf_op jit(solution)/shard_map/all_to_all | solution.py:55
  95.5 12.0 %collective-permute-start.1 = (bf16[256,1024]{1,0:T(8,128)(2,1)}, bf16[256,1024]{1,0:T(8,128)(2,1)}, u32[]{:S(2)}, u32[]{:S(2)}) collective-permute-start(bf16[256,1024]{1,0:T(8,128)(2,1)} %bitcast.2), channel_id=1, source_target_pairs={{0,16},{16,0},{32,48},{48,32},{64,80},{80,64},{96,112},{112,96},{1... | collective-permute-start | bytes 1572872 | tf_op jit(solution)/shard_map/ppermute | solution.py:144
  107.1 2.5 %copy-start.15 = (bf16[2048,1024]{1,0:T(8,128)(2,1)S(1)}, bf16[2048,1024]{1,0:T(8,128)(2,1)}, u32[]{:S(2)}) copy-start(bf16[2048,1024]{1,0:T(8,128)(2,1)} %param.17) | copy-start | bytes 12582916
  109.6 15.7 %copy-start.10 = (f32[16,1024]{1,0:T(8,128)S(1)}, f32[16,1024]{1,0:T(8,128)}, u32[]{:S(2)}) copy-start(f32[16,1024]{1,0:T(8,128)} %param.11) | copy-start | bytes 196612
  109.6 15.7 %copy-start.11 = (f32[1024]{0:T(1024)S(1)}, f32[1024]{0:T(1024)}, u32[]{:S(2)}) copy-start(f32[1024]{0:T(1024)} %param.12) | copy-start | bytes 12292
  126.7 13.8 %all-to-all-start.6 = ((bf16[16,16,1024]{2,1,0:T(8,128)(2,1)}), bf16[16,16,1024]{2,1,0:T(8,128)(2,1)S(1)}, u32[]{:S(2)}, u32[]{:S(2)}) async-start(bf16[16,16,1024]{2,1,0:T(8,128)(2,1)} %broadcast_in_dim.33), calls=%async_computation.6 | async-start | bytes 1048576 | tf_op jit(solution)/shard_map/all_to_all | solution.py:55
  140.5 4.6 %copy-start.14 = (bf16[1024,2048]{1,0:T(8,128)(2,1)S(1)}, bf16[1024,2048]{1,0:T(8,128)(2,1)}, u32[]{:S(2)}) copy-start(bf16[1024,2048]{1,0:T(8,128)(2,1)} %param.13) | copy-start | bytes 12582916
  145.1 2.3 copy-start.1
  147.4 1.0 copy-start.8
  149.8 16.2 %all-to-all-start.9 = ((bf16[128,2,640]{2,1,0:T(2,128)(2,1)}), bf16[128,2,640]{2,1,0:T(2,128)(2,1)S(1)}, u32[]{:S(2)}, u32[]{:S(2)}) async-start(bf16[128,2,640]{2,1,0:T(2,128)(2,1)} %reshape.198), calls=%async_computation.9 | async-start | bytes 655360 | tf_op jit(solution)/shard_map/all_to_all | solution.py:55
  157.2 9.6 %collective-permute-start.2 = (bf16[256,2176]{1,0:T(8,128)(2,1)}, bf16[256,2176]{1,0:T(8,128)(2,1)}, u32[]{:S(2)}, u32[]{:S(2)}) collective-permute-start(bf16[256,2176]{1,0:T(8,128)(2,1)} %pad_maximum_fusion.2), channel_id=1, source_target_pairs={{0,16},{16,0},{32,48},{48,32},{64,80},{80,64},{96,112},{112,96},{1... | collective-permute-start | bytes 3342344 | tf_op jit(solution)/shard_map/ppermute | solution.py:116
  169.3 19.0 %all-to-all-start.7 = ((bf16[4,64,2176]{2,1,0:T(8,128)(2,1)}), bf16[4,64,2176]{2,1,0:T(8,128)(2,1)S(1)}, u32[]{:S(2)}, u32[]{:S(2)}) async-start(bf16[4,64,2176]{2,1,0:T(8,128)(2,1)} %bitcast.82), calls=%async_computation.7 | async-start | bytes 2228224 | tf_op jit(solution)/shard_map/all_to_all | solution.py:55
  173.9 0.8 copy-start.6
  189.7 6.6 %copy-start.12 = (bf16[2,1,256]{2,1,0:T(2,128)(2,1)S(1)}, bf16[2,1,256]{2,1,0:T(2,128)(2,1)}, u32[]{:S(2)}) copy-start(bf16[2,1,256]{2,1,0:T(2,128)(2,1)} %copy.125) | copy-start | bytes 3076
  189.7 12.6 %all-to-all-start.8 = ((bf16[4,64,1024]{2,1,0:T(8,128)(2,1)}), bf16[4,64,1024]{2,1,0:T(8,128)(2,1)}, u32[]{:S(2)}, u32[]{:S(2)}) async-start(bf16[4,64,1024]{2,1,0:T(8,128)(2,1)} %broadcast_in_dim.34), calls=%async_computation.8 | async-start | bytes 1048576 | tf_op jit(solution)/shard_map/all_to_all | solution.py:55
  194.0 27.0 %copy-start.3 = (bf16[512,1024]{1,0:T(8,128)(2,1)S(1)}, bf16[512,1024]{1,0:T(8,128)(2,1)}, u32[]{:S(2)}) copy-start(bf16[512,1024]{1,0:T(8,128)(2,1)} %param.18) | copy-start | bytes 3145732
  203.1 16.7 %all-to-all-start.10 = ((bf16[128,2,512]{2,1,0:T(2,128)(2,1)}), bf16[128,2,512]{2,1,0:T(2,128)(2,1)}, u32[]{:S(2)}, u32[]{:S(2)}) async-start(bf16[128,2,512]{2,1,0:T(2,128)(2,1)} %bitcast.25), calls=%async_computation.10 | async-start | bytes 524288 | tf_op jit(solution)/shard_map/all_to_all | solution.py:55
  209.4 12.0 %collective-permute-start.3 = (bf16[256,1024]{1,0:T(8,128)(2,1)}, bf16[256,1024]{1,0:T(8,128)(2,1)}, u32[]{:S(2)}, u32[]{:S(2)}) collective-permute-start(bf16[256,1024]{1,0:T(8,128)(2,1)} %bitcast.15), channel_id=1, source_target_pairs={{0,16},{16,0},{32,48},{48,32},{64,80},{80,64},{96,112},{112,96},{1... | collective-permute-start | bytes 1572872 | tf_op jit(solution)/shard_map/ppermute | solution.py:144
  220.9 2.5 %copy-start.16 = (bf16[2048,1024]{1,0:T(8,128)(2,1)S(1)}, bf16[2048,1024]{1,0:T(8,128)(2,1)}, u32[]{:S(2)}) copy-start(bf16[2048,1024]{1,0:T(8,128)(2,1)} %param.17) | copy-start | bytes 12582916
  223.4 15.6 %copy-start.9 = (f32[16,1024]{1,0:T(8,128)S(1)}, f32[16,1024]{1,0:T(8,128)}, u32[]{:S(2)}) copy-start(f32[16,1024]{1,0:T(8,128)} %get-tuple-element.6) | copy-start | bytes 196612

commit v2 on v1

v2 whole, which is shorter than its diff:
```python
import functools

import jax
import jax.numpy as jnp
from jax import lax
from jax.experimental import pallas as pl
from jax.experimental.pallas import tpu as pltpu
from jax.sharding import PartitionSpec as P

D = 8192
HEADS = 32
DH = 256
STEPS = 2
EPS = 1e-06
LANES = 128
F32 = jnp.float32
BF16 = jnp.bfloat16
PARAMS = pltpu.CompilerParams(vmem_limit_bytes=16 * 1024 * 1024)
VMEM = pl.BlockSpec(memory_space=pltpu.VMEM)
SMEM = pl.BlockSpec(memory_space=pltpu.SMEM)
COST = pl.CostEstimate(flops=0, bytes_accessed=0, transcendentals=0)
LATE = pl.CostEstimate(flops=10**10, bytes_accessed=0, transcendentals=0)


def dot32(a, b):
    return jnp.dot(a, b, preferred_element_type=F32)


def call(kernel, out_shape, *args, scalars=0, cost=COST, **kwargs):
    return pl.pallas_call(
        kernel,
        out_shape=out_shape,
        in_specs=[SMEM] * scalars + [VMEM] * (len(args) - scalars),
        compiler_params=PARAMS,
        cost_estimate=cost,
        **kwargs,
    )(*args)


def stream_call(kernel, out_shape, scalars, grid, specs, args, out_specs, cost=COST, scratch=()):
    return pl.pallas_call(
        kernel,
        out_shape=out_shape,
        grid_spec=pltpu.PrefetchScalarGridSpec(
            num_scalar_prefetch=len(scalars),
            grid=grid,
            in_specs=specs,
            out_specs=out_specs,
            scratch_shapes=scratch,
        ),
        compiler_params=PARAMS,
        cost_estimate=cost,
    )(*scalars, *args)


def whole(array):
    return pl.BlockSpec(array.shape, lambda *_: (0,) * array.ndim)


def spread_kernel(x_ref, gain_ref, out_ref):
    scaled = (x_ref[...] * gain_ref[...]).astype(BF16)
    for n in range(out_ref.shape[0]):
        out_ref[n] = scaled


def add_kernel(x_ref, delta_ref, gain_ref, new_ref, out_ref=None):
    new = x_ref[...] + jnp.sum(delta_ref[...].astype(F32), axis=0)
    new_ref[...] = new
    if out_ref is not None:
        scaled = (new * gain_ref[...]).astype(BF16)
        for n in range(out_ref.shape[0]):
            out_ref[n] = scaled


def query_kernel(kv_cols, x_ref, inverse_ref, wq_ref, wkv_ref, out_ref, squares_ref):
    x = x_ref[...]
    plain = x.astype(F32) * inverse_ref[...]
    squares = jnp.sum(plain * plain, axis=1, keepdims=True)
    high = squares.astype(BF16).astype(F32)
    low = squares - high
    lane = lax.broadcasted_iota(jnp.int32, squares_ref.shape, 1)
    columns = jnp.where(lane == kv_cols, high, jnp.where(lane == kv_cols + 1, low, 0.0))
    squares_ref[...] = columns.astype(BF16)
    q_cols = wq_ref.shape[1]
    out_ref[:, :q_cols] = dot32(x, wq_ref[...]).astype(BF16)
    out_ref[:, q_cols:] = (dot32(x, wkv_ref[...]) + columns).astype(BF16)


def hidden_part_kernel(half_ref, x_ref, wg_ref, wu_ref, *outs):
    for n in range(len(outs) // 2):

        @pl.when(pl.program_id(0) == n)
        def _():
            outs[2 * n][...] = dot32(x_ref[...], wg_ref[...]).astype(BF16)
            outs[2 * n + 1][...] = dot32(x_ref[...], wu_ref[...]).astype(BF16)


def hidden_part(half_index, x, w_gate, w_up, blocks=2):
    rows, width = x.shape
    block = w_gate.shape[1] // 2 // blocks
    weight = pl.BlockSpec((width, block), lambda n, h: (0, h[0] * blocks + n))
    part = jax.ShapeDtypeStruct((rows, block), BF16)
    return stream_call(
        hidden_part_kernel,
        [part] * (2 * blocks),
        [half_index],
        (blocks,),
        [whole(x), weight, weight],
        [x, w_gate, w_up],
        [whole(part)] * (2 * blocks),
    )


def pair_kernel(gz, z_ref, *refs):
    outs = refs[-gz:]
    count = (len(refs) - gz) // 2
    half = sum(ref.shape[1] for ref in refs[: count - 1]) // 2
    size = outs[0].shape[0]
    for n in range(gz):
        here = pl.ds(pl.multiple_of(lax.rem(z_ref[0] + n, gz) * size, size), size)
        for k in range(count):
            keep, other = refs[k], refs[count + k]
            block = keep.shape[1]
            at = 2 * half if k == count - 1 else k % 2 * half + k // 2 * block
            outs[n][:, at : at + block] = (
                keep[here, :].astype(F32) + other[here, :].astype(F32)
            ).astype(BF16)


def hidden_kernel(kv_cols, *refs):
    out_ref = refs[-1]
    half = out_ref.shape[1]
    total = refs[0][...].astype(F32)
    for ref in refs[1:-1]:
        total = total + ref[...].astype(F32)
    at = 2 * half + kv_cols
    scale = lax.rsqrt((total[:, at : at + 1] + total[:, at + 1 : at + 2]) / D + EPS)
    gate = total[:, :half] * scale
    up = total[:, half : 2 * half] * scale
    out_ref[...] = (gate / (1.0 + jnp.exp(-gate)) * up).astype(BF16)


def attend_kernel(steps, lengths_ref, q_ref, *refs):
    news = refs[:steps]
    keys_ref, values_ref, out_ref = refs[steps:]
    row = pl.program_id(0)
    scale = DH**-0.5
    q = q_ref[0]
    heads = jnp.concatenate([q[:, :DH], q[:, DH:]], axis=0)
    old_s = lax.dot_general(
        heads, keys_ref[0], (((1,), (1,)), ((), ())), preferred_element_type=F32
    )
    place = lax.broadcasted_iota(jnp.int32, old_s.shape, 1)
    old_s = jnp.where(place < lengths_ref[row], old_s * scale, -jnp.inf)
    heads32 = heads.astype(F32)
    top = jnp.max(old_s, axis=1, keepdims=True)
    new_s = []
    new_v = []
    for ref in news:
        line = ref[pl.ds(row, 1), :]
        score = jnp.sum(heads32 * line[:, :DH], axis=1, keepdims=True) * scale
        new_s.append(score)
        new_v.append(line[:, DH:])
        top = jnp.maximum(top, score)
    old_e = jnp.exp(old_s - top)
    new_e = [jnp.exp(score - top) for score in new_s]
    total = jnp.sum(old_e, axis=1, keepdims=True)
    for e in new_e:
        total = total + e
    old_w = (old_e / total).astype(BF16)
    result = dot32(old_w, values_ref[0])
    for e, v in zip(new_e, new_v):
        result = result + (e / total).astype(BF16).astype(F32) * v
    count = q.shape[0]
    out_ref[0] = jnp.concatenate([result[:count], result[count:]], axis=1).astype(BF16)


def attend(lengths, query, news, keys, values):
    def by_row(array):
        return pl.BlockSpec((1,) + array.shape[1:], lambda r, n: (r, 0, 0))

    return stream_call(
        functools.partial(attend_kernel, len(news)),
        jax.ShapeDtypeStruct(query.shape, BF16),
        [lengths],
        (query.shape[0],),
        [by_row(query)] + [whole(new) for new in news] + [by_row(keys), by_row(values)],
        [query, *news, keys, values],
        by_row(query),
    )


def heads_kernel(heads_ref, wout_ref, out_ref):
    out_ref[...] = dot32(heads_ref[...], wout_ref[...])


def heads_output(heads, w_out, blocks=2):
    rows, q_cols = heads.shape
    width = w_out.shape[1]
    return stream_call(
        heads_kernel,
        jax.ShapeDtypeStruct((rows, width), F32),
        [],
        (blocks,),
        [whole(heads), pl.BlockSpec((q_cols, width // blocks), lambda n: (0, n))],
        [heads, w_out],
        pl.BlockSpec((rows, width // blocks), lambda n: (0, n)),
        cost=LATE,
    )


def output_kernel(gz, place_ref, *refs):
    pieces, others = refs[:gz], refs[gz : 2 * gz]
    heads_ref, down_ref, out_ref, hidden = refs[2 * gz :]
    size, half = pieces[0].shape

    @pl.when(pl.program_id(0) == 0)
    def _():
        z, c = place_ref[0], place_ref[1]
        mine = pl.ds(pl.multiple_of(c * half, half), half)
        theirs = pl.ds(pl.multiple_of((1 - c) * half, half), half)
        for n in range(gz):
            at = pl.ds(pl.multiple_of(lax.rem(z + gz - n, gz) * size, size), size)
            hidden[at, mine] = pieces[n][...]
            hidden[at, theirs] = others[n][...]

    out_ref[...] = (dot32(hidden[...], down_ref[...]) + heads_ref[...]).astype(BF16)


def output_part(place, pieces, others, heads_part, w_down, blocks=4):
    rows, width = heads_part.shape
    ff_cols = w_down.shape[0]
    block = width // blocks
    return stream_call(
        functools.partial(output_kernel, len(pieces)),
        jax.ShapeDtypeStruct((rows, width), BF16),
        [place],
        (blocks,),
        [whole(piece) for piece in pieces + others]
        + [
            pl.BlockSpec((rows, block), lambda n, p: (0, n)),
            pl.BlockSpec((ff_cols, block), lambda n, p: (0, n)),
        ],
        [*pieces, *others, heads_part, w_down],
        pl.BlockSpec((rows, block), lambda n, p: (0, n)),
        scratch=[pltpu.VMEM((rows, ff_cols), BF16)],
    )


def make_body(gx, gy):
    gz = gx // 2
    core_swap = [(n, n ^ 1) for n in range(gx)]

    def z_shift(n):
        return [(2 * z + c, 2 * ((z + n) % gz) + c) for z in range(gz) for c in range(2)]

    def exchange(parts, axis):
        return lax.all_to_all(parts, axis, split_axis=0, concat_axis=0, tiled=False)

    def body(
        residual,
        norm_gain,
        w_gate,
        w_up,
        w_query,
        w_keyval,
        w_down,
        w_out,
        cache_keys,
        cache_values,
        lengths,
    ):
        stream = residual
        own_rows, width = residual.shape
        rows = own_rows * gy
        half = w_gate.shape[1] // 2
        q_cols = w_query.shape[1]
        kv_cols = w_keyval.shape[1]
        cache_rows = cache_keys.shape[0]
        me = lax.axis_index("gx")
        z, core = me // 2, lax.rem(me, 2)
        place = jnp.stack([z, core]).astype(jnp.int32)
        gain = norm_gain[None, :]
        inverse_gain = 1.0 / gain
        keyval_padded = jnp.pad(w_keyval, ((0, 0), (0, LANES - kv_cols)))
        news = []
        spread = call(
            spread_kernel, jax.ShapeDtypeStruct((gy, own_rows, width), BF16), stream, gain
        )
        w_gate, w_up, w_query, w_down, w_out, cache_keys, cache_values = [
            pltpu.with_memory_space_constraint(array, pltpu.HBM)
            for array in (w_gate, w_up, w_query, w_down, w_out, cache_keys, cache_values)
        ]
        for step in range(STEPS):
            gathered = exchange(spread, "gy").reshape(rows, width)
            packed, squares = call(
                functools.partial(query_kernel, kv_cols),
                (
                    jax.ShapeDtypeStruct((rows, q_cols + LANES), BF16),
                    jax.ShapeDtypeStruct((rows, LANES), BF16),
                ),
                gathered,
                inverse_gain,
                w_query,
                keyval_padded,
            )
            packed = exchange(
                packed.reshape(gx * gy, cache_rows, q_cols + LANES), ("gx", "gy")
            )

            give = hidden_part(place[1:] ^ 1, gathered, w_gate, w_up)
            other = [lax.ppermute(part, "gx", core_swap) for part in (*give, squares)]
            keep = hidden_part(place[1:], gathered, w_gate, w_up)
            pair = call(
                functools.partial(pair_kernel, gz),
                [jax.ShapeDtypeStruct((rows // gz, 2 * half + LANES), BF16)] * gz,
                place,
                *keep,
                squares,
                *other,
                scalars=1,
            )
            arrived = [pair[0]] + [lax.ppermute(pair[n], "gx", z_shift(n)) for n in range(1, gz)]

            packed = lax.optimization_barrier((packed, pair[0]))[0]
            mine = jnp.sum(
                packed.reshape(gx, gy, cache_rows, q_cols + LANES).astype(F32), axis=0
            ).transpose(1, 0, 2)
            at = q_cols + kv_cols
            scale = lax.rsqrt((mine[:, :1, at : at + 1] + mine[:, :1, at + 1 : at + 2]) / D + EPS)
            query = (mine[:, :, :q_cols] * scale).astype(BF16)
            keyval = (mine[:, :, q_cols:at] * scale).astype(BF16).astype(F32)
            news.append(keyval.reshape(cache_rows, 2 * DH))
            attended = attend(lengths, query, news, cache_keys, cache_values)
            blocks = attended.transpose(1, 0, 2)
            blocks = jnp.broadcast_to(blocks[None], (gx, gy, cache_rows, q_cols))
            blocks = blocks.reshape(gx * gy, cache_rows, q_cols)
            heads_all = exchange(blocks, ("gx", "gy")).reshape(rows, q_cols)
            heads_part = heads_output(heads_all, w_out)

            arrived = lax.optimization_barrier((arrived, blocks))[0]
            hidden = call(
                functools.partial(hidden_kernel, kv_cols),
                jax.ShapeDtypeStruct((rows // gz, half), BF16),
                *arrived,
            )
            pieces = [hidden] + [lax.ppermute(hidden, "gx", z_shift(n)) for n in range(1, gz)]
            others = [lax.ppermute(piece, "gx", core_swap) for piece in pieces]
            delta = output_part(place, pieces, others, heads_part, w_down)
            delta = exchange(delta.reshape(gy, own_rows, width), "gy")
            stream_shape = jax.ShapeDtypeStruct(stream.shape, F32)
            spread_shape = jax.ShapeDtypeStruct((gy, own_rows, width), BF16)
            if step + 1 < STEPS:
                stream, spread = call(
                    add_kernel, (stream_shape, spread_shape), stream, delta, gain
                )
            else:
                stream = call(add_kernel, stream_shape, stream, delta, gain)
        return stream

    return body


def solution(mesh):
    in_specs = (
        P("gy", "gx"),
        P("gx"),
        P("gx", "gy"),
        P("gx", "gy"),
        P("gx", "gy"),
        P("gx", "gy"),
        P("gy", "gx"),
        P("gy", "gx"),
        P(("gx", "gy"), None, None),
        P(("gx", "gy"), None, None),
        P(("gx", "gy")),
    )
    return jax.shard_map(
        make_body(mesh.shape["gx"], mesh.shape["gy"]),
        mesh=mesh,
        in_specs=in_specs,
        out_specs=P("gy", "gx"),
        check_vma=False,
    )
```

time: 241 us -> 185 us (0.77)
  waiting for transfers between devices: 96.9 us -> 28.2 us
  Pallas kernels: 0 us -> 40.8 us
  matrix products: 25.2 us -> 0 us
  other arithmetic: 23.3 us -> 1.97 us
  blocking collectives: 28.5 us -> 49.1 us
  local copies, waits for them, and re-layouts: 13.9 us -> 6.49 us
  starting transfers between devices: 51.2 us -> 57.2 us
    all_to_all x10 -> x5, waiting for transfers between devices: 96.9 us -> 22.2 us  [exchange(): return lax.all_to_all(parts, axis, split_axis=0, concat_axis=0, tiled=False)]
    pallas_call x0 -> x19, Pallas kernels: none -> 40.8 us  [the longest x10 33.4 us: stream_call(): pl.pallas_call(kernel, out_shape=out_shape, grid_spec=pltpu.PrefetchScala...]
    dot_general x19 -> x0, matrix products: 25.2 us -> none  [the longest x12 18.5 us: dot32(): return jnp.dot(a, b, preferred_element_type=F32)]
    ppermute x4 -> x30, starting transfers between devices: 0.18 us -> 22.5 us  [the longest x6 11.3 us: body(): lax.ppermute(pair[n], 'gx', z_shift(n))]
    all_to_all x2 -> x3, blocking collectives: 28.5 us -> 49.1 us  [exchange(): return lax.all_to_all(parts, axis, split_axis=0, concat_axis=0, tiled=False)]
    all_to_all x10 -> x5, starting transfers between devices: 51 us -> 34.7 us  [exchange(): return lax.all_to_all(parts, axis, split_axis=0, concat_axis=0, tiled=False)]
    convert_element_type x6 -> x2, other arithmetic: 7.06 us -> 0.15 us  [body(): query = (mine[:, :, :q_cols] * scale).astype(BF16)]
    select_n x5 -> x0, other arithmetic: 6.61 us -> none  [the longest x2 3.01 us: body(): jnp.where(first, hidden, hidden_other)]
  transfers between devices with their start and end apart: 14 -> 35, of which waited for: 10 -> 7; matrix products, arithmetic and copies ran while one was open for 8% -> 3% of each run, Pallas kernels for 0% -> 14%
where the time goes in v2:
time: 185 us; the launch traced here: 184 us
  starting transfers between devices  57.2 us (31%)
  blocking collectives  49.1 us (27%)
  Pallas kernels  40.8 us (22%)
  waiting for transfers between devices  28.2 us (15%)
  local copies, waits for them, and re-layouts  6.49 us (4%)
  other arithmetic  1.97 us (1%)
    all_to_all x3, blocking collectives, exchange(): return lax.all_to_all(parts, axis, split_axis=0, concat_axis=0, tiled=False)  49.1 us
    all_to_all x5, starting transfers between devices, exchange(): return lax.all_to_all(parts, axis, split_axis=0, concat_axis=0, tiled=False)  34.7 us
    pallas_call x10, Pallas kernels, stream_call(): pl.pallas_call(kernel, out_shape=out_shape, grid_spec=pltpu.PrefetchScala...  33.4 us
    all_to_all x5, waiting for transfers between devices, exchange(): return lax.all_to_all(parts, axis, split_axis=0, concat_axis=0, tiled=False)  22.2 us
    ppermute x6, starting transfers between devices, body(): lax.ppermute(pair[n], 'gx', z_shift(n))  11.3 us
    ppermute x6, starting transfers between devices, body(): lax.ppermute(hidden, 'gx', z_shift(n))  8.69 us
    pallas_call x9, Pallas kernels, call(): pl.pallas_call(kernel, out_shape=out_shape, in_specs=[SMEM] * scalars + [...  7.45 us
    ppermute x6, waiting for transfers between devices, body(): lax.ppermute(hidden, 'gx', z_shift(n))  5.94 us
  transfers between devices with their start and end apart: 35, of which 7 were waited for; matrix products, arithmetic and copies ran while one was open for 3% of the time, Pallas kernels for 14%

profile of v2, /device:TPU:0, one launch (start us, length us, event | category | flops | bytes accessed | tf_op | source)
XLA Modules:
  0.0 184.4 jit_solution(3229493379652279519)
XLA Ops:
  0.0 0.8 copy-done
  0.8 0.7 copy-done.2
  1.5 0.8 shard_map.109
  2.4 7.1 %all-to-all-start = ((bf16[16,16,1024]{2,1,0:T(8,128)(2,1)}), bf16[16,16,1024]{2,1,0:T(8,128)(2,1)S(1)}, u32[]{:S(2)}, u32[]{:S(2)}) async-start(bf16[16,16,1024]{2,1,0:T(8,128)(2,1)} %shard_map.109), calls=%async_computation | async-start | bytes 1048576 | tf_op jit(solution)/shard_map/all_to_all | solution.py:258
  9.5 1.0 copy.18
  10.6 0.7 broadcast_divide_fusion
  11.3 9.7 %all-to-all-done = bf16[16,16,1024]{2,1,0:T(8,128)(2,1)S(1)} async-done(((bf16[16,16,1024]{2,1,0:T(8,128)(2,1)}), bf16[16,16,1024]{2,1,0:T(8,128)(2,1)S(1)}, u32[]{:S(2)}, u32[]{:S(2)}) %all-to-all-start) | async-done | bytes 524320 | tf_op jit(solution)/shard_map/all_to_all | solution.py:258
  21.0 1.8 shard_map.111
  22.8 0.9 reshape.50
  23.7 7.5 %all-to-all-start.1 = ((bf16[128,2,640]{2,1,0:T(2,128)(2,1)}), bf16[128,2,640]{2,1,0:T(2,128)(2,1)S(1)}, u32[]{:S(2)}, u32[]{:S(2)}) async-start(bf16[128,2,640]{2,1,0:T(2,128)(2,1)} %reshape.50), calls=%async_computation.1 | async-start | bytes 655360 | tf_op jit(solution)/shard_map/all_to_all | solution.py:258
  31.2 3.0 %shard_map.112 = (bf16[256,512]{1,0:T(8,128)(2,1)S(1)}, bf16[256,512]{1,0:T(8,128)(2,1)S(1)}, bf16[256,512]{1,0:T(8,128)(2,1)S(1)}, bf16[256,512]{1,0:T(8,128)(2,1)S(1)}) custom-call(s32[1]{0:T(128)S(6)} %xor.4.half_ref, bf16[256,1024]{1,0:T(8,128)(2,1)S(1)} %bitcast.23, bf16[1024,2048]{1,0:T(8,128)(2,1)} %wg_ref.7, bf16[1024,2048]{1,0:T(8,128)(2,1)} %wu_ref.7), custom_call_target="tpu_custom_call" | custom-call | tf_op jit(solution)/shard_map/pallas_call | solution.py:41
  34.3 0.5 collective-permute-start.1
  34.9 0.4 collective-permute-start.3
  35.5 3.0 %shard_map.110 = (bf16[256,512]{1,0:T(8,128)(2,1)S(1)}, bf16[256,512]{1,0:T(8,128)(2,1)S(1)}, bf16[256,512]{1,0:T(8,128)(2,1)S(1)}, bf16[256,512]{1,0:T(8,128)(2,1)S(1)}) custom-call(s32[1]{0:T(128)} %bitcast.1.half_ref, bf16[256,1024]{1,0:T(8,128)(2,1)S(1)} %bitcast.24, bf16[1024,2048]{1,0:T(8,128)(2,1)} %wg_ref.7, bf16[1024,2048]{1,0:T(8,128)(2,1)} %wu_ref.7), custom_call_target="tpu_custom_call" | custom-call | tf_op jit(solution)/shard_map/pallas_call | solution.py:41
  38.6 0.8 shard_map.113
  39.4 1.2 collective-permute-start.5
  40.6 3.2 %collective-permute-start.6 = (bf16[64,2176]{1,0:T(8,128)(2,1)S(1)}, bf16[64,2176]{1,0:T(8,128)(2,1)S(1)}, u32[]{:S(2)}, u32[]{:S(2)}) collective-permute-start(bf16[64,2176]{1,0:T(8,128)(2,1)S(1)} %get-tuple-element.56), channel_id=1, source_target_pairs={{0,64},{16,80},{32,96},{48,112},{64,0},{80,16},{96,32},{112,48},{1... | collective-permute-start | bytes 835592 | tf_op jit(solution)/shard_map/ppermute | solution.py:323
  43.8 1.2 collective-permute-start.7
  45.0 0.3 convert_reduce_fusion.1
  45.4 0.2 rsqrt_reduce_fusion.1
  45.8 4.3 %shard_map.114 = bf16[2,16,512]{2,1,0:T(8,128)(2,1)S(1)} custom-call(s32[2]{0:T(128)S(1)} %copy-done.4, bf16[2,16,512]{2,1,0:T(8,128)(2,1)S(1)} %fusion.1.q_ref, f32[2,512]{1,0:T(2,128)S(1)} %reshape.65.refs_0_, bf16[2,2048,256]{2,1,0:T(8,128)(2,1)} %refs_2_.3, bf16[2,2048,256]{2,1,0:T(8,128)(2,1)} %refs_3_.1), custom_call_target="tpu_custom_call" | custom-call | tf_op jit(solution)/shard_map/pallas_call | solution.py:41
  50.1 0.8 broadcast_in_dim.7
  50.9 7.7 %all-to-all-start.2 = ((bf16[128,2,512]{2,1,0:T(2,128)(2,1)}), bf16[128,2,512]{2,1,0:T(2,128)(2,1)S(1)}, u32[]{:S(2)}, u32[]{:S(2)}) async-start(bf16[128,2,512]{2,1,0:T(2,128)(2,1)} %bitcast.8), calls=%async_computation.2 | async-start | bytes 524288 | tf_op jit(solution)/shard_map/all_to_all | solution.py:258
  58.7 0.3 shard_map.115.refs_0_
  59.0 2.9 %collective-permute-start.10 = (bf16[64,1024]{1,0:T(8,128)(2,1)S(1)}, bf16[64,1024]{1,0:T(8,128)(2,1)S(1)}, u32[]{:S(2)}, u32[]{:S(2)}) collective-permute-start(bf16[64,1024]{1,0:T(8,128)(2,1)S(1)} %shard_map.115.refs_0_), channel_id=1, source_target_pairs={{0,96},{16,112},{32,0},{48,16},{64,32},{80,48},{96,64},{112,80},{1... | collective-permute-start | bytes 393224 | tf_op jit(solution)/shard_map/ppermute | solution.py:347
  61.9 0.3 collective-permute-start.9
  62.2 1.1 collective-permute-start.8
  63.3 6.3 %all-to-all-done.2 = bf16[128,2,512]{2,1,0:T(2,128)(2,1)S(1)} async-done(((bf16[128,2,512]{2,1,0:T(2,128)(2,1)}), bf16[128,2,512]{2,1,0:T(2,128)(2,1)S(1)}, u32[]{:S(2)}, u32[]{:S(2)}) %all-to-all-start.2) | async-done | bytes 262176 | tf_op jit(solution)/shard_map/all_to_all | solution.py:258
  69.6 0.1 reshape.54.heads_ref
  69.8 0.8 collective-permute-done.9.refs_2_
  70.5 2.2 %collective-permute-done.8.refs_1_ = bf16[64,1024]{1,0:T(8,128)(2,1)S(1)} collective-permute-done((bf16[64,1024]{1,0:T(8,128)(2,1)S(1)}, bf16[64,1024]{1,0:T(8,128)(2,1)S(1)}, u32[]{:S(2)}, u32[]{:S(2)}) %collective-permute-start.8) | collective-permute-done | bytes 131104 | tf_op jit(solution)/shard_map/ppermute | solution.py:347
  72.8 1.7 shard_map.116.refs_8_
  74.6 4.6 %shard_map.117 = bf16[256,1024]{1,0:T(8,128)(2,1)S(1)} custom-call(s32[2]{0:T(128)S(1)} %pad_add_fusion.z_ref.place_ref, bf16[64,1024]{1,0:T(8,128)(2,1)S(1)} %shard_map.115.refs_0_, bf16[64,1024]{1,0:T(8,128)(2,1)S(1)} %collective-permute-done.8.refs_1_, bf16[64,1024]{1,0:T(8,128)(2,1)S(1)} %collective-permute-done.9.refs_2_, ...), custom_call_target="tpu_custom_call" | custom-call | tf_op jit(solution)/shard_map/pallas_call | solution.py:41
  79.2 17.4 %all_to_all.40.delta_ref = bf16[16,16,1024]{2,1,0:T(8,128)(2,1)S(1)} all-to-all(bf16[16,16,1024]{2,1,0:T(8,128)(2,1)S(1)} %bitcast.29), channel_id=1, replica_groups=mesh['gx'=8,'gy'=16] {'gy'}, dimensions={0} | all-to-all | bytes 1048576 | tf_op jit(solution)/shard_map/all_to_all | solution.py:258
  96.6 0.1 shard_map.118
  96.7 14.3 %all_to_all.41 = bf16[16,16,1024]{2,1,0:T(8,128)(2,1)S(1)} all-to-all(bf16[16,16,1024]{2,1,0:T(8,128)(2,1)S(1)} %get-tuple-element.65), channel_id=1, replica_groups=mesh['gx'=8,'gy'=16] {'gy'}, dimensions={0} | all-to-all | bytes 1048576 | tf_op jit(solution)/shard_map/all_to_all | solution.py:258
  111.0 1.8 shard_map.120
  112.9 0.9 reshape.57
  113.7 4.6 %all-to-all-start.5 = ((bf16[128,2,640]{2,1,0:T(2,128)(2,1)}), bf16[128,2,640]{2,1,0:T(2,128)(2,1)S(1)}, u32[]{:S(2)}, u32[]{:S(2)}) async-start(bf16[128,2,640]{2,1,0:T(2,128)(2,1)} %reshape.57), calls=%async_computation.5 | async-start | bytes 655360 | tf_op jit(solution)/shard_map/all_to_all | solution.py:258
  118.3 3.0 %shard_map.121 = (bf16[256,512]{1,0:T(8,128)(2,1)S(1)}, bf16[256,512]{1,0:T(8,128)(2,1)S(1)}, bf16[256,512]{1,0:T(8,128)(2,1)S(1)}, bf16[256,512]{1,0:T(8,128)(2,1)S(1)}) custom-call(s32[1]{0:T(128)S(6)} %xor.4.half_ref, bf16[256,1024]{1,0:T(8,128)(2,1)S(1)} %bitcast.26, bf16[1024,2048]{1,0:T(8,128)(2,1)} %wg_ref.7, bf16[1024,2048]{1,0:T(8,128)(2,1)} %wu_ref.7), custom_call_target="tpu_custom_call" | custom-call | tf_op jit(solution)/shard_map/pallas_call | solution.py:41
  121.5 0.5 collective-permute-start.16
  122.1 0.4 collective-permute-start.18
  122.6 3.0 %shard_map.119 = (bf16[256,512]{1,0:T(8,128)(2,1)S(1)}, bf16[256,512]{1,0:T(8,128)(2,1)S(1)}, bf16[256,512]{1,0:T(8,128)(2,1)S(1)}, bf16[256,512]{1,0:T(8,128)(2,1)S(1)}) custom-call(s32[1]{0:T(128)} %bitcast.1.half_ref, bf16[256,1024]{1,0:T(8,128)(2,1)S(1)} %bitcast.27, bf16[1024,2048]{1,0:T(8,128)(2,1)} %wg_ref.7, bf16[1024,2048]{1,0:T(8,128)(2,1)} %wu_ref.7), custom_call_target="tpu_custom_call" | custom-call | tf_op jit(solution)/shard_map/pallas_call | solution.py:41
  125.7 0.8 shard_map.122
  126.5 1.2 collective-permute-start.20
  127.7 3.2 %collective-permute-start.21 = (bf16[64,2176]{1,0:T(8,128)(2,1)S(1)}, bf16[64,2176]{1,0:T(8,128)(2,1)S(1)}, u32[]{:S(2)}, u32[]{:S(2)}) collective-permute-start(bf16[64,2176]{1,0:T(8,128)(2,1)S(1)} %get-tuple-element.77), channel_id=1, source_target_pairs={{0,64},{16,80},{32,96},{48,112},{64,0},{80,16},{96,32},{112,48},{1... | collective-permute-start | bytes 835592 | tf_op jit(solution)/shard_map/ppermute | solution.py:323
  130.9 1.2 collective-permute-start.22
  132.1 0.3 convert_reduce_fusion
  132.4 0.2 rsqrt_reduce_fusion
  132.8 4.3 %shard_map.123 = bf16[2,16,512]{2,1,0:T(8,128)(2,1)S(1)} custom-call(s32[2]{0:T(128)S(1)} %copy-done.4, bf16[2,16,512]{2,1,0:T(8,128)(2,1)S(1)} %fusion.q_ref, f32[2,512]{1,0:T(2,128)S(1)} %reshape.65.refs_0_, f32[2,512]{1,0:T(2,128)S(1)} %reshape.68.refs_1_, bf16[2,2048,256]{2,1,0:T(8,128)(2,1)} %refs_2_.3, bf16[2,2048,256]{2,1,0:T(8,128)(2,1)} %refs_3_.1), custom_call_target="tpu_custom_call" | custom-call | tf_op jit(solution)/shard_map/pallas_call | solution.py:41
  137.1 0.8 broadcast_in_dim.8
  138.0 7.7 %all-to-all-start.6 = ((bf16[128,2,512]{2,1,0:T(2,128)(2,1)}), bf16[128,2,512]{2,1,0:T(2,128)(2,1)S(1)}, u32[]{:S(2)}, u32[]{:S(2)}) async-start(bf16[128,2,512]{2,1,0:T(2,128)(2,1)} %bitcast.14), calls=%async_computation.6 | async-start | bytes 524288 | tf_op jit(solution)/shard_map/all_to_all | solution.py:258
  145.8 0.3 shard_map.124.refs_0_
  146.0 2.9 %collective-permute-start.25 = (bf16[64,1024]{1,0:T(8,128)(2,1)S(1)}, bf16[64,1024]{1,0:T(8,128)(2,1)S(1)}, u32[]{:S(2)}, u32[]{:S(2)}) collective-permute-start(bf16[64,1024]{1,0:T(8,128)(2,1)S(1)} %shard_map.124.refs_0_), channel_id=1, source_target_pairs={{0,96},{16,112},{32,0},{48,16},{64,32},{80,48},{96,64},{112,80},{1... | collective-permute-start | bytes 393224 | tf_op jit(solution)/shard_map/ppermute | solution.py:347
  148.9 0.3 collective-permute-start.24
  149.3 1.1 collective-permute-start.23
  150.4 6.3 %all-to-all-done.6 = bf16[128,2,512]{2,1,0:T(2,128)(2,1)S(1)} async-done(((bf16[128,2,512]{2,1,0:T(2,128)(2,1)}), bf16[128,2,512]{2,1,0:T(2,128)(2,1)S(1)}, u32[]{:S(2)}, u32[]{:S(2)}) %all-to-all-start.6) | async-done | bytes 262176 | tf_op jit(solution)/shard_map/all_to_all | solution.py:258
  156.6 0.1 reshape.61.heads_ref
  156.9 0.8 collective-permute-done.24.refs_2_
  157.6 2.2 %collective-permute-done.23.refs_1_ = bf16[64,1024]{1,0:T(8,128)(2,1)S(1)} collective-permute-done((bf16[64,1024]{1,0:T(8,128)(2,1)S(1)}, bf16[64,1024]{1,0:T(8,128)(2,1)S(1)}, u32[]{:S(2)}, u32[]{:S(2)}) %collective-permute-start.23) | collective-permute-done | bytes 131104 | tf_op jit(solution)/shard_map/ppermute | solution.py:347
  159.8 1.7 shard_map.125.refs_8_
  161.6 4.6 %shard_map.126 = bf16[256,1024]{1,0:T(8,128)(2,1)S(1)} custom-call(s32[2]{0:T(128)S(1)} %pad_add_fusion.z_ref.place_ref, bf16[64,1024]{1,0:T(8,128)(2,1)S(1)} %shard_map.124.refs_0_, bf16[64,1024]{1,0:T(8,128)(2,1)S(1)} %collective-permute-done.23.refs_1_, bf16[64,1024]{1,0:T(8,128)(2,1)S(1)} %collective-permute-done.24.refs_2_, ...), custom_call_target="tpu_custom_call" | custom-call | tf_op jit(solution)/shard_map/pallas_call | solution.py:41
  166.3 17.4 %all_to_all.42.delta_ref = bf16[16,16,1024]{2,1,0:T(8,128)(2,1)S(1)} all-to-all(bf16[16,16,1024]{2,1,0:T(8,128)(2,1)S(1)} %bitcast.28), channel_id=1, replica_groups=mesh['gx'=8,'gy'=16] {'gy'}, dimensions={0} | all-to-all | bytes 1048576 | tf_op jit(solution)/shard_map/all_to_all | solution.py:258
  183.7 0.7 shard_map.127
  (62 shorter events, 1.5 us)
Async XLA Ops:
  0.0 0.8 copy-start
  0.8 0.7 copy-start.2
  2.4 18.6 %all-to-all-start = ((bf16[16,16,1024]{2,1,0:T(8,128)(2,1)}), bf16[16,16,1024]{2,1,0:T(8,128)(2,1)S(1)}, u32[]{:S(2)}, u32[]{:S(2)}) async-start(bf16[16,16,1024]{2,1,0:T(8,128)(2,1)} %shard_map.109), calls=%async_computation | async-start | bytes 1048576 | tf_op jit(solution)/shard_map/all_to_all | solution.py:258
  23.7 21.4 %all-to-all-start.1 = ((bf16[128,2,640]{2,1,0:T(2,128)(2,1)}), bf16[128,2,640]{2,1,0:T(2,128)(2,1)S(1)}, u32[]{:S(2)}, u32[]{:S(2)}) async-start(bf16[128,2,640]{2,1,0:T(2,128)(2,1)} %reshape.50), calls=%async_computation.1 | async-start | bytes 655360 | tf_op jit(solution)/shard_map/all_to_all | solution.py:258
  34.2 4.3 %collective-permute-start = (bf16[256,512]{1,0:T(8,128)(2,1)S(1)}, bf16[256,512]{1,0:T(8,128)(2,1)S(1)}, u32[]{:S(2)}, u32[]{:S(2)}) collective-permute-start(bf16[256,512]{1,0:T(8,128)(2,1)S(1)} %get-tuple-element.50), channel_id=1, source_target_pairs={{0,16},{16,0},{32,48},{48,32},{64,80},{80,64},{96,112},{112,96},{1... | collective-permute-start | bytes 786440 | tf_op jit(solution)/shard_map/ppermute | solution.py:312
  34.3 4.2 %collective-permute-start.1 = (bf16[256,512]{1,0:T(8,128)(2,1)S(1)}, bf16[256,512]{1,0:T(8,128)(2,1)S(1)}, u32[]{:S(2)}, u32[]{:S(2)}) collective-permute-start(bf16[256,512]{1,0:T(8,128)(2,1)S(1)} %get-tuple-element.51), channel_id=1, source_target_pairs={{0,16},{16,0},{32,48},{48,32},{64,80},{80,64},{96,112},{112,96},{1... | collective-permute-start | bytes 786440 | tf_op jit(solution)/shard_map/ppermute | solution.py:312
  34.8 3.8 %collective-permute-start.2 = (bf16[256,512]{1,0:T(8,128)(2,1)S(1)}, bf16[256,512]{1,0:T(8,128)(2,1)S(1)}, u32[]{:S(2)}, u32[]{:S(2)}) collective-permute-start(bf16[256,512]{1,0:T(8,128)(2,1)S(1)} %get-tuple-element.52), channel_id=1, source_target_pairs={{0,16},{16,0},{32,48},{48,32},{64,80},{80,64},{96,112},{112,96},{1... | collective-permute-start | bytes 786440 | tf_op jit(solution)/shard_map/ppermute | solution.py:312
  34.9 3.7 %collective-permute-start.3 = (bf16[256,512]{1,0:T(8,128)(2,1)S(1)}, bf16[256,512]{1,0:T(8,128)(2,1)S(1)}, u32[]{:S(2)}, u32[]{:S(2)}) collective-permute-start(bf16[256,512]{1,0:T(8,128)(2,1)S(1)} %get-tuple-element.53), channel_id=1, source_target_pairs={{0,16},{16,0},{32,48},{48,32},{64,80},{80,64},{96,112},{112,96},{1... | collective-permute-start | bytes 786440 | tf_op jit(solution)/shard_map/ppermute | solution.py:312
  35.3 3.2 %collective-permute-start.4 = (bf16[256,128]{1,0:T(8,128)(2,1)S(1)}, bf16[256,128]{1,0:T(8,128)(2,1)S(1)}, u32[]{:S(2)}, u32[]{:S(2)}) collective-permute-start(bf16[256,128]{1,0:T(8,128)(2,1)S(1)} %get-tuple-element.49.refs_4_), channel_id=1, source_target_pairs={{0,16},{16,0},{32,48},{48,32},{64,80},{80,64},{96,112},{112,96},{1... | collective-permute-start | bytes 196616 | tf_op jit(solution)/shard_map/ppermute | solution.py:312
  35.5 10.3 %copy-start.4 = (s32[2]{0:T(128)S(1)}, s32[2]{0:T(128)}, u32[]{:S(2)}) copy-start(s32[2]{0:T(128)} %lengths_ref.3) | copy-start | bytes 28
  39.4 19.2 %collective-permute-start.5 = (bf16[64,2176]{1,0:T(8,128)(2,1)S(1)}, bf16[64,2176]{1,0:T(8,128)(2,1)S(1)}, u32[]{:S(2)}, u32[]{:S(2)}) collective-permute-start(bf16[64,2176]{1,0:T(8,128)(2,1)S(1)} %get-tuple-element.55), channel_id=1, source_target_pairs={{0,32},{16,48},{32,64},{48,80},{64,96},{80,112},{96,0},{112,16},{1... | collective-permute-start | bytes 835592 | tf_op jit(solution)/shard_map/ppermute | solution.py:323
  40.6 18.0 %collective-permute-start.6 = (bf16[64,2176]{1,0:T(8,128)(2,1)S(1)}, bf16[64,2176]{1,0:T(8,128)(2,1)S(1)}, u32[]{:S(2)}, u32[]{:S(2)}) collective-permute-start(bf16[64,2176]{1,0:T(8,128)(2,1)S(1)} %get-tuple-element.56), channel_id=1, source_target_pairs={{0,64},{16,80},{32,96},{48,112},{64,0},{80,16},{96,32},{112,48},{1... | collective-permute-start | bytes 835592 | tf_op jit(solution)/shard_map/ppermute | solution.py:323
  43.8 14.8 %collective-permute-start.7 = (bf16[64,2176]{1,0:T(8,128)(2,1)S(1)}, bf16[64,2176]{1,0:T(8,128)(2,1)S(1)}, u32[]{:S(2)}, u32[]{:S(2)}) collective-permute-start(bf16[64,2176]{1,0:T(8,128)(2,1)S(1)} %get-tuple-element.57), channel_id=1, source_target_pairs={{0,96},{16,112},{32,0},{48,16},{64,32},{80,48},{96,64},{112,80},{1... | collective-permute-start | bytes 835592 | tf_op jit(solution)/shard_map/ppermute | solution.py:323
  50.9 18.7 %all-to-all-start.2 = ((bf16[128,2,512]{2,1,0:T(2,128)(2,1)}), bf16[128,2,512]{2,1,0:T(2,128)(2,1)S(1)}, u32[]{:S(2)}, u32[]{:S(2)}) async-start(bf16[128,2,512]{2,1,0:T(2,128)(2,1)} %bitcast.8), calls=%async_computation.2 | async-start | bytes 524288 | tf_op jit(solution)/shard_map/all_to_all | solution.py:258
  59.0 10.7 %collective-permute-start.10 = (bf16[64,1024]{1,0:T(8,128)(2,1)S(1)}, bf16[64,1024]{1,0:T(8,128)(2,1)S(1)}, u32[]{:S(2)}, u32[]{:S(2)}) collective-permute-start(bf16[64,1024]{1,0:T(8,128)(2,1)S(1)} %shard_map.115.refs_0_), channel_id=1, source_target_pairs={{0,96},{16,112},{32,0},{48,16},{64,32},{80,48},{96,64},{112,80},{1... | collective-permute-start | bytes 393224 | tf_op jit(solution)/shard_map/ppermute | solution.py:347
  61.9 8.7 %collective-permute-start.9 = (bf16[64,1024]{1,0:T(8,128)(2,1)S(1)}, bf16[64,1024]{1,0:T(8,128)(2,1)S(1)}, u32[]{:S(2)}, u32[]{:S(2)}) collective-permute-start(bf16[64,1024]{1,0:T(8,128)(2,1)S(1)} %shard_map.115.refs_0_), channel_id=1, source_target_pairs={{0,64},{16,80},{32,96},{48,112},{64,0},{80,16},{96,32},{112,48},{1... | collective-permute-start | bytes 393224 | tf_op jit(solution)/shard_map/ppermute | solution.py:347
  62.2 10.6 %collective-permute-start.8 = (bf16[64,1024]{1,0:T(8,128)(2,1)S(1)}, bf16[64,1024]{1,0:T(8,128)(2,1)S(1)}, u32[]{:S(2)}, u32[]{:S(2)}) collective-permute-start(bf16[64,1024]{1,0:T(8,128)(2,1)S(1)} %shard_map.115.refs_0_), channel_id=1, source_target_pairs={{0,32},{16,48},{32,64},{48,80},{64,96},{80,112},{96,0},{112,16},{1... | collective-permute-start | bytes 393224 | tf_op jit(solution)/shard_map/ppermute | solution.py:347
  63.3 11.2 %collective-permute-start.11 = (bf16[64,1024]{1,0:T(8,128)(2,1)S(1)}, bf16[64,1024]{1,0:T(8,128)(2,1)S(1)}, u32[]{:S(2)}, u32[]{:S(2)}) collective-permute-start(bf16[64,1024]{1,0:T(8,128)(2,1)S(1)} %shard_map.115.refs_0_), channel_id=1, source_target_pairs={{0,16},{16,0},{32,48},{48,32},{64,80},{80,64},{96,112},{112,96},{1... | collective-permute-start | bytes 393224 | tf_op jit(solution)/shard_map/ppermute | solution.py:348
  69.7 4.9 %collective-permute-start.14 = (bf16[64,1024]{1,0:T(8,128)(2,1)S(1)}, bf16[64,1024]{1,0:T(8,128)(2,1)S(1)}, u32[]{:S(2)}, u32[]{:S(2)}) collective-permute-start(bf16[64,1024]{1,0:T(8,128)(2,1)S(1)} %collective-permute-done.10.refs_3_), channel_id=1, source_target_pairs={{0,16},{16,0},{32,48},{48,32},{64,80},{80,64},{96,112},{112,96},{1... | collective-permute-start | bytes 393224 | tf_op jit(solution)/shard_map/ppermute | solution.py:348
  70.5 4.0 %collective-permute-start.13 = (bf16[64,1024]{1,0:T(8,128)(2,1)S(1)}, bf16[64,1024]{1,0:T(8,128)(2,1)S(1)}, u32[]{:S(2)}, u32[]{:S(2)}) collective-permute-start(bf16[64,1024]{1,0:T(8,128)(2,1)S(1)} %collective-permute-done.9.refs_2_), channel_id=1, source_target_pairs={{0,16},{16,0},{32,48},{48,32},{64,80},{80,64},{96,112},{112,96},{1... | collective-permute-start | bytes 393224 | tf_op jit(solution)/shard_map/ppermute | solution.py:348
  72.8 1.8 collective-permute-start.12
  74.5 22.1 %copy-start.1 = (f32[16,1024]{1,0:T(8,128)S(1)}, f32[16,1024]{1,0:T(8,128)}, u32[]{:S(2)}) copy-start(f32[16,1024]{1,0:T(8,128)} %x_ref.3) | copy-start | bytes 196612
  74.5 22.1 %copy-start.3 = (f32[1024]{0:T(1024)S(1)}, f32[1024]{0:T(1024)}, u32[]{:S(2)}) copy-start(f32[1024]{0:T(1024)} %param.12) | copy-start | bytes 12292
  113.7 18.4 %all-to-all-start.5 = ((bf16[128,2,640]{2,1,0:T(2,128)(2,1)}), bf16[128,2,640]{2,1,0:T(2,128)(2,1)S(1)}, u32[]{:S(2)}, u32[]{:S(2)}) async-start(bf16[128,2,640]{2,1,0:T(2,128)(2,1)} %reshape.57), calls=%async_computation.5 | async-start | bytes 655360 | tf_op jit(solution)/shard_map/all_to_all | solution.py:258
  121.4 4.2 %collective-permute-start.15 = (bf16[256,512]{1,0:T(8,128)(2,1)S(1)}, bf16[256,512]{1,0:T(8,128)(2,1)S(1)}, u32[]{:S(2)}, u32[]{:S(2)}) collective-permute-start(bf16[256,512]{1,0:T(8,128)(2,1)S(1)} %get-tuple-element.71), channel_id=1, source_target_pairs={{0,16},{16,0},{32,48},{48,32},{64,80},{80,64},{96,112},{112,96},{1... | collective-permute-start | bytes 786440 | tf_op jit(solution)/shard_map/ppermute | solution.py:312
  121.5 4.1 %collective-permute-start.16 = (bf16[256,512]{1,0:T(8,128)(2,1)S(1)}, bf16[256,512]{1,0:T(8,128)(2,1)S(1)}, u32[]{:S(2)}, u32[]{:S(2)}) collective-permute-start(bf16[256,512]{1,0:T(8,128)(2,1)S(1)} %get-tuple-element.72), channel_id=1, source_target_pairs={{0,16},{16,0},{32,48},{48,32},{64,80},{80,64},{96,112},{112,96},{1... | collective-permute-start | bytes 786440 | tf_op jit(solution)/shard_map/ppermute | solution.py:312
  122.0 3.7 %collective-permute-start.17 = (bf16[256,512]{1,0:T(8,128)(2,1)S(1)}, bf16[256,512]{1,0:T(8,128)(2,1)S(1)}, u32[]{:S(2)}, u32[]{:S(2)}) collective-permute-start(bf16[256,512]{1,0:T(8,128)(2,1)S(1)} %get-tuple-element.73), channel_id=1, source_target_pairs={{0,16},{16,0},{32,48},{48,32},{64,80},{80,64},{96,112},{112,96},{1... | collective-permute-start | bytes 786440 | tf_op jit(solution)/shard_map/ppermute | solution.py:312
  122.1 3.6 %collective-permute-start.18 = (bf16[256,512]{1,0:T(8,128)(2,1)S(1)}, bf16[256,512]{1,0:T(8,128)(2,1)S(1)}, u32[]{:S(2)}, u32[]{:S(2)}) collective-permute-start(bf16[256,512]{1,0:T(8,128)(2,1)S(1)} %get-tuple-element.74), channel_id=1, source_target_pairs={{0,16},{16,0},{32,48},{48,32},{64,80},{80,64},{96,112},{112,96},{1... | collective-permute-start | bytes 786440 | tf_op jit(solution)/shard_map/ppermute | solution.py:312
  122.5 3.1 %collective-permute-start.19 = (bf16[256,128]{1,0:T(8,128)(2,1)S(1)}, bf16[256,128]{1,0:T(8,128)(2,1)S(1)}, u32[]{:S(2)}, u32[]{:S(2)}) collective-permute-start(bf16[256,128]{1,0:T(8,128)(2,1)S(1)} %get-tuple-element.70.refs_4_), channel_id=1, source_target_pairs={{0,16},{16,0},{32,48},{48,32},{64,80},{80,64},{96,112},{112,96},{1... | collective-permute-start | bytes 196616 | tf_op jit(solution)/shard_map/ppermute | solution.py:312
  126.5 19.2 %collective-permute-start.20 = (bf16[64,2176]{1,0:T(8,128)(2,1)S(1)}, bf16[64,2176]{1,0:T(8,128)(2,1)S(1)}, u32[]{:S(2)}, u32[]{:S(2)}) collective-permute-start(bf16[64,2176]{1,0:T(8,128)(2,1)S(1)} %get-tuple-element.76), channel_id=1, source_target_pairs={{0,32},{16,48},{32,64},{48,80},{64,96},{80,112},{96,0},{112,16},{1... | collective-permute-start | bytes 835592 | tf_op jit(solution)/shard_map/ppermute | solution.py:323
  127.7 18.0 %collective-permute-start.21 = (bf16[64,2176]{1,0:T(8,128)(2,1)S(1)}, bf16[64,2176]{1,0:T(8,128)(2,1)S(1)}, u32[]{:S(2)}, u32[]{:S(2)}) collective-permute-start(bf16[64,2176]{1,0:T(8,128)(2,1)S(1)} %get-tuple-element.77), channel_id=1, source_target_pairs={{0,64},{16,80},{32,96},{48,112},{64,0},{80,16},{96,32},{112,48},{1... | collective-permute-start | bytes 835592 | tf_op jit(solution)/shard_map/ppermute | solution.py:323
  130.9 14.8 %collective-permute-start.22 = (bf16[64,2176]{1,0:T(8,128)(2,1)S(1)}, bf16[64,2176]{1,0:T(8,128)(2,1)S(1)}, u32[]{:S(2)}, u32[]{:S(2)}) collective-permute-start(bf16[64,2176]{1,0:T(8,128)(2,1)S(1)} %get-tuple-element.78), channel_id=1, source_target_pairs={{0,96},{16,112},{32,0},{48,16},{64,32},{80,48},{96,64},{112,80},{1... | collective-permute-start | bytes 835592 | tf_op jit(solution)/shard_map/ppermute | solution.py:323
  138.0 18.7 %all-to-all-start.6 = ((bf16[128,2,512]{2,1,0:T(2,128)(2,1)}), bf16[128,2,512]{2,1,0:T(2,128)(2,1)S(1)}, u32[]{:S(2)}, u32[]{:S(2)}) async-start(bf16[128,2,512]{2,1,0:T(2,128)(2,1)} %bitcast.14), calls=%async_computation.6 | async-start | bytes 524288 | tf_op jit(solution)/shard_map/all_to_all | solution.py:258
  146.0 10.7 %collective-permute-start.25 = (bf16[64,1024]{1,0:T(8,128)(2,1)S(1)}, bf16[64,1024]{1,0:T(8,128)(2,1)S(1)}, u32[]{:S(2)}, u32[]{:S(2)}) collective-permute-start(bf16[64,1024]{1,0:T(8,128)(2,1)S(1)} %shard_map.124.refs_0_), channel_id=1, source_target_pairs={{0,96},{16,112},{32,0},{48,16},{64,32},{80,48},{96,64},{112,80},{1... | collective-permute-start | bytes 393224 | tf_op jit(solution)/shard_map/ppermute | solution.py:347
  148.9 8.7 %collective-permute-start.24 = (bf16[64,1024]{1,0:T(8,128)(2,1)S(1)}, bf16[64,1024]{1,0:T(8,128)(2,1)S(1)}, u32[]{:S(2)}, u32[]{:S(2)}) collective-permute-start(bf16[64,1024]{1,0:T(8,128)(2,1)S(1)} %shard_map.124.refs_0_), channel_id=1, source_target_pairs={{0,64},{16,80},{32,96},{48,112},{64,0},{80,16},{96,32},{112,48},{1... | collective-permute-start | bytes 393224 | tf_op jit(solution)/shard_map/ppermute | solution.py:347
  149.3 10.6 %collective-permute-start.23 = (bf16[64,1024]{1,0:T(8,128)(2,1)S(1)}, bf16[64,1024]{1,0:T(8,128)(2,1)S(1)}, u32[]{:S(2)}, u32[]{:S(2)}) collective-permute-start(bf16[64,1024]{1,0:T(8,128)(2,1)S(1)} %shard_map.124.refs_0_), channel_id=1, source_target_pairs={{0,32},{16,48},{32,64},{48,80},{64,96},{80,112},{96,0},{112,16},{1... | collective-permute-start | bytes 393224 | tf_op jit(solution)/shard_map/ppermute | solution.py:347
  150.4 11.2 %collective-permute-start.26 = (bf16[64,1024]{1,0:T(8,128)(2,1)S(1)}, bf16[64,1024]{1,0:T(8,128)(2,1)S(1)}, u32[]{:S(2)}, u32[]{:S(2)}) collective-permute-start(bf16[64,1024]{1,0:T(8,128)(2,1)S(1)} %shard_map.124.refs_0_), channel_id=1, source_target_pairs={{0,16},{16,0},{32,48},{48,32},{64,80},{80,64},{96,112},{112,96},{1... | collective-permute-start | bytes 393224 | tf_op jit(solution)/shard_map/ppermute | solution.py:348
  156.8 4.8 %collective-permute-start.29 = (bf16[64,1024]{1,0:T(8,128)(2,1)S(1)}, bf16[64,1024]{1,0:T(8,128)(2,1)S(1)}, u32[]{:S(2)}, u32[]{:S(2)}) collective-permute-start(bf16[64,1024]{1,0:T(8,128)(2,1)S(1)} %collective-permute-done.25.refs_3_), channel_id=1, source_target_pairs={{0,16},{16,0},{32,48},{48,32},{64,80},{80,64},{96,112},{112,96},{1... | collective-permute-start | bytes 393224 | tf_op jit(solution)/shard_map/ppermute | solution.py:348
  157.6 4.0 %collective-permute-start.28 = (bf16[64,1024]{1,0:T(8,128)(2,1)S(1)}, bf16[64,1024]{1,0:T(8,128)(2,1)S(1)}, u32[]{:S(2)}, u32[]{:S(2)}) collective-permute-start(bf16[64,1024]{1,0:T(8,128)(2,1)S(1)} %collective-permute-done.24.refs_2_), channel_id=1, source_target_pairs={{0,16},{16,0},{32,48},{48,32},{64,80},{80,64},{96,112},{112,96},{1... | collective-permute-start | bytes 393224 | tf_op jit(solution)/shard_map/ppermute | solution.py:348
  159.8 1.8 collective-permute-start.27

commit v3 on v2

v3 whole, which is shorter than its diff:
```python
import functools

import jax
import jax.numpy as jnp
from jax import lax
from jax.experimental import pallas as pl
from jax.experimental.pallas import tpu as pltpu
from jax.sharding import PartitionSpec as P

D = 8192
HEADS = 32
DH = 256
STEPS = 2
EPS = 1e-06
LANES = 128
F32 = jnp.float32
BF16 = jnp.bfloat16
PARAMS = pltpu.CompilerParams(vmem_limit_bytes=16 * 1024 * 1024)
VMEM = pl.BlockSpec(memory_space=pltpu.VMEM)
SMEM = pl.BlockSpec(memory_space=pltpu.SMEM)
COST = pl.CostEstimate(flops=0, bytes_accessed=0, transcendentals=0)
LATE = pl.CostEstimate(flops=10**10, bytes_accessed=0, transcendentals=0)


def dot32(a, b):
    return jnp.dot(a, b, preferred_element_type=F32)


HBM = pl.BlockSpec(memory_space=pltpu.HBM)


def call(kernel, out_shape, *args, scalars=0, far=0, copies=0, buffers=(), cost=COST):
    near = len(args) - scalars - far
    far_args = [pltpu.with_memory_space_constraint(a, pltpu.HBM) for a in args[scalars + near :]]
    scratch = list(buffers)
    if copies:
        scratch.append(pltpu.SemaphoreType.DMA((copies,)))
    return pl.pallas_call(
        kernel,
        out_shape=out_shape,
        in_specs=[SMEM] * scalars + [VMEM] * near + [HBM] * far,
        scratch_shapes=scratch,
        compiler_params=PARAMS,
        cost_estimate=cost,
    )(*args[: scalars + near], *far_args)


def start_copies(pairs, sems):
    copies = [
        pltpu.make_async_copy(source, target, sems.at[n]) for n, (source, target) in enumerate(pairs)
    ]
    for copy in copies:
        copy.start()
    return copies


def spread_kernel(x_ref, gain_ref, out_ref, x, gain, sems):
    for copy in start_copies([(x_ref, x), (gain_ref, gain)], sems):
        copy.wait()
    scaled = (x[...] * gain[...]).astype(BF16)
    for n in range(out_ref.shape[0]):
        out_ref[n] = scaled


def add_kernel(x_ref, delta_ref, gain_ref, new_ref, out_ref=None):
    new = x_ref[...] + jnp.sum(delta_ref[...].astype(F32), axis=0)
    new_ref[...] = new
    if out_ref is not None:
        scaled = (new * gain_ref[...]).astype(BF16)
        for n in range(out_ref.shape[0]):
            out_ref[n] = scaled


def query_kernel(kv_cols, x_ref, inverse_ref, wkv_ref, wq_ref, out_ref, squares_ref):
    x = x_ref[...]
    plain = x.astype(F32) * inverse_ref[...]
    squares = jnp.sum(plain * plain, axis=1, keepdims=True)
    high = squares.astype(BF16).astype(F32)
    low = squares - high
    lane = lax.broadcasted_iota(jnp.int32, squares_ref.shape, 1)
    columns = jnp.where(lane == kv_cols, high, jnp.where(lane == kv_cols + 1, low, 0.0))
    squares_ref[...] = columns.astype(BF16)
    q_cols = wq_ref.shape[1]
    out_ref[:, :q_cols] = dot32(x, wq_ref[...]).astype(BF16)
    out_ref[:, q_cols:] = (dot32(x, wkv_ref[...]) + columns).astype(BF16)


def hidden_part_kernel(half_ref, x_ref, wg_ref, wu_ref, *outs):
    block = wg_ref.shape[1]
    wide = outs[0].shape[1]
    for n in range(len(outs) // 2 * (wide // block)):

        @pl.when(pl.program_id(0) == n)
        def _():
            at = n * block
            for k, ref in enumerate((wg_ref, wu_ref)):
                outs[at // wide * 2 + k][:, at % wide : at % wide + block] = dot32(
                    x_ref[...], ref[...]
                ).astype(BF16)


def hidden_part(half_index, x, w_gate, w_up, outs=2, blocks=2):
    rows, width = x.shape
    half = w_gate.shape[1] // 2
    weight = pl.BlockSpec((width, half // blocks), lambda n, h: (0, h[0] * blocks + n))
    part = jax.ShapeDtypeStruct((rows, half // outs), BF16)
    return pl.pallas_call(
        hidden_part_kernel,
        out_shape=[part] * (2 * outs),
        grid_spec=pltpu.PrefetchScalarGridSpec(
            num_scalar_prefetch=1,
            grid=(blocks,),
            in_specs=[pl.BlockSpec(x.shape, lambda n, h: (0, 0)), weight, weight],
            out_specs=[pl.BlockSpec(part.shape, lambda n, h: (0, 0))] * (2 * outs),
        ),
        compiler_params=PARAMS,
        cost_estimate=COST,
    )(
        half_index,
        x,
        pltpu.with_memory_space_constraint(w_gate, pltpu.HBM),
        pltpu.with_memory_space_constraint(w_up, pltpu.HBM),
    )


def pair_kernel(gz, z_ref, *refs):
    outs = refs[-gz:]
    count = (len(refs) - gz) // 2
    half = sum(ref.shape[1] for ref in refs[: count - 1]) // 2
    size = outs[0].shape[0]
    for n in range(gz):
        here = pl.ds(pl.multiple_of(lax.rem(z_ref[0] + n, gz) * size, size), size)
        for k in range(count):
            keep, other = refs[k], refs[count + k]
            block = keep.shape[1]
            at = 2 * half if k == count - 1 else k % 2 * half + k // 2 * block
            outs[n][:, at : at + block] = (
                keep[here, :].astype(F32) + other[here, :].astype(F32)
            ).astype(BF16)


def hidden_kernel(kv_cols, *refs):
    out_ref = refs[-1]
    half = out_ref.shape[1]
    total = refs[0][...].astype(F32)
    for ref in refs[1:-1]:
        total = total + ref[...].astype(F32)
    at = 2 * half + kv_cols
    scale = lax.rsqrt((total[:, at : at + 1] + total[:, at + 1 : at + 2]) / D + EPS)
    gate = total[:, :half] * scale
    up = total[:, half : 2 * half] * scale
    out_ref[...] = (gate / (1.0 + jnp.exp(-gate)) * up).astype(BF16)


def attend_kernel(steps, lengths_ref, q_ref, *refs):
    news = refs[:steps]
    keys_ref, values_ref, out_ref, keys, values, sems = refs[steps:]
    rows = q_ref.shape[0]
    key_copies = start_copies(
        [(keys_ref.at[row], keys.at[row]) for row in range(rows)], sems.at[:rows]
    )
    scale = DH**-0.5
    heads, scores, new_scores, new_values = [], [], [], []
    for row in range(rows):
        q = q_ref[row]
        heads.append(jnp.concatenate([q[:, :DH], q[:, DH:]], axis=0))
        heads32 = heads[row].astype(F32)
        lines = [ref[row : row + 1, :] for ref in news]
        new_scores.append(
            [jnp.sum(heads32 * line[:, :DH], axis=1, keepdims=True) * scale for line in lines]
        )
        new_values.append([line[:, DH:] for line in lines])
    for copy in key_copies:
        copy.wait()
    value_copies = start_copies(
        [(values_ref.at[row], values.at[row]) for row in range(rows)], sems.at[rows:]
    )
    for row in range(rows):
        old_s = lax.dot_general(
            heads[row], keys[row], (((1,), (1,)), ((), ())), preferred_element_type=F32
        )
        place = lax.broadcasted_iota(jnp.int32, old_s.shape, 1)
        scores.append(jnp.where(place < lengths_ref[row], old_s * scale, -jnp.inf))
    weights = []
    for row in range(rows):
        top = jnp.max(scores[row], axis=1, keepdims=True)
        for score in new_scores[row]:
            top = jnp.maximum(top, score)
        old_e = jnp.exp(scores[row] - top)
        new_e = [jnp.exp(score - top) for score in new_scores[row]]
        total = jnp.sum(old_e, axis=1, keepdims=True)
        for e in new_e:
            total = total + e
        weights.append(((old_e / total).astype(BF16), [(e / total).astype(BF16) for e in new_e]))
    for copy in value_copies:
        copy.wait()
    for row in range(rows):
        old_w, new_w = weights[row]
        result = dot32(old_w, values[row])
        for w, v in zip(new_w, new_values[row]):
            result = result + w.astype(F32) * v
        count = q_ref.shape[1]
        out_ref[row] = jnp.concatenate([result[:count], result[count:]], axis=1).astype(BF16)


def attend(lengths, query, news, keys, values):
    return call(
        functools.partial(attend_kernel, len(news)),
        jax.ShapeDtypeStruct(query.shape, BF16),
        lengths,
        query,
        *news,
        keys,
        values,
        scalars=1,
        far=2,
        copies=2 * keys.shape[0],
        buffers=[pltpu.VMEM(keys.shape, BF16), pltpu.VMEM(values.shape, BF16)],
    )


def heads_kernel(blocks, heads_ref, wout_ref, down_ref, out_ref, held_ref, buffer, sems):
    width = out_ref.shape[1]
    block = width // blocks
    spots = [pl.ds(at, block) for at in range(0, width, block)]
    pairs = [(wout_ref.at[:, spot], buffer.at[:, spot]) for spot in spots]
    pairs += [(down_ref.at[:, spot], held_ref.at[:, spot]) for spot in spots]
    copies = start_copies(pairs, sems)
    for n, spot in enumerate(spots):
        copies[n].wait()
        out_ref[:, spot] = dot32(heads_ref[...], buffer[:, spot])
    for copy in copies[blocks:]:
        copy.wait()


def heads_output(heads, w_out, w_down, blocks=4):
    width = w_out.shape[1]
    return call(
        functools.partial(heads_kernel, blocks),
        [
            jax.ShapeDtypeStruct((heads.shape[0], width), F32),
            pltpu.VMEM(w_down.shape, w_down.dtype),
        ],
        heads,
        w_out,
        w_down,
        far=2,
        copies=2 * blocks,
        buffers=[pltpu.VMEM(w_out.shape, BF16)],
        cost=LATE,
    )


def output_kernel(gz, block, place_ref, *refs):
    pieces, others = refs[:gz], refs[gz : 2 * gz]
    heads_ref, down_ref, out_ref, hidden = refs[2 * gz :]
    size, half = pieces[0].shape
    z, c = place_ref[0], place_ref[1]
    mine = pl.ds(pl.multiple_of(c * half, half), half)
    theirs = pl.ds(pl.multiple_of((1 - c) * half, half), half)
    for n in range(gz):
        at = pl.ds(pl.multiple_of(lax.rem(z + gz - n, gz) * size, size), size)
        hidden[at, mine] = pieces[n][...]
        hidden[at, theirs] = others[n][...]
    for at in range(0, out_ref.shape[1], block):
        out_ref[:, at : at + block] = (
            dot32(hidden[...], down_ref[:, at : at + block]) + heads_ref[:, at : at + block]
        ).astype(BF16)


def output_part(place, pieces, others, heads_part, w_down):
    return call(
        functools.partial(output_kernel, len(pieces), 512),
        jax.ShapeDtypeStruct(heads_part.shape, BF16),
        place,
        *pieces,
        *others,
        heads_part,
        w_down,
        scalars=1,
        buffers=[pltpu.VMEM((heads_part.shape[0], w_down.shape[0]), BF16)],
    )


def make_body(gx, gy):
    gz = gx // 2
    core_swap = [(n, n ^ 1) for n in range(gx)]

    def z_shift(n):
        return [(2 * z + c, 2 * ((z + n) % gz) + c) for z in range(gz) for c in range(2)]

    def exchange(parts, axis):
        return lax.all_to_all(parts, axis, split_axis=0, concat_axis=0, tiled=False)

    def body(
        residual,
        norm_gain,
        w_gate,
        w_up,
        w_query,
        w_keyval,
        w_down,
        w_out,
        cache_keys,
        cache_values,
        lengths,
    ):
        stream = residual
        own_rows, width = residual.shape
        rows = own_rows * gy
        half = w_gate.shape[1] // 2
        q_cols = w_query.shape[1]
        kv_cols = w_keyval.shape[1]
        cache_rows = cache_keys.shape[0]
        me = lax.axis_index("gx")
        z, core = me // 2, lax.rem(me, 2)
        place = jnp.stack([z, core]).astype(jnp.int32)
        gain = norm_gain[None, :]
        inverse_gain = 1.0 / gain
        keyval_padded = jnp.pad(w_keyval, ((0, 0), (0, LANES - kv_cols)))
        news = []
        spread = call(
            spread_kernel,
            jax.ShapeDtypeStruct((gy, own_rows, width), BF16),
            stream,
            gain,
            far=2,
            copies=2,
            buffers=[pltpu.VMEM(stream.shape, F32), pltpu.VMEM(gain.shape, F32)],
        )
        for step in range(STEPS):
            gathered = exchange(spread, "gy").reshape(rows, width)
            packed, squares = call(
                functools.partial(query_kernel, kv_cols),
                (
                    jax.ShapeDtypeStruct((rows, q_cols + LANES), BF16),
                    jax.ShapeDtypeStruct((rows, LANES), BF16),
                ),
                gathered,
                inverse_gain,
                keyval_padded,
                w_query,
            )
            packed = exchange(
                packed.reshape(gx * gy, cache_rows, q_cols + LANES), ("gx", "gy")
            )

            give = hidden_part(place[1:] ^ 1, gathered, w_gate, w_up)
            other = [lax.ppermute(part, "gx", core_swap) for part in (*give, squares)]
            keep = hidden_part(place[1:], gathered, w_gate, w_up)
            pair = call(
                functools.partial(pair_kernel, gz),
                [jax.ShapeDtypeStruct((rows // gz, 2 * half + LANES), BF16)] * gz,
                place,
                *keep,
                squares,
                *other,
                scalars=1,
            )
            arrived = [pair[0]] + [lax.ppermute(pair[n], "gx", z_shift(n)) for n in range(1, gz)]

            packed = lax.optimization_barrier((packed, pair[0]))[0]
            mine = jnp.sum(
                packed.reshape(gx, gy, cache_rows, q_cols + LANES).astype(F32), axis=0
            ).transpose(1, 0, 2)
            at = q_cols + kv_cols
            scale = lax.rsqrt((mine[:, :1, at : at + 1] + mine[:, :1, at + 1 : at + 2]) / D + EPS)
            query = (mine[:, :, :q_cols] * scale).astype(BF16)
            keyval = (mine[:, :, q_cols:at] * scale).astype(BF16).astype(F32)
            news.append(keyval.reshape(cache_rows, 2 * DH))
            attended = attend(lengths, query, news, cache_keys, cache_values)
            blocks = attended.transpose(1, 0, 2)
            blocks = jnp.broadcast_to(blocks[None], (gx, gy, cache_rows, q_cols))
            blocks = blocks.reshape(gx * gy, cache_rows, q_cols)
            heads_all = exchange(blocks, ("gx", "gy")).reshape(rows, q_cols)
            heads_part, held_down = heads_output(heads_all, w_out, w_down)

            arrived = lax.optimization_barrier((arrived, blocks))[0]
            hidden = call(
                functools.partial(hidden_kernel, kv_cols),
                jax.ShapeDtypeStruct((rows // gz, half), BF16),
                *arrived,
            )
            pieces = [hidden] + [lax.ppermute(hidden, "gx", z_shift(n)) for n in range(1, gz)]
            others = [lax.ppermute(piece, "gx", core_swap) for piece in pieces]
            delta = output_part(place, pieces, others, heads_part, held_down)
            delta = exchange(delta.reshape(gy, own_rows, width), "gy")
            stream_shape = jax.ShapeDtypeStruct(stream.shape, F32)
            spread_shape = jax.ShapeDtypeStruct((gy, own_rows, width), BF16)
            if step + 1 < STEPS:
                stream, spread = call(
                    add_kernel, (stream_shape, spread_shape), stream, delta, gain
                )
            else:
                stream = call(add_kernel, stream_shape, stream, delta, gain)
        return stream

    return body


def solution(mesh):
    in_specs = (
        P("gy", "gx"),
        P("gx"),
        P("gx", "gy"),
        P("gx", "gy"),
        P("gx", "gy"),
        P("gx", "gy"),
        P("gy", "gx"),
        P("gy", "gx"),
        P(("gx", "gy"), None, None),
        P(("gx", "gy"), None, None),
        P(("gx", "gy")),
    )
    return jax.shard_map(
        make_body(mesh.shape["gx"], mesh.shape["gy"]),
        mesh=mesh,
        in_specs=in_specs,
        out_specs=P("gy", "gx"),
        check_vma=False,
    )
```

time: 185 us -> 179 us (0.968)
  Pallas kernels: 40.8 us -> 35.3 us
    pallas_call x10 -> x4, Pallas kernels: 33.4 us -> 12.1 us  [hidden_part(): pl.pallas_call(hidden_part_kernel, out_shape=[part] * (2 * outs), grid_sp...]
    pallas_call x9 -> x15, Pallas kernels: 7.45 us -> 23.2 us  [call(): pl.pallas_call(kernel, out_shape=out_shape, in_specs=[SMEM] * scalars + [...]
  transfers between devices with their start and end apart: 35 -> 35, of which waited for: 7 -> 7; matrix products, arithmetic and copies ran while one was open for 3% -> 3% of each run, Pallas kernels for 14% -> 16%
where the time goes in v3:
time: 179 us
  starting transfers between devices  57.2 us (32%)
  blocking collectives  49.1 us (27%)
  Pallas kernels  35.3 us (20%)
  waiting for transfers between devices  28.2 us (16%)
  local copies, waits for them, and re-layouts  6.16 us (3%)
  other arithmetic  1.97 us (1%)
    all_to_all x3, blocking collectives, exchange(): return lax.all_to_all(parts, axis, split_axis=0, concat_axis=0, tiled=False)  49.1 us
    all_to_all x5, starting transfers between devices, exchange(): return lax.all_to_all(parts, axis, split_axis=0, concat_axis=0, tiled=False)  34.7 us
    pallas_call x15, Pallas kernels, call(): pl.pallas_call(kernel, out_shape=out_shape, in_specs=[SMEM] * scalars + [...  23.2 us
    all_to_all x5, waiting for transfers between devices, exchange(): return lax.all_to_all(parts, axis, split_axis=0, concat_axis=0, tiled=False)  22.2 us
    pallas_call x4, Pallas kernels, hidden_part(): pl.pallas_call(hidden_part_kernel, out_shape=[part] * (2 * outs), grid_sp...  12.1 us
    ppermute x6, starting transfers between devices, body(): lax.ppermute(pair[n], 'gx', z_shift(n))  11.3 us
    ppermute x6, starting transfers between devices, body(): lax.ppermute(hidden, 'gx', z_shift(n))  8.69 us
    ppermute x6, waiting for transfers between devices, body(): lax.ppermute(hidden, 'gx', z_shift(n))  5.94 us
  transfers between devices with their start and end apart: 35, of which 7 were waited for; matrix products, arithmetic and copies ran while one was open for 3% of the time, Pallas kernels for 16%

profile of v3, /device:TPU:0, one launch (start us, length us, event | category | flops | bytes accessed | tf_op | source)
XLA Modules:
  0.0 178.6 jit_solution(327320493545814332)
XLA Ops:
  0.0 1.7 shard_map.109
  1.7 7.1 %all-to-all-start = ((bf16[16,16,1024]{2,1,0:T(8,128)(2,1)}), bf16[16,16,1024]{2,1,0:T(8,128)(2,1)S(1)}, u32[]{:S(2)}, u32[]{:S(2)}) async-start(bf16[16,16,1024]{2,1,0:T(8,128)(2,1)} %shard_map.109), calls=%async_computation | async-start | bytes 1048576 | tf_op jit(solution)/shard_map/all_to_all | solution.py:293
  8.9 1.0 copy.18
  9.9 0.7 broadcast_divide_fusion
  10.6 9.7 %all-to-all-done = bf16[16,16,1024]{2,1,0:T(8,128)(2,1)S(1)} async-done(((bf16[16,16,1024]{2,1,0:T(8,128)(2,1)}), bf16[16,16,1024]{2,1,0:T(8,128)(2,1)S(1)}, u32[]{:S(2)}, u32[]{:S(2)}) %all-to-all-start) | async-done | bytes 524320 | tf_op jit(solution)/shard_map/all_to_all | solution.py:293
  20.3 1.2 copy-done
  21.6 0.6 shard_map.111
  22.2 0.9 reshape.50
  23.0 7.5 %all-to-all-start.1 = ((bf16[128,2,640]{2,1,0:T(2,128)(2,1)}), bf16[128,2,640]{2,1,0:T(2,128)(2,1)S(1)}, u32[]{:S(2)}, u32[]{:S(2)}) async-start(bf16[128,2,640]{2,1,0:T(2,128)(2,1)} %reshape.50), calls=%async_computation.1 | async-start | bytes 655360 | tf_op jit(solution)/shard_map/all_to_all | solution.py:293
  30.6 3.0 %shard_map.112 = (bf16[256,512]{1,0:T(8,128)(2,1)S(1)}, bf16[256,512]{1,0:T(8,128)(2,1)S(1)}, bf16[256,512]{1,0:T(8,128)(2,1)S(1)}, bf16[256,512]{1,0:T(8,128)(2,1)S(1)}) custom-call(s32[1]{0:T(128)S(6)} %xor.4.half_ref, bf16[256,1024]{1,0:T(8,128)(2,1)S(1)} %bitcast.23, bf16[1024,2048]{1,0:T(8,128)(2,1)} %wg_ref.7, bf16[1024,2048]{1,0:T(8,128)(2,1)} %wu_ref.7), custom_call_target="tpu_custom_call" | custom-call | tf_op jit(solution)/shard_map/pallas_call | solution.py:107
  33.7 0.5 collective-permute-start.1
  34.3 0.4 collective-permute-start.3
  34.7 0.1 collective-permute-start.4
  34.9 3.0 %shard_map.110 = (bf16[256,512]{1,0:T(8,128)(2,1)S(1)}, bf16[256,512]{1,0:T(8,128)(2,1)S(1)}, bf16[256,512]{1,0:T(8,128)(2,1)S(1)}, bf16[256,512]{1,0:T(8,128)(2,1)S(1)}) custom-call(s32[1]{0:T(128)} %bitcast.1.half_ref, bf16[256,1024]{1,0:T(8,128)(2,1)S(1)} %bitcast.24, bf16[1024,2048]{1,0:T(8,128)(2,1)} %wg_ref.7, bf16[1024,2048]{1,0:T(8,128)(2,1)} %wu_ref.7), custom_call_target="tpu_custom_call" | custom-call | tf_op jit(solution)/shard_map/pallas_call | solution.py:107
  38.0 0.8 shard_map.113
  38.8 1.2 collective-permute-start.5
  40.0 3.2 %collective-permute-start.6 = (bf16[64,2176]{1,0:T(8,128)(2,1)S(1)}, bf16[64,2176]{1,0:T(8,128)(2,1)S(1)}, u32[]{:S(2)}, u32[]{:S(2)}) collective-permute-start(bf16[64,2176]{1,0:T(8,128)(2,1)S(1)} %get-tuple-element.60), channel_id=1, source_target_pairs={{0,64},{16,80},{32,96},{48,112},{64,0},{80,16},{96,32},{112,48},{1... | collective-permute-start | bytes 835592 | tf_op jit(solution)/shard_map/ppermute | solution.py:360
  43.2 1.2 collective-permute-start.7
  44.4 0.3 convert_reduce_fusion.1
  44.7 0.2 rsqrt_reduce_fusion.1
  45.1 4.1 %shard_map.114 = bf16[2,16,512]{2,1,0:T(8,128)(2,1)S(1)} custom-call(s32[2]{0:T(128)S(1)} %copy-done.4, bf16[2,16,512]{2,1,0:T(8,128)(2,1)S(1)} %fusion.1.q_ref, f32[2,512]{1,0:T(2,128)S(1)} %reshape.65.refs_0_, bf16[2,2048,256]{2,1,0:T(8,128)(2,1)} %refs_2_.3, bf16[2,2048,256]{2,1,0:T(8,128)(2,1)} %refs_3_.1), custom_call_target="tpu_custom_call" | custom-call | tf_op jit(solution)/shard_map/pallas_call | solution.py:38
  49.3 0.8 broadcast_in_dim.7
  50.2 7.7 %all-to-all-start.2 = ((bf16[128,2,512]{2,1,0:T(2,128)(2,1)}), bf16[128,2,512]{2,1,0:T(2,128)(2,1)S(1)}, u32[]{:S(2)}, u32[]{:S(2)}) async-start(bf16[128,2,512]{2,1,0:T(2,128)(2,1)} %bitcast.8), calls=%async_computation.2 | async-start | bytes 524288 | tf_op jit(solution)/shard_map/all_to_all | solution.py:293
  57.9 0.3 shard_map.115.refs_0_
  58.2 2.9 %collective-permute-start.10 = (bf16[64,1024]{1,0:T(8,128)(2,1)S(1)}, bf16[64,1024]{1,0:T(8,128)(2,1)S(1)}, u32[]{:S(2)}, u32[]{:S(2)}) collective-permute-start(bf16[64,1024]{1,0:T(8,128)(2,1)S(1)} %shard_map.115.refs_0_), channel_id=1, source_target_pairs={{0,96},{16,112},{32,0},{48,16},{64,32},{80,48},{96,64},{112,80},{1... | collective-permute-start | bytes 393224 | tf_op jit(solution)/shard_map/ppermute | solution.py:384
  61.1 0.3 collective-permute-start.9
  61.4 1.1 collective-permute-start.8
  62.6 6.3 %all-to-all-done.2 = bf16[128,2,512]{2,1,0:T(2,128)(2,1)S(1)} async-done(((bf16[128,2,512]{2,1,0:T(2,128)(2,1)}), bf16[128,2,512]{2,1,0:T(2,128)(2,1)S(1)}, u32[]{:S(2)}, u32[]{:S(2)}) %all-to-all-start.2) | async-done | bytes 262176 | tf_op jit(solution)/shard_map/all_to_all | solution.py:293
  68.8 0.1 reshape.54.heads_ref
  69.0 0.8 collective-permute-done.9.refs_2_
  69.8 2.2 %collective-permute-done.8.refs_1_ = bf16[64,1024]{1,0:T(8,128)(2,1)S(1)} collective-permute-done((bf16[64,1024]{1,0:T(8,128)(2,1)S(1)}, bf16[64,1024]{1,0:T(8,128)(2,1)S(1)}, u32[]{:S(2)}, u32[]{:S(2)}) %collective-permute-start.8) | collective-permute-done | bytes 131104 | tf_op jit(solution)/shard_map/ppermute | solution.py:384
  72.0 2.6 %shard_map.116 = (f32[256,1024]{1,0:T(8,128)S(1)}, bf16[2048,1024]{1,0:T(8,128)(2,1)S(1)}) custom-call(bf16[256,512]{1,0:T(8,128)(2,1)S(1)} %reshape.54.heads_ref, bf16[512,1024]{1,0:T(8,128)(2,1)} %wout_ref.3, bf16[2048,1024]{1,0:T(8,128)(2,1)} %down_ref.3), custom_call_target="tpu_custom_call" | custom-call | flops 10000000000 | tf_op jit(solution)/shard_map/pallas_call | solution.py:38
  74.7 1.9 %shard_map.117 = bf16[256,1024]{1,0:T(8,128)(2,1)S(1)} custom-call(s32[2]{0:T(128)S(1)} %pad_add_fusion.z_ref.place_ref, bf16[64,1024]{1,0:T(8,128)(2,1)S(1)} %shard_map.115.refs_0_, bf16[64,1024]{1,0:T(8,128)(2,1)S(1)} %collective-permute-done.8.refs_1_, bf16[64,1024]{1,0:T(8,128)(2,1)S(1)} %collective-permute-done.9.refs_2_, ...), custom_call_target="tpu_custom_call" | custom-call | tf_op jit(solution)/shard_map/pallas_call | solution.py:38
  76.6 17.4 %all_to_all.40.delta_ref = bf16[16,16,1024]{2,1,0:T(8,128)(2,1)S(1)} all-to-all(bf16[16,16,1024]{2,1,0:T(8,128)(2,1)S(1)} %bitcast.29), channel_id=1, replica_groups=mesh['gx'=8,'gy'=16] {'gy'}, dimensions={0} | all-to-all | bytes 1048576 | tf_op jit(solution)/shard_map/all_to_all | solution.py:293
  94.0 0.1 shard_map.118
  94.1 14.3 %all_to_all.41 = bf16[16,16,1024]{2,1,0:T(8,128)(2,1)S(1)} all-to-all(bf16[16,16,1024]{2,1,0:T(8,128)(2,1)S(1)} %get-tuple-element.71), channel_id=1, replica_groups=mesh['gx'=8,'gy'=16] {'gy'}, dimensions={0} | all-to-all | bytes 1048576 | tf_op jit(solution)/shard_map/all_to_all | solution.py:293
  108.5 0.6 shard_map.120
  109.1 0.9 reshape.57
  109.9 4.6 %all-to-all-start.5 = ((bf16[128,2,640]{2,1,0:T(2,128)(2,1)}), bf16[128,2,640]{2,1,0:T(2,128)(2,1)S(1)}, u32[]{:S(2)}, u32[]{:S(2)}) async-start(bf16[128,2,640]{2,1,0:T(2,128)(2,1)} %reshape.57), calls=%async_computation.5 | async-start | bytes 655360 | tf_op jit(solution)/shard_map/all_to_all | solution.py:293
  114.5 3.0 %shard_map.121 = (bf16[256,512]{1,0:T(8,128)(2,1)S(1)}, bf16[256,512]{1,0:T(8,128)(2,1)S(1)}, bf16[256,512]{1,0:T(8,128)(2,1)S(1)}, bf16[256,512]{1,0:T(8,128)(2,1)S(1)}) custom-call(s32[1]{0:T(128)S(6)} %xor.4.half_ref, bf16[256,1024]{1,0:T(8,128)(2,1)S(1)} %bitcast.26, bf16[1024,2048]{1,0:T(8,128)(2,1)} %wg_ref.7, bf16[1024,2048]{1,0:T(8,128)(2,1)} %wu_ref.7), custom_call_target="tpu_custom_call" | custom-call | tf_op jit(solution)/shard_map/pallas_call | solution.py:107
  117.7 0.5 collective-permute-start.16
  118.3 0.4 collective-permute-start.18
  118.8 3.0 %shard_map.119 = (bf16[256,512]{1,0:T(8,128)(2,1)S(1)}, bf16[256,512]{1,0:T(8,128)(2,1)S(1)}, bf16[256,512]{1,0:T(8,128)(2,1)S(1)}, bf16[256,512]{1,0:T(8,128)(2,1)S(1)}) custom-call(s32[1]{0:T(128)} %bitcast.1.half_ref, bf16[256,1024]{1,0:T(8,128)(2,1)S(1)} %bitcast.27, bf16[1024,2048]{1,0:T(8,128)(2,1)} %wg_ref.7, bf16[1024,2048]{1,0:T(8,128)(2,1)} %wu_ref.7), custom_call_target="tpu_custom_call" | custom-call | tf_op jit(solution)/shard_map/pallas_call | solution.py:107
  121.8 0.8 shard_map.122
  122.7 1.2 collective-permute-start.20
  123.9 3.2 %collective-permute-start.21 = (bf16[64,2176]{1,0:T(8,128)(2,1)S(1)}, bf16[64,2176]{1,0:T(8,128)(2,1)S(1)}, u32[]{:S(2)}, u32[]{:S(2)}) collective-permute-start(bf16[64,2176]{1,0:T(8,128)(2,1)S(1)} %get-tuple-element.83), channel_id=1, source_target_pairs={{0,64},{16,80},{32,96},{48,112},{64,0},{80,16},{96,32},{112,48},{1... | collective-permute-start | bytes 835592 | tf_op jit(solution)/shard_map/ppermute | solution.py:360
  127.1 1.2 collective-permute-start.22
  128.3 0.3 convert_reduce_fusion
  128.6 0.2 rsqrt_reduce_fusion
  129.0 4.1 %shard_map.123 = bf16[2,16,512]{2,1,0:T(8,128)(2,1)S(1)} custom-call(s32[2]{0:T(128)S(1)} %copy-done.4, bf16[2,16,512]{2,1,0:T(8,128)(2,1)S(1)} %fusion.q_ref, f32[2,512]{1,0:T(2,128)S(1)} %reshape.65.refs_0_, f32[2,512]{1,0:T(2,128)S(1)} %reshape.68.refs_1_, bf16[2,2048,256]{2,1,0:T(8,128)(2,1)} %refs_2_.3, bf16[2,2048,256]{2,1,0:T(8,128)(2,1)} %refs_3_.1), custom_call_target="tpu_custom_call" | custom-call | tf_op jit(solution)/shard_map/pallas_call | solution.py:38
  133.2 0.8 broadcast_in_dim.8
  134.0 7.7 %all-to-all-start.6 = ((bf16[128,2,512]{2,1,0:T(2,128)(2,1)}), bf16[128,2,512]{2,1,0:T(2,128)(2,1)S(1)}, u32[]{:S(2)}, u32[]{:S(2)}) async-start(bf16[128,2,512]{2,1,0:T(2,128)(2,1)} %bitcast.14), calls=%async_computation.6 | async-start | bytes 524288 | tf_op jit(solution)/shard_map/all_to_all | solution.py:293
  141.8 0.3 shard_map.124.refs_0_
  142.1 2.9 %collective-permute-start.25 = (bf16[64,1024]{1,0:T(8,128)(2,1)S(1)}, bf16[64,1024]{1,0:T(8,128)(2,1)S(1)}, u32[]{:S(2)}, u32[]{:S(2)}) collective-permute-start(bf16[64,1024]{1,0:T(8,128)(2,1)S(1)} %shard_map.124.refs_0_), channel_id=1, source_target_pairs={{0,96},{16,112},{32,0},{48,16},{64,32},{80,48},{96,64},{112,80},{1... | collective-permute-start | bytes 393224 | tf_op jit(solution)/shard_map/ppermute | solution.py:384
  145.0 0.3 collective-permute-start.24
  145.3 1.1 collective-permute-start.23
  146.4 6.3 %all-to-all-done.6 = bf16[128,2,512]{2,1,0:T(2,128)(2,1)S(1)} async-done(((bf16[128,2,512]{2,1,0:T(2,128)(2,1)}), bf16[128,2,512]{2,1,0:T(2,128)(2,1)S(1)}, u32[]{:S(2)}, u32[]{:S(2)}) %all-to-all-start.6) | async-done | bytes 262176 | tf_op jit(solution)/shard_map/all_to_all | solution.py:293
  152.7 0.1 reshape.61.heads_ref
  152.9 0.8 collective-permute-done.24.refs_2_
  153.7 2.2 %collective-permute-done.23.refs_1_ = bf16[64,1024]{1,0:T(8,128)(2,1)S(1)} collective-permute-done((bf16[64,1024]{1,0:T(8,128)(2,1)S(1)}, bf16[64,1024]{1,0:T(8,128)(2,1)S(1)}, u32[]{:S(2)}, u32[]{:S(2)}) %collective-permute-start.23) | collective-permute-done | bytes 131104 | tf_op jit(solution)/shard_map/ppermute | solution.py:384
  155.9 2.6 %shard_map.125 = (f32[256,1024]{1,0:T(8,128)S(1)}, bf16[2048,1024]{1,0:T(8,128)(2,1)S(1)}) custom-call(bf16[256,512]{1,0:T(8,128)(2,1)S(1)} %reshape.61.heads_ref, bf16[512,1024]{1,0:T(8,128)(2,1)} %wout_ref.3, bf16[2048,1024]{1,0:T(8,128)(2,1)} %down_ref.3), custom_call_target="tpu_custom_call" | custom-call | flops 10000000000 | tf_op jit(solution)/shard_map/pallas_call | solution.py:38
  158.6 1.9 %shard_map.126 = bf16[256,1024]{1,0:T(8,128)(2,1)S(1)} custom-call(s32[2]{0:T(128)S(1)} %pad_add_fusion.z_ref.place_ref, bf16[64,1024]{1,0:T(8,128)(2,1)S(1)} %shard_map.124.refs_0_, bf16[64,1024]{1,0:T(8,128)(2,1)S(1)} %collective-permute-done.23.refs_1_, bf16[64,1024]{1,0:T(8,128)(2,1)S(1)} %collective-permute-done.24.refs_2_, ...), custom_call_target="tpu_custom_call" | custom-call | tf_op jit(solution)/shard_map/pallas_call | solution.py:38
  160.5 17.4 %all_to_all.42.delta_ref = bf16[16,16,1024]{2,1,0:T(8,128)(2,1)S(1)} all-to-all(bf16[16,16,1024]{2,1,0:T(8,128)(2,1)S(1)} %bitcast.28), channel_id=1, replica_groups=mesh['gx'=8,'gy'=16] {'gy'}, dimensions={0} | all-to-all | bytes 1048576 | tf_op jit(solution)/shard_map/all_to_all | solution.py:293
  177.9 0.7 shard_map.127
  (62 shorter events, 1.4 us)
Async XLA Ops:
  1.7 18.6 %all-to-all-start = ((bf16[16,16,1024]{2,1,0:T(8,128)(2,1)}), bf16[16,16,1024]{2,1,0:T(8,128)(2,1)S(1)}, u32[]{:S(2)}, u32[]{:S(2)}) async-start(bf16[16,16,1024]{2,1,0:T(8,128)(2,1)} %shard_map.109), calls=%async_computation | async-start | bytes 1048576 | tf_op jit(solution)/shard_map/all_to_all | solution.py:293
  20.3 1.2 copy-start
  23.0 21.4 %all-to-all-start.1 = ((bf16[128,2,640]{2,1,0:T(2,128)(2,1)}), bf16[128,2,640]{2,1,0:T(2,128)(2,1)S(1)}, u32[]{:S(2)}, u32[]{:S(2)}) async-start(bf16[128,2,640]{2,1,0:T(2,128)(2,1)} %reshape.50), calls=%async_computation.1 | async-start | bytes 655360 | tf_op jit(solution)/shard_map/all_to_all | solution.py:293
  33.6 4.3 %collective-permute-start = (bf16[256,512]{1,0:T(8,128)(2,1)S(1)}, bf16[256,512]{1,0:T(8,128)(2,1)S(1)}, u32[]{:S(2)}, u32[]{:S(2)}) collective-permute-start(bf16[256,512]{1,0:T(8,128)(2,1)S(1)} %get-tuple-element.54), channel_id=1, source_target_pairs={{0,16},{16,0},{32,48},{48,32},{64,80},{80,64},{96,112},{112,96},{1... | collective-permute-start | bytes 786440 | tf_op jit(solution)/shard_map/ppermute | solution.py:349
  33.7 4.2 %collective-permute-start.1 = (bf16[256,512]{1,0:T(8,128)(2,1)S(1)}, bf16[256,512]{1,0:T(8,128)(2,1)S(1)}, u32[]{:S(2)}, u32[]{:S(2)}) collective-permute-start(bf16[256,512]{1,0:T(8,128)(2,1)S(1)} %get-tuple-element.55), channel_id=1, source_target_pairs={{0,16},{16,0},{32,48},{48,32},{64,80},{80,64},{96,112},{112,96},{1... | collective-permute-start | bytes 786440 | tf_op jit(solution)/shard_map/ppermute | solution.py:349
  34.2 3.8 %collective-permute-start.2 = (bf16[256,512]{1,0:T(8,128)(2,1)S(1)}, bf16[256,512]{1,0:T(8,128)(2,1)S(1)}, u32[]{:S(2)}, u32[]{:S(2)}) collective-permute-start(bf16[256,512]{1,0:T(8,128)(2,1)S(1)} %get-tuple-element.56), channel_id=1, source_target_pairs={{0,16},{16,0},{32,48},{48,32},{64,80},{80,64},{96,112},{112,96},{1... | collective-permute-start | bytes 786440 | tf_op jit(solution)/shard_map/ppermute | solution.py:349
  34.3 3.7 %collective-permute-start.3 = (bf16[256,512]{1,0:T(8,128)(2,1)S(1)}, bf16[256,512]{1,0:T(8,128)(2,1)S(1)}, u32[]{:S(2)}, u32[]{:S(2)}) collective-permute-start(bf16[256,512]{1,0:T(8,128)(2,1)S(1)} %get-tuple-element.57), channel_id=1, source_target_pairs={{0,16},{16,0},{32,48},{48,32},{64,80},{80,64},{96,112},{112,96},{1... | collective-permute-start | bytes 786440 | tf_op jit(solution)/shard_map/ppermute | solution.py:349
  34.7 3.2 %collective-permute-start.4 = (bf16[256,128]{1,0:T(8,128)(2,1)S(1)}, bf16[256,128]{1,0:T(8,128)(2,1)S(1)}, u32[]{:S(2)}, u32[]{:S(2)}) collective-permute-start(bf16[256,128]{1,0:T(8,128)(2,1)S(1)} %get-tuple-element.53.refs_4_), channel_id=1, source_target_pairs={{0,16},{16,0},{32,48},{48,32},{64,80},{80,64},{96,112},{112,96},{1... | collective-permute-start | bytes 196616 | tf_op jit(solution)/shard_map/ppermute | solution.py:349
  34.9 10.3 %copy-start.4 = (s32[2]{0:T(128)S(1)}, s32[2]{0:T(128)}, u32[]{:S(2)}) copy-start(s32[2]{0:T(128)} %lengths_ref.3) | copy-start | bytes 28
  38.8 19.1 %collective-permute-start.5 = (bf16[64,2176]{1,0:T(8,128)(2,1)S(1)}, bf16[64,2176]{1,0:T(8,128)(2,1)S(1)}, u32[]{:S(2)}, u32[]{:S(2)}) collective-permute-start(bf16[64,2176]{1,0:T(8,128)(2,1)S(1)} %get-tuple-element.59), channel_id=1, source_target_pairs={{0,32},{16,48},{32,64},{48,80},{64,96},{80,112},{96,0},{112,16},{1... | collective-permute-start | bytes 835592 | tf_op jit(solution)/shard_map/ppermute | solution.py:360
  40.0 17.9 %collective-permute-start.6 = (bf16[64,2176]{1,0:T(8,128)(2,1)S(1)}, bf16[64,2176]{1,0:T(8,128)(2,1)S(1)}, u32[]{:S(2)}, u32[]{:S(2)}) collective-permute-start(bf16[64,2176]{1,0:T(8,128)(2,1)S(1)} %get-tuple-element.60), channel_id=1, source_target_pairs={{0,64},{16,80},{32,96},{48,112},{64,0},{80,16},{96,32},{112,48},{1... | collective-permute-start | bytes 835592 | tf_op jit(solution)/shard_map/ppermute | solution.py:360
  43.2 14.7 %collective-permute-start.7 = (bf16[64,2176]{1,0:T(8,128)(2,1)S(1)}, bf16[64,2176]{1,0:T(8,128)(2,1)S(1)}, u32[]{:S(2)}, u32[]{:S(2)}) collective-permute-start(bf16[64,2176]{1,0:T(8,128)(2,1)S(1)} %get-tuple-element.61), channel_id=1, source_target_pairs={{0,96},{16,112},{32,0},{48,16},{64,32},{80,48},{96,64},{112,80},{1... | collective-permute-start | bytes 835592 | tf_op jit(solution)/shard_map/ppermute | solution.py:360
  50.2 18.7 %all-to-all-start.2 = ((bf16[128,2,512]{2,1,0:T(2,128)(2,1)}), bf16[128,2,512]{2,1,0:T(2,128)(2,1)S(1)}, u32[]{:S(2)}, u32[]{:S(2)}) async-start(bf16[128,2,512]{2,1,0:T(2,128)(2,1)} %bitcast.8), calls=%async_computation.2 | async-start | bytes 524288 | tf_op jit(solution)/shard_map/all_to_all | solution.py:293
  58.2 10.7 %collective-permute-start.10 = (bf16[64,1024]{1,0:T(8,128)(2,1)S(1)}, bf16[64,1024]{1,0:T(8,128)(2,1)S(1)}, u32[]{:S(2)}, u32[]{:S(2)}) collective-permute-start(bf16[64,1024]{1,0:T(8,128)(2,1)S(1)} %shard_map.115.refs_0_), channel_id=1, source_target_pairs={{0,96},{16,112},{32,0},{48,16},{64,32},{80,48},{96,64},{112,80},{1... | collective-permute-start | bytes 393224 | tf_op jit(solution)/shard_map/ppermute | solution.py:384
  61.1 8.7 %collective-permute-start.9 = (bf16[64,1024]{1,0:T(8,128)(2,1)S(1)}, bf16[64,1024]{1,0:T(8,128)(2,1)S(1)}, u32[]{:S(2)}, u32[]{:S(2)}) collective-permute-start(bf16[64,1024]{1,0:T(8,128)(2,1)S(1)} %shard_map.115.refs_0_), channel_id=1, source_target_pairs={{0,64},{16,80},{32,96},{48,112},{64,0},{80,16},{96,32},{112,48},{1... | collective-permute-start | bytes 393224 | tf_op jit(solution)/shard_map/ppermute | solution.py:384
  61.4 10.6 %collective-permute-start.8 = (bf16[64,1024]{1,0:T(8,128)(2,1)S(1)}, bf16[64,1024]{1,0:T(8,128)(2,1)S(1)}, u32[]{:S(2)}, u32[]{:S(2)}) collective-permute-start(bf16[64,1024]{1,0:T(8,128)(2,1)S(1)} %shard_map.115.refs_0_), channel_id=1, source_target_pairs={{0,32},{16,48},{32,64},{48,80},{64,96},{80,112},{96,0},{112,16},{1... | collective-permute-start | bytes 393224 | tf_op jit(solution)/shard_map/ppermute | solution.py:384
  62.6 12.1 %collective-permute-start.11 = (bf16[64,1024]{1,0:T(8,128)(2,1)S(1)}, bf16[64,1024]{1,0:T(8,128)(2,1)S(1)}, u32[]{:S(2)}, u32[]{:S(2)}) collective-permute-start(bf16[64,1024]{1,0:T(8,128)(2,1)S(1)} %shard_map.115.refs_0_), channel_id=1, source_target_pairs={{0,16},{16,0},{32,48},{48,32},{64,80},{80,64},{96,112},{112,96},{1... | collective-permute-start | bytes 393224 | tf_op jit(solution)/shard_map/ppermute | solution.py:385
  68.9 5.7 %collective-permute-start.14 = (bf16[64,1024]{1,0:T(8,128)(2,1)S(1)}, bf16[64,1024]{1,0:T(8,128)(2,1)S(1)}, u32[]{:S(2)}, u32[]{:S(2)}) collective-permute-start(bf16[64,1024]{1,0:T(8,128)(2,1)S(1)} %collective-permute-done.10.refs_3_), channel_id=1, source_target_pairs={{0,16},{16,0},{32,48},{48,32},{64,80},{80,64},{96,112},{112,96},{1... | collective-permute-start | bytes 393224 | tf_op jit(solution)/shard_map/ppermute | solution.py:385
  69.8 4.9 %collective-permute-start.13 = (bf16[64,1024]{1,0:T(8,128)(2,1)S(1)}, bf16[64,1024]{1,0:T(8,128)(2,1)S(1)}, u32[]{:S(2)}, u32[]{:S(2)}) collective-permute-start(bf16[64,1024]{1,0:T(8,128)(2,1)S(1)} %collective-permute-done.9.refs_2_), channel_id=1, source_target_pairs={{0,16},{16,0},{32,48},{48,32},{64,80},{80,64},{96,112},{112,96},{1... | collective-permute-start | bytes 393224 | tf_op jit(solution)/shard_map/ppermute | solution.py:385
  72.0 2.7 %collective-permute-start.12 = (bf16[64,1024]{1,0:T(8,128)(2,1)S(1)}, bf16[64,1024]{1,0:T(8,128)(2,1)S(1)}, u32[]{:S(2)}, u32[]{:S(2)}) collective-permute-start(bf16[64,1024]{1,0:T(8,128)(2,1)S(1)} %collective-permute-done.8.refs_1_), channel_id=1, source_target_pairs={{0,16},{16,0},{32,48},{48,32},{64,80},{80,64},{96,112},{112,96},{1... | collective-permute-start | bytes 393224 | tf_op jit(solution)/shard_map/ppermute | solution.py:385
  74.6 19.4 %copy-start.2 = (f32[16,1024]{1,0:T(8,128)S(1)}, f32[16,1024]{1,0:T(8,128)}, u32[]{:S(2)}) copy-start(f32[16,1024]{1,0:T(8,128)} %x_ref.3) | copy-start | bytes 196612
  74.7 19.4 %copy-start.3 = (f32[1024]{0:T(1024)S(1)}, f32[1024]{0:T(1024)}, u32[]{:S(2)}) copy-start(f32[1024]{0:T(1024)} %param.12) | copy-start | bytes 12292
  74.7 33.7 %copy-start.1 = (bf16[1024,512]{1,0:T(8,128)(2,1)S(1)}, bf16[1024,512]{1,0:T(8,128)(2,1)}, u32[]{:S(2)}) copy-start(bf16[1024,512]{1,0:T(8,128)(2,1)} %wq_ref.3) | copy-start | bytes 3145732
  109.9 18.4 %all-to-all-start.5 = ((bf16[128,2,640]{2,1,0:T(2,128)(2,1)}), bf16[128,2,640]{2,1,0:T(2,128)(2,1)S(1)}, u32[]{:S(2)}, u32[]{:S(2)}) async-start(bf16[128,2,640]{2,1,0:T(2,128)(2,1)} %reshape.57), calls=%async_computation.5 | async-start | bytes 655360 | tf_op jit(solution)/shard_map/all_to_all | solution.py:293
  117.6 4.2 %collective-permute-start.15 = (bf16[256,512]{1,0:T(8,128)(2,1)S(1)}, bf16[256,512]{1,0:T(8,128)(2,1)S(1)}, u32[]{:S(2)}, u32[]{:S(2)}) collective-permute-start(bf16[256,512]{1,0:T(8,128)(2,1)S(1)} %get-tuple-element.77), channel_id=1, source_target_pairs={{0,16},{16,0},{32,48},{48,32},{64,80},{80,64},{96,112},{112,96},{1... | collective-permute-start | bytes 786440 | tf_op jit(solution)/shard_map/ppermute | solution.py:349
  117.7 4.1 %collective-permute-start.16 = (bf16[256,512]{1,0:T(8,128)(2,1)S(1)}, bf16[256,512]{1,0:T(8,128)(2,1)S(1)}, u32[]{:S(2)}, u32[]{:S(2)}) collective-permute-start(bf16[256,512]{1,0:T(8,128)(2,1)S(1)} %get-tuple-element.78), channel_id=1, source_target_pairs={{0,16},{16,0},{32,48},{48,32},{64,80},{80,64},{96,112},{112,96},{1... | collective-permute-start | bytes 786440 | tf_op jit(solution)/shard_map/ppermute | solution.py:349
  118.2 3.7 %collective-permute-start.17 = (bf16[256,512]{1,0:T(8,128)(2,1)S(1)}, bf16[256,512]{1,0:T(8,128)(2,1)S(1)}, u32[]{:S(2)}, u32[]{:S(2)}) collective-permute-start(bf16[256,512]{1,0:T(8,128)(2,1)S(1)} %get-tuple-element.79), channel_id=1, source_target_pairs={{0,16},{16,0},{32,48},{48,32},{64,80},{80,64},{96,112},{112,96},{1... | collective-permute-start | bytes 786440 | tf_op jit(solution)/shard_map/ppermute | solution.py:349
  118.3 3.6 %collective-permute-start.18 = (bf16[256,512]{1,0:T(8,128)(2,1)S(1)}, bf16[256,512]{1,0:T(8,128)(2,1)S(1)}, u32[]{:S(2)}, u32[]{:S(2)}) collective-permute-start(bf16[256,512]{1,0:T(8,128)(2,1)S(1)} %get-tuple-element.80), channel_id=1, source_target_pairs={{0,16},{16,0},{32,48},{48,32},{64,80},{80,64},{96,112},{112,96},{1... | collective-permute-start | bytes 786440 | tf_op jit(solution)/shard_map/ppermute | solution.py:349
  118.7 3.1 %collective-permute-start.19 = (bf16[256,128]{1,0:T(8,128)(2,1)S(1)}, bf16[256,128]{1,0:T(8,128)(2,1)S(1)}, u32[]{:S(2)}, u32[]{:S(2)}) collective-permute-start(bf16[256,128]{1,0:T(8,128)(2,1)S(1)} %get-tuple-element.76.refs_4_), channel_id=1, source_target_pairs={{0,16},{16,0},{32,48},{48,32},{64,80},{80,64},{96,112},{112,96},{1... | collective-permute-start | bytes 196616 | tf_op jit(solution)/shard_map/ppermute | solution.py:349
  122.7 19.1 %collective-permute-start.20 = (bf16[64,2176]{1,0:T(8,128)(2,1)S(1)}, bf16[64,2176]{1,0:T(8,128)(2,1)S(1)}, u32[]{:S(2)}, u32[]{:S(2)}) collective-permute-start(bf16[64,2176]{1,0:T(8,128)(2,1)S(1)} %get-tuple-element.82), channel_id=1, source_target_pairs={{0,32},{16,48},{32,64},{48,80},{64,96},{80,112},{96,0},{112,16},{1... | collective-permute-start | bytes 835592 | tf_op jit(solution)/shard_map/ppermute | solution.py:360
  123.9 17.9 %collective-permute-start.21 = (bf16[64,2176]{1,0:T(8,128)(2,1)S(1)}, bf16[64,2176]{1,0:T(8,128)(2,1)S(1)}, u32[]{:S(2)}, u32[]{:S(2)}) collective-permute-start(bf16[64,2176]{1,0:T(8,128)(2,1)S(1)} %get-tuple-element.83), channel_id=1, source_target_pairs={{0,64},{16,80},{32,96},{48,112},{64,0},{80,16},{96,32},{112,48},{1... | collective-permute-start | bytes 835592 | tf_op jit(solution)/shard_map/ppermute | solution.py:360
  127.1 14.7 %collective-permute-start.22 = (bf16[64,2176]{1,0:T(8,128)(2,1)S(1)}, bf16[64,2176]{1,0:T(8,128)(2,1)S(1)}, u32[]{:S(2)}, u32[]{:S(2)}) collective-permute-start(bf16[64,2176]{1,0:T(8,128)(2,1)S(1)} %get-tuple-element.84), channel_id=1, source_target_pairs={{0,96},{16,112},{32,0},{48,16},{64,32},{80,48},{96,64},{112,80},{1... | collective-permute-start | bytes 835592 | tf_op jit(solution)/shard_map/ppermute | solution.py:360
  134.0 18.7 %all-to-all-start.6 = ((bf16[128,2,512]{2,1,0:T(2,128)(2,1)}), bf16[128,2,512]{2,1,0:T(2,128)(2,1)S(1)}, u32[]{:S(2)}, u32[]{:S(2)}) async-start(bf16[128,2,512]{2,1,0:T(2,128)(2,1)} %bitcast.14), calls=%async_computation.6 | async-start | bytes 524288 | tf_op jit(solution)/shard_map/all_to_all | solution.py:293
  142.1 10.7 %collective-permute-start.25 = (bf16[64,1024]{1,0:T(8,128)(2,1)S(1)}, bf16[64,1024]{1,0:T(8,128)(2,1)S(1)}, u32[]{:S(2)}, u32[]{:S(2)}) collective-permute-start(bf16[64,1024]{1,0:T(8,128)(2,1)S(1)} %shard_map.124.refs_0_), channel_id=1, source_target_pairs={{0,96},{16,112},{32,0},{48,16},{64,32},{80,48},{96,64},{112,80},{1... | collective-permute-start | bytes 393224 | tf_op jit(solution)/shard_map/ppermute | solution.py:384
  145.0 8.7 %collective-permute-start.24 = (bf16[64,1024]{1,0:T(8,128)(2,1)S(1)}, bf16[64,1024]{1,0:T(8,128)(2,1)S(1)}, u32[]{:S(2)}, u32[]{:S(2)}) collective-permute-start(bf16[64,1024]{1,0:T(8,128)(2,1)S(1)} %shard_map.124.refs_0_), channel_id=1, source_target_pairs={{0,64},{16,80},{32,96},{48,112},{64,0},{80,16},{96,32},{112,48},{1... | collective-permute-start | bytes 393224 | tf_op jit(solution)/shard_map/ppermute | solution.py:384
  145.3 10.6 %collective-permute-start.23 = (bf16[64,1024]{1,0:T(8,128)(2,1)S(1)}, bf16[64,1024]{1,0:T(8,128)(2,1)S(1)}, u32[]{:S(2)}, u32[]{:S(2)}) collective-permute-start(bf16[64,1024]{1,0:T(8,128)(2,1)S(1)} %shard_map.124.refs_0_), channel_id=1, source_target_pairs={{0,32},{16,48},{32,64},{48,80},{64,96},{80,112},{96,0},{112,16},{1... | collective-permute-start | bytes 393224 | tf_op jit(solution)/shard_map/ppermute | solution.py:384
  146.4 12.1 %collective-permute-start.26 = (bf16[64,1024]{1,0:T(8,128)(2,1)S(1)}, bf16[64,1024]{1,0:T(8,128)(2,1)S(1)}, u32[]{:S(2)}, u32[]{:S(2)}) collective-permute-start(bf16[64,1024]{1,0:T(8,128)(2,1)S(1)} %shard_map.124.refs_0_), channel_id=1, source_target_pairs={{0,16},{16,0},{32,48},{48,32},{64,80},{80,64},{96,112},{112,96},{1... | collective-permute-start | bytes 393224 | tf_op jit(solution)/shard_map/ppermute | solution.py:385
  152.8 5.7 %collective-permute-start.29 = (bf16[64,1024]{1,0:T(8,128)(2,1)S(1)}, bf16[64,1024]{1,0:T(8,128)(2,1)S(1)}, u32[]{:S(2)}, u32[]{:S(2)}) collective-permute-start(bf16[64,1024]{1,0:T(8,128)(2,1)S(1)} %collective-permute-done.25.refs_3_), channel_id=1, source_target_pairs={{0,16},{16,0},{32,48},{48,32},{64,80},{80,64},{96,112},{112,96},{1... | collective-permute-start | bytes 393224 | tf_op jit(solution)/shard_map/ppermute | solution.py:385
  153.7 4.9 %collective-permute-start.28 = (bf16[64,1024]{1,0:T(8,128)(2,1)S(1)}, bf16[64,1024]{1,0:T(8,128)(2,1)S(1)}, u32[]{:S(2)}, u32[]{:S(2)}) collective-permute-start(bf16[64,1024]{1,0:T(8,128)(2,1)S(1)} %collective-permute-done.24.refs_2_), channel_id=1, source_target_pairs={{0,16},{16,0},{32,48},{48,32},{64,80},{80,64},{96,112},{112,96},{1... | collective-permute-start | bytes 393224 | tf_op jit(solution)/shard_map/ppermute | solution.py:385
  155.9 2.7 %collective-permute-start.27 = (bf16[64,1024]{1,0:T(8,128)(2,1)S(1)}, bf16[64,1024]{1,0:T(8,128)(2,1)S(1)}, u32[]{:S(2)}, u32[]{:S(2)}) collective-permute-start(bf16[64,1024]{1,0:T(8,128)(2,1)S(1)} %collective-permute-done.23.refs_1_), channel_id=1, source_target_pairs={{0,16},{16,0},{32,48},{48,32},{64,80},{80,64},{96,112},{112,96},{1... | collective-permute-start | bytes 393224 | tf_op jit(solution)/shard_map/ppermute | solution.py:385

commit v4 on v3

--- a/solution.py
+++ b/solution.py
@@ -13,6 +13,7 @@
 STEPS = 2
 EPS = 1e-06
 LANES = 128
+FIRST = 16
 F32 = jnp.float32
 BF16 = jnp.bfloat16
 PARAMS = pltpu.CompilerParams(vmem_limit_bytes=16 * 1024 * 1024)
@@ -152,29 +153,39 @@
     out_ref[...] = (gate / (1.0 + jnp.exp(-gate)) * up).astype(BF16)
 
 
-def attend_kernel(steps, lengths_ref, q_ref, *refs):
-    news = refs[:steps]
-    keys_ref, values_ref, out_ref, keys, values, sems = refs[steps:]
-    rows = q_ref.shape[0]
+def attend_kernel(steps, kv_cols, lengths_ref, sums_ref, raw_ref, *refs):
+    news = refs[: steps - 1]
+    keys_ref, values_ref, out_ref, fresh_ref, keys, values, sems = refs[steps - 1 :]
+    rows, count = sums_ref.shape[:2]
+    q_cols = sums_ref.shape[2] - LANES
+    first = pl.ds(0, FIRST)
+    rest = pl.ds(FIRST, keys.shape[1] - FIRST)
+    spots = [(0, first), (0, rest)] + [(row, pl.ds(0, keys.shape[1])) for row in range(1, rows)]
     key_copies = start_copies(
-        [(keys_ref.at[row], keys.at[row]) for row in range(rows)], sems.at[:rows]
+        [(keys_ref.at[row, at], keys.at[row, at]) for row, at in spots], sems.at[: rows + 1]
+    )
+    key_copies[0].wait()
+    value_copies = start_copies(
+        [(values_ref.at[row], values.at[row]) for row in range(rows)], sems.at[rows + 1 :]
     )
     scale = DH**-0.5
     heads, scores, new_scores, new_values = [], [], [], []
     for row in range(rows):
-        q = q_ref[row]
+        at = q_cols + kv_cols
+        line = sums_ref[row, 0:1, :]
+        row_scale = lax.rsqrt((line[:, at : at + 1] + line[:, at + 1 : at + 2]) / D + EPS)
+        q = (sums_ref[row, :, :q_cols] * row_scale).astype(BF16)
+        fresh = (raw_ref[row : row + 1, :] * row_scale).astype(BF16).astype(F32)
+        fresh_ref[row : row + 1, :] = fresh
         heads.append(jnp.concatenate([q[:, :DH], q[:, DH:]], axis=0))
         heads32 = heads[row].astype(F32)
-        lines = [ref[row : row + 1, :] for ref in news]
+        lines = [ref[row : row + 1, :] for ref in news] + [fresh]
         new_scores.append(
             [jnp.sum(heads32 * line[:, :DH], axis=1, keepdims=True) * scale for line in lines]
         )
         new_values.append([line[:, DH:] for line in lines])
-    for copy in key_copies:
+    for copy in key_copies[1:]:
         copy.wait()
-    value_copies = start_copies(
-        [(values_ref.at[row], values.at[row]) for row in range(rows)], sems.at[rows:]
-    )
     for row in range(rows):
         old_s = lax.dot_general(
             heads[row], keys[row], (((1,), (1,)), ((), ())), preferred_element_type=F32
@@ -191,7 +202,8 @@
         total = jnp.sum(old_e, axis=1, keepdims=True)
         for e in new_e:
             total = total + e
-        weights.append(((old_e / total).astype(BF16), [(e / total).astype(BF16) for e in new_e]))
+        share = 1.0 / total
+        weights.append(((old_e * share).astype(BF16), [(e * share).astype(BF16) for e in new_e]))
     for copy in value_copies:
         copy.wait()
     for row in range(rows):
@@ -199,22 +211,26 @@
         result = dot32(old_w, values[row])
         for w, v in zip(new_w, new_values[row]):
             result = result + w.astype(F32) * v
-        count = q_ref.shape[1]
         out_ref[row] = jnp.concatenate([result[:count], result[count:]], axis=1).astype(BF16)
 
 
-def attend(lengths, query, news, keys, values):
+def attend(lengths, sums, raw, news, keys, values, kv_cols):
+    rows, blocks, cols = sums.shape
     return call(
-        functools.partial(attend_kernel, len(news)),
-        jax.ShapeDtypeStruct(query.shape, BF16),
+        functools.partial(attend_kernel, len(news) + 1, kv_cols),
+        [
+            jax.ShapeDtypeStruct((rows, blocks, cols - LANES), BF16),
+            jax.ShapeDtypeStruct(raw.shape, F32),
+        ],
         lengths,
-        query,
+        sums,
+        raw,
         *news,
         keys,
         values,
         scalars=1,
         far=2,
-        copies=2 * keys.shape[0],
+        copies=2 * rows + 1,
         buffers=[pltpu.VMEM(keys.shape, BF16), pltpu.VMEM(values.shape, BF16)],
     )
 
@@ -364,17 +380,15 @@
                 packed.reshape(gx, gy, cache_rows, q_cols + LANES).astype(F32), axis=0
             ).transpose(1, 0, 2)
             at = q_cols + kv_cols
-            scale = lax.rsqrt((mine[:, :1, at : at + 1] + mine[:, :1, at + 1 : at + 2]) / D + EPS)
-            query = (mine[:, :, :q_cols] * scale).astype(BF16)
-            keyval = (mine[:, :, q_cols:at] * scale).astype(BF16).astype(F32)
-            news.append(keyval.reshape(cache_rows, 2 * DH))
-            attended = attend(lengths, query, news, cache_keys, cache_values)
+            raw = mine[:, :, q_cols:at].reshape(cache_rows, 2 * DH)
+            attended, fresh = attend(
+                lengths, mine, raw, news, cache_keys, cache_values, kv_cols
+            )
+            news.append(fresh)
             blocks = attended.transpose(1, 0, 2)
             blocks = jnp.broadcast_to(blocks[None], (gx, gy, cache_rows, q_cols))
             blocks = blocks.reshape(gx * gy, cache_rows, q_cols)
             heads_all = exchange(blocks, ("gx", "gy")).reshape(rows, q_cols)
-            heads_part, held_down = heads_output(heads_all, w_out, w_down)
-
             arrived = lax.optimization_barrier((arrived, blocks))[0]
             hidden = call(
                 functools.partial(hidden_kernel, kv_cols),
@@ -382,7 +396,11 @@
                 *arrived,
             )
             pieces = [hidden] + [lax.ppermute(hidden, "gx", z_shift(n)) for n in range(1, gz)]
-            others = [lax.ppermute(piece, "gx", core_swap) for piece in pieces]
+            own_other = lax.ppermute(hidden, "gx", core_swap)
+            heads_all = lax.optimization_barrier((heads_all, own_other))[0]
+            heads_part, held_down = heads_output(heads_all, w_out, w_down)
+            late = lax.optimization_barrier((pieces[1:], heads_part))[0]
+            others = [own_other] + [lax.ppermute(piece, "gx", core_swap) for piece in late]
             delta = output_part(place, pieces, others, heads_part, held_down)
             delta = exchange(delta.reshape(gy, own_rows, width), "gy")
             stream_shape = jax.ShapeDtypeStruct(stream.shape, F32)

time: 179 us -> 175 us (0.978)
  waiting for transfers between devices: 28.2 us -> 25.7 us
    ppermute x6, waiting for transfers between devices: 5.94 us -> 1.04 us  [body(): lax.ppermute(hidden, 'gx', z_shift(n))]
    ppermute x8, waiting for transfers between devices: 0.02 us -> 2.69 us  [the longest x6 2.69 us: body(): lax.ppermute(piece, 'gx', core_swap)]
  transfers between devices with their start and end apart: 35 -> 35, of which waited for: 7 -> 11; matrix products, arithmetic and copies ran while one was open for 3% -> 3% of each run, Pallas kernels for 16% -> 15%
where the time goes in v4:
time: 175 us
  starting transfers between devices  58.4 us (33%)
  blocking collectives  48.4 us (28%)
  Pallas kernels  34.3 us (20%)
  waiting for transfers between devices  25.7 us (15%)
  local copies, waits for them, and re-layouts  6.16 us (4%)
    all_to_all x3, blocking collectives, exchange(): return lax.all_to_all(parts, axis, split_axis=0, concat_axis=0, tiled=False)  48.4 us
    all_to_all x5, starting transfers between devices, exchange(): return lax.all_to_all(parts, axis, split_axis=0, concat_axis=0, tiled=False)  34.7 us
    pallas_call x15, Pallas kernels, call(): pl.pallas_call(kernel, out_shape=out_shape, in_specs=[SMEM] * scalars + [...  22.2 us
    all_to_all x5, waiting for transfers between devices, exchange(): return lax.all_to_all(parts, axis, split_axis=0, concat_axis=0, tiled=False)  21.9 us
    pallas_call x4, Pallas kernels, hidden_part(): pl.pallas_call(hidden_part_kernel, out_shape=[part] * (2 * outs), grid_sp...  12.1 us
    ppermute x6, starting transfers between devices, body(): lax.ppermute(pair[n], 'gx', z_shift(n))  11.3 us
    ppermute x6, starting transfers between devices, body(): lax.ppermute(hidden, 'gx', z_shift(n))  8.85 us
  transfers between devices with their start and end apart: 35, of which 11 were waited for; matrix products, arithmetic and copies ran while one was open for 3% of the time, Pallas kernels for 15%

profile of v4, /device:TPU:0, one launch (start us, length us, event | category | flops | bytes accessed | tf_op | source)
XLA Modules:
  0.0 174.8 jit_solution(10500420568192503008)
XLA Ops:
  0.0 1.7 shard_map.109
  1.7 7.1 %all-to-all-start = ((bf16[16,16,1024]{2,1,0:T(8,128)(2,1)}), bf16[16,16,1024]{2,1,0:T(8,128)(2,1)S(1)}, u32[]{:S(2)}, u32[]{:S(2)}) async-start(bf16[16,16,1024]{2,1,0:T(8,128)(2,1)} %shard_map.109), calls=%async_computation | async-start | bytes 1048576 | tf_op jit(solution)/shard_map/all_to_all | solution.py:309
  8.9 1.0 copy.15
  9.9 0.7 broadcast_divide_fusion
  10.6 9.7 %all-to-all-done = bf16[16,16,1024]{2,1,0:T(8,128)(2,1)S(1)} async-done(((bf16[16,16,1024]{2,1,0:T(8,128)(2,1)}), bf16[16,16,1024]{2,1,0:T(8,128)(2,1)S(1)}, u32[]{:S(2)}, u32[]{:S(2)}) %all-to-all-start) | async-done | bytes 524320 | tf_op jit(solution)/shard_map/all_to_all | solution.py:309
  20.3 1.2 copy-done
  21.6 0.6 shard_map.111
  22.2 0.9 reshape.46
  23.0 7.5 %all-to-all-start.1 = ((bf16[128,2,640]{2,1,0:T(2,128)(2,1)}), bf16[128,2,640]{2,1,0:T(2,128)(2,1)S(1)}, u32[]{:S(2)}, u32[]{:S(2)}) async-start(bf16[128,2,640]{2,1,0:T(2,128)(2,1)} %reshape.46), calls=%async_computation.1 | async-start | bytes 655360 | tf_op jit(solution)/shard_map/all_to_all | solution.py:309
  30.6 3.0 %shard_map.112 = (bf16[256,512]{1,0:T(8,128)(2,1)S(1)}, bf16[256,512]{1,0:T(8,128)(2,1)S(1)}, bf16[256,512]{1,0:T(8,128)(2,1)S(1)}, bf16[256,512]{1,0:T(8,128)(2,1)S(1)}) custom-call(s32[1]{0:T(128)S(6)} %xor.4.half_ref, bf16[256,1024]{1,0:T(8,128)(2,1)S(1)} %bitcast.23, bf16[1024,2048]{1,0:T(8,128)(2,1)} %wg_ref.7, bf16[1024,2048]{1,0:T(8,128)(2,1)} %wu_ref.7), custom_call_target="tpu_custom_call" | custom-call | tf_op jit(solution)/shard_map/pallas_call | solution.py:108
  33.7 0.5 collective-permute-start.1
  34.3 0.4 collective-permute-start.3
  34.9 3.0 %shard_map.110 = (bf16[256,512]{1,0:T(8,128)(2,1)S(1)}, bf16[256,512]{1,0:T(8,128)(2,1)S(1)}, bf16[256,512]{1,0:T(8,128)(2,1)S(1)}, bf16[256,512]{1,0:T(8,128)(2,1)S(1)}) custom-call(s32[1]{0:T(128)} %bitcast.1.half_ref, bf16[256,1024]{1,0:T(8,128)(2,1)S(1)} %bitcast.24, bf16[1024,2048]{1,0:T(8,128)(2,1)} %wg_ref.7, bf16[1024,2048]{1,0:T(8,128)(2,1)} %wu_ref.7), custom_call_target="tpu_custom_call" | custom-call | tf_op jit(solution)/shard_map/pallas_call | solution.py:108
  38.0 0.8 shard_map.113
  38.8 1.2 collective-permute-start.5
  40.0 3.2 %collective-permute-start.6 = (bf16[64,2176]{1,0:T(8,128)(2,1)S(1)}, bf16[64,2176]{1,0:T(8,128)(2,1)S(1)}, u32[]{:S(2)}, u32[]{:S(2)}) collective-permute-start(bf16[64,2176]{1,0:T(8,128)(2,1)S(1)} %get-tuple-element.71), channel_id=1, source_target_pairs={{0,64},{16,80},{32,96},{48,112},{64,0},{80,16},{96,32},{112,48},{1... | collective-permute-start | bytes 835592 | tf_op jit(solution)/shard_map/ppermute | solution.py:376
  43.2 1.2 collective-permute-start.7
  44.4 0.3 convert_reduce_fusion.1
  44.8 3.6 %shard_map.114 = (bf16[2,16,512]{2,1,0:T(8,128)(2,1)S(1)}, f32[2,512]{1,0:T(2,128)S(1)}) custom-call(s32[2]{0:T(128)S(1)} %copy-done.4, f32[2,16,640]{2,1,0:T(8,128)S(1)} %bitcast.33, f32[2,512]{1,0:T(2,128)S(1)} %reshape.47.raw_ref, bf16[2,2048,256]{2,1,0:T(8,128)(2,1)} %refs_1_.3, bf16[2,2048,256]{2,1,0:T(8,128)(2,1)} %refs_2_.1), custom_call_target="tpu_custom_call" | custom-call | tf_op jit(solution)/shard_map/pallas_call | solution.py:39
  48.4 0.8 broadcast_in_dim.7
  49.3 7.7 %all-to-all-start.2 = ((bf16[128,2,512]{2,1,0:T(2,128)(2,1)}), bf16[128,2,512]{2,1,0:T(2,128)(2,1)S(1)}, u32[]{:S(2)}, u32[]{:S(2)}) async-start(bf16[128,2,512]{2,1,0:T(2,128)(2,1)} %bitcast.8), calls=%async_computation.2 | async-start | bytes 524288 | tf_op jit(solution)/shard_map/all_to_all | solution.py:309
  57.0 0.3 shard_map.115.refs_0_
  57.4 3.0 %collective-permute-start.10 = (bf16[64,1024]{1,0:T(8,128)(2,1)S(1)}, bf16[64,1024]{1,0:T(8,128)(2,1)S(1)}, u32[]{:S(2)}, u32[]{:S(2)}) collective-permute-start(bf16[64,1024]{1,0:T(8,128)(2,1)S(1)} %shard_map.115.refs_0_), channel_id=1, source_target_pairs={{0,96},{16,112},{32,0},{48,16},{64,32},{80,48},{96,64},{112,80},{1... | collective-permute-start | bytes 393224 | tf_op jit(solution)/shard_map/ppermute | solution.py:398
  60.4 0.3 collective-permute-start.9
  60.7 1.1 collective-permute-start.8
  61.8 6.1 %all-to-all-done.2 = bf16[128,2,512]{2,1,0:T(2,128)(2,1)S(1)} async-done(((bf16[128,2,512]{2,1,0:T(2,128)(2,1)}), bf16[128,2,512]{2,1,0:T(2,128)(2,1)S(1)}, u32[]{:S(2)}, u32[]{:S(2)}) %all-to-all-start.2) | async-done | bytes 262176 | tf_op jit(solution)/shard_map/all_to_all | solution.py:309
  68.1 2.6 %shard_map.116 = (f32[256,1024]{1,0:T(8,128)S(1)}, bf16[2048,1024]{1,0:T(8,128)(2,1)S(1)}) custom-call(bf16[256,512]{1,0:T(8,128)(2,1)S(1)} %reshape.49.heads_ref, bf16[512,1024]{1,0:T(8,128)(2,1)} %wout_ref.3, bf16[2048,1024]{1,0:T(8,128)(2,1)} %down_ref.3), custom_call_target="tpu_custom_call" | custom-call | flops 10000000000 | tf_op jit(solution)/shard_map/pallas_call | solution.py:39
  70.8 0.5 collective-permute-done.8.refs_1_
  71.3 0.5 collective-permute-start.13
  71.8 0.8 collective-permute-done.12.refs_5_
  72.6 0.2 collective-permute-done.13.refs_6_
  72.8 0.3 collective-permute-done.14.refs_7_
  73.1 1.9 %shard_map.117 = bf16[256,1024]{1,0:T(8,128)(2,1)S(1)} custom-call(s32[2]{0:T(128)S(1)} %pad_add_fusion.z_ref.place_ref, bf16[64,1024]{1,0:T(8,128)(2,1)S(1)} %shard_map.115.refs_0_, bf16[64,1024]{1,0:T(8,128)(2,1)S(1)} %collective-permute-done.8.refs_1_, bf16[64,1024]{1,0:T(8,128)(2,1)S(1)} %collective-permute-done.9.refs_2_, ...), custom_call_target="tpu_custom_call" | custom-call | tf_op jit(solution)/shard_map/pallas_call | solution.py:39
  75.0 17.2 %all_to_all.40.delta_ref = bf16[16,16,1024]{2,1,0:T(8,128)(2,1)S(1)} all-to-all(bf16[16,16,1024]{2,1,0:T(8,128)(2,1)S(1)} %bitcast.29), channel_id=1, replica_groups=mesh['gx'=8,'gy'=16] {'gy'}, dimensions={0} | all-to-all | bytes 1048576 | tf_op jit(solution)/shard_map/all_to_all | solution.py:309
  92.3 13.9 %all_to_all.41 = bf16[16,16,1024]{2,1,0:T(8,128)(2,1)S(1)} all-to-all(bf16[16,16,1024]{2,1,0:T(8,128)(2,1)S(1)} %get-tuple-element.87), channel_id=1, replica_groups=mesh['gx'=8,'gy'=16] {'gy'}, dimensions={0} | all-to-all | bytes 1048576 | tf_op jit(solution)/shard_map/all_to_all | solution.py:309
  106.3 0.6 shard_map.120
  106.9 0.9 reshape.52
  107.7 4.6 %all-to-all-start.5 = ((bf16[128,2,640]{2,1,0:T(2,128)(2,1)}), bf16[128,2,640]{2,1,0:T(2,128)(2,1)S(1)}, u32[]{:S(2)}, u32[]{:S(2)}) async-start(bf16[128,2,640]{2,1,0:T(2,128)(2,1)} %reshape.52), calls=%async_computation.5 | async-start | bytes 655360 | tf_op jit(solution)/shard_map/all_to_all | solution.py:309
  112.3 3.0 %shard_map.121 = (bf16[256,512]{1,0:T(8,128)(2,1)S(1)}, bf16[256,512]{1,0:T(8,128)(2,1)S(1)}, bf16[256,512]{1,0:T(8,128)(2,1)S(1)}, bf16[256,512]{1,0:T(8,128)(2,1)S(1)}) custom-call(s32[1]{0:T(128)S(6)} %xor.4.half_ref, bf16[256,1024]{1,0:T(8,128)(2,1)S(1)} %bitcast.26, bf16[1024,2048]{1,0:T(8,128)(2,1)} %wg_ref.7, bf16[1024,2048]{1,0:T(8,128)(2,1)} %wu_ref.7), custom_call_target="tpu_custom_call" | custom-call | tf_op jit(solution)/shard_map/pallas_call | solution.py:108
  115.5 0.5 collective-permute-start.16
  116.1 0.4 collective-permute-start.18
  116.6 3.0 %shard_map.119 = (bf16[256,512]{1,0:T(8,128)(2,1)S(1)}, bf16[256,512]{1,0:T(8,128)(2,1)S(1)}, bf16[256,512]{1,0:T(8,128)(2,1)S(1)}, bf16[256,512]{1,0:T(8,128)(2,1)S(1)}) custom-call(s32[1]{0:T(128)} %bitcast.1.half_ref, bf16[256,1024]{1,0:T(8,128)(2,1)S(1)} %bitcast.27, bf16[1024,2048]{1,0:T(8,128)(2,1)} %wg_ref.7, bf16[1024,2048]{1,0:T(8,128)(2,1)} %wu_ref.7), custom_call_target="tpu_custom_call" | custom-call | tf_op jit(solution)/shard_map/pallas_call | solution.py:108
  119.7 0.8 shard_map.122
  120.5 1.2 collective-permute-start.20
  121.7 3.2 %collective-permute-start.21 = (bf16[64,2176]{1,0:T(8,128)(2,1)S(1)}, bf16[64,2176]{1,0:T(8,128)(2,1)S(1)}, u32[]{:S(2)}, u32[]{:S(2)}) collective-permute-start(bf16[64,2176]{1,0:T(8,128)(2,1)S(1)} %get-tuple-element.99), channel_id=1, source_target_pairs={{0,64},{16,80},{32,96},{48,112},{64,0},{80,16},{96,32},{112,48},{1... | collective-permute-start | bytes 835592 | tf_op jit(solution)/shard_map/ppermute | solution.py:376
  124.9 1.2 collective-permute-start.22
  126.1 0.3 convert_reduce_fusion
  126.5 3.7 %shard_map.123 = (bf16[2,16,512]{2,1,0:T(8,128)(2,1)S(1)}, f32[2,512]{1,0:T(2,128)}) custom-call(s32[2]{0:T(128)S(1)} %copy-done.4, f32[2,16,640]{2,1,0:T(8,128)S(1)} %bitcast.31, f32[2,512]{1,0:T(2,128)S(1)} %reshape.53.raw_ref, f32[2,512]{1,0:T(2,128)S(1)} %get-tuple-element.103.refs_0_, bf16[2,2048,256]{2,1,0:T(8,128)(2,1)} %refs_1_.3, ...), custom_call_target="tpu_custom_call" | custom-call | tf_op jit(solution)/shard_map/pallas_call | solution.py:39
  130.2 0.8 broadcast_in_dim.8
  131.1 7.7 %all-to-all-start.6 = ((bf16[128,2,512]{2,1,0:T(2,128)(2,1)}), bf16[128,2,512]{2,1,0:T(2,128)(2,1)S(1)}, u32[]{:S(2)}, u32[]{:S(2)}) async-start(bf16[128,2,512]{2,1,0:T(2,128)(2,1)} %bitcast.14), calls=%async_computation.6 | async-start | bytes 524288 | tf_op jit(solution)/shard_map/all_to_all | solution.py:309
  138.9 0.3 shard_map.124.refs_0_
  139.2 3.0 %collective-permute-start.25 = (bf16[64,1024]{1,0:T(8,128)(2,1)S(1)}, bf16[64,1024]{1,0:T(8,128)(2,1)S(1)}, u32[]{:S(2)}, u32[]{:S(2)}) collective-permute-start(bf16[64,1024]{1,0:T(8,128)(2,1)S(1)} %shard_map.124.refs_0_), channel_id=1, source_target_pairs={{0,96},{16,112},{32,0},{48,16},{64,32},{80,48},{96,64},{112,80},{1... | collective-permute-start | bytes 393224 | tf_op jit(solution)/shard_map/ppermute | solution.py:398
  142.2 0.3 collective-permute-start.24
  142.5 1.1 collective-permute-start.23
  143.7 6.1 %all-to-all-done.6 = bf16[128,2,512]{2,1,0:T(2,128)(2,1)S(1)} async-done(((bf16[128,2,512]{2,1,0:T(2,128)(2,1)}), bf16[128,2,512]{2,1,0:T(2,128)(2,1)S(1)}, u32[]{:S(2)}, u32[]{:S(2)}) %all-to-all-start.6) | async-done | bytes 262176 | tf_op jit(solution)/shard_map/all_to_all | solution.py:309
  149.9 2.6 %shard_map.125 = (f32[256,1024]{1,0:T(8,128)S(1)}, bf16[2048,1024]{1,0:T(8,128)(2,1)S(1)}) custom-call(bf16[256,512]{1,0:T(8,128)(2,1)S(1)} %reshape.55.heads_ref, bf16[512,1024]{1,0:T(8,128)(2,1)} %wout_ref.3, bf16[2048,1024]{1,0:T(8,128)(2,1)} %down_ref.3), custom_call_target="tpu_custom_call" | custom-call | flops 10000000000 | tf_op jit(solution)/shard_map/pallas_call | solution.py:39
  152.6 0.5 collective-permute-done.23.refs_1_
  153.1 0.5 collective-permute-start.28
  153.6 0.8 collective-permute-done.27.refs_5_
  154.4 0.2 collective-permute-done.28.refs_6_
  154.6 0.3 collective-permute-done.29.refs_7_
  154.9 1.9 %shard_map.126 = bf16[256,1024]{1,0:T(8,128)(2,1)S(1)} custom-call(s32[2]{0:T(128)S(1)} %pad_add_fusion.z_ref.place_ref, bf16[64,1024]{1,0:T(8,128)(2,1)S(1)} %shard_map.124.refs_0_, bf16[64,1024]{1,0:T(8,128)(2,1)S(1)} %collective-permute-done.23.refs_1_, bf16[64,1024]{1,0:T(8,128)(2,1)S(1)} %collective-permute-done.24.refs_2_, ...), custom_call_target="tpu_custom_call" | custom-call | tf_op jit(solution)/shard_map/pallas_call | solution.py:39
  156.8 17.2 %all_to_all.42.delta_ref = bf16[16,16,1024]{2,1,0:T(8,128)(2,1)S(1)} all-to-all(bf16[16,16,1024]{2,1,0:T(8,128)(2,1)S(1)} %bitcast.28), channel_id=1, replica_groups=mesh['gx'=8,'gy'=16] {'gy'}, dimensions={0} | all-to-all | bytes 1048576 | tf_op jit(solution)/shard_map/all_to_all | solution.py:309
  174.1 0.7 shard_map.127
  (58 shorter events, 1.5 us)
Async XLA Ops:
  1.7 18.6 %all-to-all-start = ((bf16[16,16,1024]{2,1,0:T(8,128)(2,1)}), bf16[16,16,1024]{2,1,0:T(8,128)(2,1)S(1)}, u32[]{:S(2)}, u32[]{:S(2)}) async-start(bf16[16,16,1024]{2,1,0:T(8,128)(2,1)} %shard_map.109), calls=%async_computation | async-start | bytes 1048576 | tf_op jit(solution)/shard_map/all_to_all | solution.py:309
  20.3 1.2 copy-start
  23.0 21.4 %all-to-all-start.1 = ((bf16[128,2,640]{2,1,0:T(2,128)(2,1)}), bf16[128,2,640]{2,1,0:T(2,128)(2,1)S(1)}, u32[]{:S(2)}, u32[]{:S(2)}) async-start(bf16[128,2,640]{2,1,0:T(2,128)(2,1)} %reshape.46), calls=%async_computation.1 | async-start | bytes 655360 | tf_op jit(solution)/shard_map/all_to_all | solution.py:309
  33.6 4.3 %collective-permute-start = (bf16[256,512]{1,0:T(8,128)(2,1)S(1)}, bf16[256,512]{1,0:T(8,128)(2,1)S(1)}, u32[]{:S(2)}, u32[]{:S(2)}) collective-permute-start(bf16[256,512]{1,0:T(8,128)(2,1)S(1)} %get-tuple-element.65), channel_id=1, source_target_pairs={{0,16},{16,0},{32,48},{48,32},{64,80},{80,64},{96,112},{112,96},{1... | collective-permute-start | bytes 786440 | tf_op jit(solution)/shard_map/ppermute | solution.py:365
  33.7 4.2 %collective-permute-start.1 = (bf16[256,512]{1,0:T(8,128)(2,1)S(1)}, bf16[256,512]{1,0:T(8,128)(2,1)S(1)}, u32[]{:S(2)}, u32[]{:S(2)}) collective-permute-start(bf16[256,512]{1,0:T(8,128)(2,1)S(1)} %get-tuple-element.66), channel_id=1, source_target_pairs={{0,16},{16,0},{32,48},{48,32},{64,80},{80,64},{96,112},{112,96},{1... | collective-permute-start | bytes 786440 | tf_op jit(solution)/shard_map/ppermute | solution.py:365
  34.2 3.8 %collective-permute-start.2 = (bf16[256,512]{1,0:T(8,128)(2,1)S(1)}, bf16[256,512]{1,0:T(8,128)(2,1)S(1)}, u32[]{:S(2)}, u32[]{:S(2)}) collective-permute-start(bf16[256,512]{1,0:T(8,128)(2,1)S(1)} %get-tuple-element.67), channel_id=1, source_target_pairs={{0,16},{16,0},{32,48},{48,32},{64,80},{80,64},{96,112},{112,96},{1... | collective-permute-start | bytes 786440 | tf_op jit(solution)/shard_map/ppermute | solution.py:365
  34.3 3.7 %collective-permute-start.3 = (bf16[256,512]{1,0:T(8,128)(2,1)S(1)}, bf16[256,512]{1,0:T(8,128)(2,1)S(1)}, u32[]{:S(2)}, u32[]{:S(2)}) collective-permute-start(bf16[256,512]{1,0:T(8,128)(2,1)S(1)} %get-tuple-element.68), channel_id=1, source_target_pairs={{0,16},{16,0},{32,48},{48,32},{64,80},{80,64},{96,112},{112,96},{1... | collective-permute-start | bytes 786440 | tf_op jit(solution)/shard_map/ppermute | solution.py:365
  34.7 3.2 %collective-permute-start.4 = (bf16[256,128]{1,0:T(8,128)(2,1)S(1)}, bf16[256,128]{1,0:T(8,128)(2,1)S(1)}, u32[]{:S(2)}, u32[]{:S(2)}) collective-permute-start(bf16[256,128]{1,0:T(8,128)(2,1)S(1)} %get-tuple-element.64.refs_4_), channel_id=1, source_target_pairs={{0,16},{16,0},{32,48},{48,32},{64,80},{80,64},{96,112},{112,96},{1... | collective-permute-start | bytes 196616 | tf_op jit(solution)/shard_map/ppermute | solution.py:365
  34.9 9.9 %copy-start.4 = (s32[2]{0:T(128)S(1)}, s32[2]{0:T(128)}, u32[]{:S(2)}) copy-start(s32[2]{0:T(128)} %lengths_ref.3) | copy-start | bytes 28
  38.8 18.2 %collective-permute-start.5 = (bf16[64,2176]{1,0:T(8,128)(2,1)S(1)}, bf16[64,2176]{1,0:T(8,128)(2,1)S(1)}, u32[]{:S(2)}, u32[]{:S(2)}) collective-permute-start(bf16[64,2176]{1,0:T(8,128)(2,1)S(1)} %get-tuple-element.70), channel_id=1, source_target_pairs={{0,32},{16,48},{32,64},{48,80},{64,96},{80,112},{96,0},{112,16},{1... | collective-permute-start | bytes 835592 | tf_op jit(solution)/shard_map/ppermute | solution.py:376
  40.0 17.0 %collective-permute-start.6 = (bf16[64,2176]{1,0:T(8,128)(2,1)S(1)}, bf16[64,2176]{1,0:T(8,128)(2,1)S(1)}, u32[]{:S(2)}, u32[]{:S(2)}) collective-permute-start(bf16[64,2176]{1,0:T(8,128)(2,1)S(1)} %get-tuple-element.71), channel_id=1, source_target_pairs={{0,64},{16,80},{32,96},{48,112},{64,0},{80,16},{96,32},{112,48},{1... | collective-permute-start | bytes 835592 | tf_op jit(solution)/shard_map/ppermute | solution.py:376
  43.2 13.8 %collective-permute-start.7 = (bf16[64,2176]{1,0:T(8,128)(2,1)S(1)}, bf16[64,2176]{1,0:T(8,128)(2,1)S(1)}, u32[]{:S(2)}, u32[]{:S(2)}) collective-permute-start(bf16[64,2176]{1,0:T(8,128)(2,1)S(1)} %get-tuple-element.72), channel_id=1, source_target_pairs={{0,96},{16,112},{32,0},{48,16},{64,32},{80,48},{96,64},{112,80},{1... | collective-permute-start | bytes 835592 | tf_op jit(solution)/shard_map/ppermute | solution.py:376
  49.3 18.7 %all-to-all-start.2 = ((bf16[128,2,512]{2,1,0:T(2,128)(2,1)}), bf16[128,2,512]{2,1,0:T(2,128)(2,1)S(1)}, u32[]{:S(2)}, u32[]{:S(2)}) async-start(bf16[128,2,512]{2,1,0:T(2,128)(2,1)} %bitcast.8), calls=%async_computation.2 | async-start | bytes 524288 | tf_op jit(solution)/shard_map/all_to_all | solution.py:309
  57.3 10.7 %collective-permute-start.11 = (bf16[64,1024]{1,0:T(8,128)(2,1)S(1)}, bf16[64,1024]{1,0:T(8,128)(2,1)S(1)}, u32[]{:S(2)}, u32[]{:S(2)}) collective-permute-start(bf16[64,1024]{1,0:T(8,128)(2,1)S(1)} %shard_map.115.refs_0_), channel_id=1, source_target_pairs={{0,16},{16,0},{32,48},{48,32},{64,80},{80,64},{96,112},{112,96},{1... | collective-permute-start | bytes 393224 | tf_op jit(solution)/shard_map/ppermute | solution.py:399
  57.4 13.3 %collective-permute-start.10 = (bf16[64,1024]{1,0:T(8,128)(2,1)S(1)}, bf16[64,1024]{1,0:T(8,128)(2,1)S(1)}, u32[]{:S(2)}, u32[]{:S(2)}) collective-permute-start(bf16[64,1024]{1,0:T(8,128)(2,1)S(1)} %shard_map.115.refs_0_), channel_id=1, source_target_pairs={{0,96},{16,112},{32,0},{48,16},{64,32},{80,48},{96,64},{112,80},{1... | collective-permute-start | bytes 393224 | tf_op jit(solution)/shard_map/ppermute | solution.py:398
  60.4 10.3 %collective-permute-start.9 = (bf16[64,1024]{1,0:T(8,128)(2,1)S(1)}, bf16[64,1024]{1,0:T(8,128)(2,1)S(1)}, u32[]{:S(2)}, u32[]{:S(2)}) collective-permute-start(bf16[64,1024]{1,0:T(8,128)(2,1)S(1)} %shard_map.115.refs_0_), channel_id=1, source_target_pairs={{0,64},{16,80},{32,96},{48,112},{64,0},{80,16},{96,32},{112,48},{1... | collective-permute-start | bytes 393224 | tf_op jit(solution)/shard_map/ppermute | solution.py:398
  60.7 10.5 %collective-permute-start.8 = (bf16[64,1024]{1,0:T(8,128)(2,1)S(1)}, bf16[64,1024]{1,0:T(8,128)(2,1)S(1)}, u32[]{:S(2)}, u32[]{:S(2)}) collective-permute-start(bf16[64,1024]{1,0:T(8,128)(2,1)S(1)} %shard_map.115.refs_0_), channel_id=1, source_target_pairs={{0,32},{16,48},{32,64},{48,80},{64,96},{80,112},{96,0},{112,16},{1... | collective-permute-start | bytes 393224 | tf_op jit(solution)/shard_map/ppermute | solution.py:398
  70.7 21.5 %copy-start.2 = (f32[16,1024]{1,0:T(8,128)S(1)}, f32[16,1024]{1,0:T(8,128)}, u32[]{:S(2)}) copy-start(f32[16,1024]{1,0:T(8,128)} %x_ref.3) | copy-start | bytes 196612
  70.7 21.5 %copy-start.3 = (f32[1024]{0:T(1024)S(1)}, f32[1024]{0:T(1024)}, u32[]{:S(2)}) copy-start(f32[1024]{0:T(1024)} %param.12) | copy-start | bytes 12292
  71.3 1.3 collective-permute-start.12
  71.3 1.5 collective-permute-start.13
  71.8 1.3 collective-permute-start.14
  73.1 33.2 %copy-start.1 = (bf16[1024,512]{1,0:T(8,128)(2,1)S(1)}, bf16[1024,512]{1,0:T(8,128)(2,1)}, u32[]{:S(2)}) copy-start(bf16[1024,512]{1,0:T(8,128)(2,1)} %wq_ref.3) | copy-start | bytes 3145732
  107.7 18.4 %all-to-all-start.5 = ((bf16[128,2,640]{2,1,0:T(2,128)(2,1)}), bf16[128,2,640]{2,1,0:T(2,128)(2,1)S(1)}, u32[]{:S(2)}, u32[]{:S(2)}) async-start(bf16[128,2,640]{2,1,0:T(2,128)(2,1)} %reshape.52), calls=%async_computation.5 | async-start | bytes 655360 | tf_op jit(solution)/shard_map/all_to_all | solution.py:309
  115.4 4.2 %collective-permute-start.15 = (bf16[256,512]{1,0:T(8,128)(2,1)S(1)}, bf16[256,512]{1,0:T(8,128)(2,1)S(1)}, u32[]{:S(2)}, u32[]{:S(2)}) collective-permute-start(bf16[256,512]{1,0:T(8,128)(2,1)S(1)} %get-tuple-element.93), channel_id=1, source_target_pairs={{0,16},{16,0},{32,48},{48,32},{64,80},{80,64},{96,112},{112,96},{1... | collective-permute-start | bytes 786440 | tf_op jit(solution)/shard_map/ppermute | solution.py:365
  115.5 4.1 %collective-permute-start.16 = (bf16[256,512]{1,0:T(8,128)(2,1)S(1)}, bf16[256,512]{1,0:T(8,128)(2,1)S(1)}, u32[]{:S(2)}, u32[]{:S(2)}) collective-permute-start(bf16[256,512]{1,0:T(8,128)(2,1)S(1)} %get-tuple-element.94), channel_id=1, source_target_pairs={{0,16},{16,0},{32,48},{48,32},{64,80},{80,64},{96,112},{112,96},{1... | collective-permute-start | bytes 786440 | tf_op jit(solution)/shard_map/ppermute | solution.py:365
  116.0 3.7 %collective-permute-start.17 = (bf16[256,512]{1,0:T(8,128)(2,1)S(1)}, bf16[256,512]{1,0:T(8,128)(2,1)S(1)}, u32[]{:S(2)}, u32[]{:S(2)}) collective-permute-start(bf16[256,512]{1,0:T(8,128)(2,1)S(1)} %get-tuple-element.95), channel_id=1, source_target_pairs={{0,16},{16,0},{32,48},{48,32},{64,80},{80,64},{96,112},{112,96},{1... | collective-permute-start | bytes 786440 | tf_op jit(solution)/shard_map/ppermute | solution.py:365
  116.1 3.6 %collective-permute-start.18 = (bf16[256,512]{1,0:T(8,128)(2,1)S(1)}, bf16[256,512]{1,0:T(8,128)(2,1)S(1)}, u32[]{:S(2)}, u32[]{:S(2)}) collective-permute-start(bf16[256,512]{1,0:T(8,128)(2,1)S(1)} %get-tuple-element.96), channel_id=1, source_target_pairs={{0,16},{16,0},{32,48},{48,32},{64,80},{80,64},{96,112},{112,96},{1... | collective-permute-start | bytes 786440 | tf_op jit(solution)/shard_map/ppermute | solution.py:365
  116.5 3.1 %collective-permute-start.19 = (bf16[256,128]{1,0:T(8,128)(2,1)S(1)}, bf16[256,128]{1,0:T(8,128)(2,1)S(1)}, u32[]{:S(2)}, u32[]{:S(2)}) collective-permute-start(bf16[256,128]{1,0:T(8,128)(2,1)S(1)} %get-tuple-element.92.refs_4_), channel_id=1, source_target_pairs={{0,16},{16,0},{32,48},{48,32},{64,80},{80,64},{96,112},{112,96},{1... | collective-permute-start | bytes 196616 | tf_op jit(solution)/shard_map/ppermute | solution.py:365
  120.5 18.4 %collective-permute-start.20 = (bf16[64,2176]{1,0:T(8,128)(2,1)S(1)}, bf16[64,2176]{1,0:T(8,128)(2,1)S(1)}, u32[]{:S(2)}, u32[]{:S(2)}) collective-permute-start(bf16[64,2176]{1,0:T(8,128)(2,1)S(1)} %get-tuple-element.98), channel_id=1, source_target_pairs={{0,32},{16,48},{32,64},{48,80},{64,96},{80,112},{96,0},{112,16},{1... | collective-permute-start | bytes 835592 | tf_op jit(solution)/shard_map/ppermute | solution.py:376
  121.7 17.2 %collective-permute-start.21 = (bf16[64,2176]{1,0:T(8,128)(2,1)S(1)}, bf16[64,2176]{1,0:T(8,128)(2,1)S(1)}, u32[]{:S(2)}, u32[]{:S(2)}) collective-permute-start(bf16[64,2176]{1,0:T(8,128)(2,1)S(1)} %get-tuple-element.99), channel_id=1, source_target_pairs={{0,64},{16,80},{32,96},{48,112},{64,0},{80,16},{96,32},{112,48},{1... | collective-permute-start | bytes 835592 | tf_op jit(solution)/shard_map/ppermute | solution.py:376
  124.9 14.0 %collective-permute-start.22 = (bf16[64,2176]{1,0:T(8,128)(2,1)S(1)}, bf16[64,2176]{1,0:T(8,128)(2,1)S(1)}, u32[]{:S(2)}, u32[]{:S(2)}) collective-permute-start(bf16[64,2176]{1,0:T(8,128)(2,1)S(1)} %get-tuple-element.100), channel_id=1, source_target_pairs={{0,96},{16,112},{32,0},{48,16},{64,32},{80,48},{96,64},{112,80},{1... | collective-permute-start | bytes 835592 | tf_op jit(solution)/shard_map/ppermute | solution.py:376
  131.1 18.7 %all-to-all-start.6 = ((bf16[128,2,512]{2,1,0:T(2,128)(2,1)}), bf16[128,2,512]{2,1,0:T(2,128)(2,1)S(1)}, u32[]{:S(2)}, u32[]{:S(2)}) async-start(bf16[128,2,512]{2,1,0:T(2,128)(2,1)} %bitcast.14), calls=%async_computation.6 | async-start | bytes 524288 | tf_op jit(solution)/shard_map/all_to_all | solution.py:309
  139.2 10.7 %collective-permute-start.26 = (bf16[64,1024]{1,0:T(8,128)(2,1)S(1)}, bf16[64,1024]{1,0:T(8,128)(2,1)S(1)}, u32[]{:S(2)}, u32[]{:S(2)}) collective-permute-start(bf16[64,1024]{1,0:T(8,128)(2,1)S(1)} %shard_map.124.refs_0_), channel_id=1, source_target_pairs={{0,16},{16,0},{32,48},{48,32},{64,80},{80,64},{96,112},{112,96},{1... | collective-permute-start | bytes 393224 | tf_op jit(solution)/shard_map/ppermute | solution.py:399
  139.2 13.3 %collective-permute-start.25 = (bf16[64,1024]{1,0:T(8,128)(2,1)S(1)}, bf16[64,1024]{1,0:T(8,128)(2,1)S(1)}, u32[]{:S(2)}, u32[]{:S(2)}) collective-permute-start(bf16[64,1024]{1,0:T(8,128)(2,1)S(1)} %shard_map.124.refs_0_), channel_id=1, source_target_pairs={{0,96},{16,112},{32,0},{48,16},{64,32},{80,48},{96,64},{112,80},{1... | collective-permute-start | bytes 393224 | tf_op jit(solution)/shard_map/ppermute | solution.py:398
  142.2 10.3 %collective-permute-start.24 = (bf16[64,1024]{1,0:T(8,128)(2,1)S(1)}, bf16[64,1024]{1,0:T(8,128)(2,1)S(1)}, u32[]{:S(2)}, u32[]{:S(2)}) collective-permute-start(bf16[64,1024]{1,0:T(8,128)(2,1)S(1)} %shard_map.124.refs_0_), channel_id=1, source_target_pairs={{0,64},{16,80},{32,96},{48,112},{64,0},{80,16},{96,32},{112,48},{1... | collective-permute-start | bytes 393224 | tf_op jit(solution)/shard_map/ppermute | solution.py:398
  142.5 10.5 %collective-permute-start.23 = (bf16[64,1024]{1,0:T(8,128)(2,1)S(1)}, bf16[64,1024]{1,0:T(8,128)(2,1)S(1)}, u32[]{:S(2)}, u32[]{:S(2)}) collective-permute-start(bf16[64,1024]{1,0:T(8,128)(2,1)S(1)} %shard_map.124.refs_0_), channel_id=1, source_target_pairs={{0,32},{16,48},{32,64},{48,80},{64,96},{80,112},{96,0},{112,16},{1... | collective-permute-start | bytes 393224 | tf_op jit(solution)/shard_map/ppermute | solution.py:398
  153.1 1.3 collective-permute-start.27
  153.1 1.5 collective-permute-start.28
  153.6 1.3 collective-permute-start.29

commit v5 on v4

--- a/solution.py
+++ b/solution.py
@@ -72,9 +72,10 @@
             out_ref[n] = scaled
 
 
-def query_kernel(kv_cols, x_ref, inverse_ref, wkv_ref, wq_ref, out_ref, squares_ref):
+def query_kernel(x_ref, gain_ref, wkv_ref, wq_ref, out_ref, squares_ref):
     x = x_ref[...]
-    plain = x.astype(F32) * inverse_ref[...]
+    kv_cols, depth = wkv_ref.shape
+    plain = x.astype(F32) * (1.0 / gain_ref[...])
     squares = jnp.sum(plain * plain, axis=1, keepdims=True)
     high = squares.astype(BF16).astype(F32)
     low = squares - high
@@ -83,44 +84,25 @@
     squares_ref[...] = columns.astype(BF16)
     q_cols = wq_ref.shape[1]
     out_ref[:, :q_cols] = dot32(x, wq_ref[...]).astype(BF16)
-    out_ref[:, q_cols:] = (dot32(x, wkv_ref[...]) + columns).astype(BF16)
+    wkv = jnp.concatenate([wkv_ref[...], jnp.zeros((LANES - kv_cols, depth), BF16)], axis=0)
+    keyval = lax.dot_general(x, wkv, (((1,), (1,)), ((), ())), preferred_element_type=F32)
+    out_ref[:, q_cols:] = (keyval + columns).astype(BF16)
 
 
 def hidden_part_kernel(half_ref, x_ref, wg_ref, wu_ref, *outs):
-    block = wg_ref.shape[1]
-    wide = outs[0].shape[1]
-    for n in range(len(outs) // 2 * (wide // block)):
-
-        @pl.when(pl.program_id(0) == n)
-        def _():
-            at = n * block
-            for k, ref in enumerate((wg_ref, wu_ref)):
-                outs[at // wide * 2 + k][:, at % wide : at % wide + block] = dot32(
-                    x_ref[...], ref[...]
-                ).astype(BF16)
-
-
-def hidden_part(half_index, x, w_gate, w_up, outs=2, blocks=2):
-    rows, width = x.shape
-    half = w_gate.shape[1] // 2
-    weight = pl.BlockSpec((width, half // blocks), lambda n, h: (0, h[0] * blocks + n))
-    part = jax.ShapeDtypeStruct((rows, half // outs), BF16)
-    return pl.pallas_call(
-        hidden_part_kernel,
-        out_shape=[part] * (2 * outs),
-        grid_spec=pltpu.PrefetchScalarGridSpec(
-            num_scalar_prefetch=1,
-            grid=(blocks,),
-            in_specs=[pl.BlockSpec(x.shape, lambda n, h: (0, 0)), weight, weight],
-            out_specs=[pl.BlockSpec(part.shape, lambda n, h: (0, 0))] * (2 * outs),
-        ),
-        compiler_params=PARAMS,
-        cost_estimate=COST,
-    )(
-        half_index,
-        x,
-        pltpu.with_memory_space_constraint(w_gate, pltpu.HBM),
-        pltpu.with_memory_space_constraint(w_up, pltpu.HBM),
+    half = wg_ref.shape[1] // 2
+    block = outs[0].shape[1]
+    start = half_ref[0] * half
+    for n in range(len(outs) // 2):
+        here = pl.ds(pl.multiple_of(start + n * block, block), block)
+        outs[2 * n][...] = dot32(x_ref[...], wg_ref[:, here]).astype(BF16)
+        outs[2 * n + 1][...] = dot32(x_ref[...], wu_ref[:, here]).astype(BF16)
+
+
+def hidden_part(half_index, x, w_gate, w_up, blocks=2):
+    part = jax.ShapeDtypeStruct((x.shape[0], w_gate.shape[1] // 2 // blocks), BF16)
+    return call(
+        hidden_part_kernel, [part] * (2 * blocks), half_index, x, w_gate, w_up, scalars=1
     )
 
 
@@ -267,34 +249,32 @@
     )
 
 
-def output_kernel(gz, block, place_ref, *refs):
-    pieces, others = refs[:gz], refs[gz : 2 * gz]
-    heads_ref, down_ref, out_ref, hidden = refs[2 * gz :]
+def output_kernel(gz, block, core_flip, place_ref, *refs):
+    pieces = refs[:gz]
+    part_ref, down_ref, out_ref, hidden = refs[gz:]
     size, half = pieces[0].shape
-    z, c = place_ref[0], place_ref[1]
-    mine = pl.ds(pl.multiple_of(c * half, half), half)
-    theirs = pl.ds(pl.multiple_of((1 - c) * half, half), half)
+    z = place_ref[0]
+    core = 1 - place_ref[1] if core_flip else place_ref[1]
+    here = pl.ds(pl.multiple_of(core * half, half), half)
     for n in range(gz):
         at = pl.ds(pl.multiple_of(lax.rem(z + gz - n, gz) * size, size), size)
-        hidden[at, mine] = pieces[n][...]
-        hidden[at, theirs] = others[n][...]
+        hidden[at, :] = pieces[n][...]
     for at in range(0, out_ref.shape[1], block):
         out_ref[:, at : at + block] = (
-            dot32(hidden[...], down_ref[:, at : at + block]) + heads_ref[:, at : at + block]
-        ).astype(BF16)
-
-
-def output_part(place, pieces, others, heads_part, w_down):
+            dot32(hidden[...], down_ref[here, at : at + block]) + part_ref[:, at : at + block]
+        ).astype(out_ref.dtype)
+
+
+def output_part(place, pieces, part, w_down, core_flip, dtype):
     return call(
-        functools.partial(output_kernel, len(pieces), 512),
-        jax.ShapeDtypeStruct(heads_part.shape, BF16),
+        functools.partial(output_kernel, len(pieces), 512, core_flip),
+        jax.ShapeDtypeStruct(part.shape, dtype),
         place,
         *pieces,
-        *others,
-        heads_part,
+        part,
         w_down,
         scalars=1,
-        buffers=[pltpu.VMEM((heads_part.shape[0], w_down.shape[0]), BF16)],
+        buffers=[pltpu.VMEM((part.shape[0], w_down.shape[0] // 2), BF16)],
     )
 
 
@@ -321,7 +301,6 @@
         cache_values,
         lengths,
     ):
-        stream = residual
         own_rows, width = residual.shape
         rows = own_rows * gy
         half = w_gate.shape[1] // 2
@@ -331,9 +310,10 @@
         me = lax.axis_index("gx")
         z, core = me // 2, lax.rem(me, 2)
         place = jnp.stack([z, core]).astype(jnp.int32)
+        stream, place, mine_half, other_half = lax.optimization_barrier(
+            (residual, place, place[1:], place[1:] ^ 1)
+        )
         gain = norm_gain[None, :]
-        inverse_gain = 1.0 / gain
-        keyval_padded = jnp.pad(w_keyval, ((0, 0), (0, LANES - kv_cols)))
         news = []
         spread = call(
             spread_kernel,
@@ -343,27 +323,28 @@
             far=2,
             copies=2,
             buffers=[pltpu.VMEM(stream.shape, F32), pltpu.VMEM(gain.shape, F32)],
+            cost=LATE,
         )
         for step in range(STEPS):
             gathered = exchange(spread, "gy").reshape(rows, width)
             packed, squares = call(
-                functools.partial(query_kernel, kv_cols),
+                query_kernel,
                 (
                     jax.ShapeDtypeStruct((rows, q_cols + LANES), BF16),
                     jax.ShapeDtypeStruct((rows, LANES), BF16),
                 ),
                 gathered,
-                inverse_gain,
-                keyval_padded,
+                gain,
+                w_keyval.T,
                 w_query,
             )
+            give = hidden_part(other_half, gathered, w_gate, w_up)
+            other = [lax.ppermute(part, "gx", core_swap) for part in (*give, squares)]
+            keep = hidden_part(mine_half, gathered, w_gate, w_up)
+            packed = lax.optimization_barrier((packed, give, keep))[0]
             packed = exchange(
                 packed.reshape(gx * gy, cache_rows, q_cols + LANES), ("gx", "gy")
             )
-
-            give = hidden_part(place[1:] ^ 1, gathered, w_gate, w_up)
-            other = [lax.ppermute(part, "gx", core_swap) for part in (*give, squares)]
-            keep = hidden_part(place[1:], gathered, w_gate, w_up)
             pair = call(
                 functools.partial(pair_kernel, gz),
                 [jax.ShapeDtypeStruct((rows // gz, 2 * half + LANES), BF16)] * gz,
@@ -401,7 +382,8 @@
             heads_part, held_down = heads_output(heads_all, w_out, w_down)
             late = lax.optimization_barrier((pieces[1:], heads_part))[0]
             others = [own_other] + [lax.ppermute(piece, "gx", core_swap) for piece in late]
-            delta = output_part(place, pieces, others, heads_part, held_down)
+            part = output_part(place, pieces, heads_part, held_down, False, F32)
+            delta = output_part(place, others, part, held_down, True, BF16)
             delta = exchange(delta.reshape(gy, own_rows, width), "gy")
             stream_shape = jax.ShapeDtypeStruct(stream.shape, F32)
             spread_shape = jax.ShapeDtypeStruct((gy, own_rows, width), BF16)

time: 175 us -> 171 us (0.977)
  blocking collectives: 48.4 us -> 65.9 us
  waiting for transfers between devices: 25.7 us -> 17.7 us
  starting transfers between devices: 58.4 us -> 50.7 us
  Pallas kernels: 34.3 us -> 28 us
    all_to_all x3 -> x4, blocking collectives: 48.4 us -> 65.9 us  [exchange(): return lax.all_to_all(parts, axis, split_axis=0, concat_axis=0, tiled=False)]
    pallas_call x4 -> x0, Pallas kernels: 12.1 us -> none  [hidden_part(): pl.pallas_call(hidden_part_kernel, out_shape=[part] * (2 * outs), grid_sp...]
    all_to_all x5 -> x4, starting transfers between devices: 34.7 us -> 25.1 us  [exchange(): return lax.all_to_all(parts, axis, split_axis=0, concat_axis=0, tiled=False)]
    all_to_all x5 -> x4, waiting for transfers between devices: 21.9 us -> 14.3 us  [exchange(): return lax.all_to_all(parts, axis, split_axis=0, concat_axis=0, tiled=False)]
    pallas_call x15 -> x21, Pallas kernels: 22.2 us -> 28 us  [call(): pl.pallas_call(kernel, out_shape=out_shape, in_specs=[SMEM] * scalars + [...]
    ppermute x10, waiting for transfers between devices: 0.03 us -> 3.3 us  [body(): other = [lax.ppermute(part, 'gx', core_swap) for part in (*give, squares)]]
    ppermute x6, waiting for transfers between devices: 2.69 us -> 0.02 us  [body(): lax.ppermute(piece, 'gx', core_swap)]
  transfers between devices with their start and end apart: 35 -> 34, of which waited for: 11 -> 6; matrix products, arithmetic and copies ran while one was open for 3% -> 3% of each run, Pallas kernels for 15% -> 10%
where the time goes in v5:
time: 171 us
  blocking collectives  65.9 us (39%)
  starting transfers between devices  50.7 us (30%)
  Pallas kernels  28 us (16%)
  waiting for transfers between devices  17.7 us (10%)
  local copies, waits for them, and re-layouts  6.29 us (4%)
    all_to_all x4, blocking collectives, exchange(): return lax.all_to_all(parts, axis, split_axis=0, concat_axis=0, tiled=False)  65.9 us
    pallas_call x21, Pallas kernels, call(): pl.pallas_call(kernel, out_shape=out_shape, in_specs=[SMEM] * scalars + [...  28 us
    all_to_all x4, starting transfers between devices, exchange(): return lax.all_to_all(parts, axis, split_axis=0, concat_axis=0, tiled=False)  25.1 us
    all_to_all x4, waiting for transfers between devices, exchange(): return lax.all_to_all(parts, axis, split_axis=0, concat_axis=0, tiled=False)  14.3 us
    ppermute x6, starting transfers between devices, body(): lax.ppermute(pair[n], 'gx', z_shift(n))  11 us
    ppermute x6, starting transfers between devices, body(): lax.ppermute(hidden, 'gx', z_shift(n))  10.6 us
  transfers between devices with their start and end apart: 34, of which 6 were waited for; matrix products, arithmetic and copies ran while one was open for 3% of the time, Pallas kernels for 10%

profile of v5, /device:TPU:0, one launch (start us, length us, event | category | flops | bytes accessed | tf_op | source)
XLA Modules:
  0.0 170.8 jit_solution(4819771824835328778)
XLA Ops:
  0.1 1.1 shard_map.109
  1.1 18.7 %all_to_all.40 = bf16[16,16,1024]{2,1,0:T(8,128)(2,1)S(1)} all-to-all(bf16[16,16,1024]{2,1,0:T(8,128)(2,1)S(1)} %shard_map.109), channel_id=1, replica_groups=mesh['gx'=8,'gy'=16] {'gy'}, dimensions={0} | all-to-all | bytes 1048576 | tf_op jit(solution)/shard_map/all_to_all | solution.py:289
  19.8 1.3 shard_map.112
  21.1 0.7 copy-done.10
  21.8 1.3 shard_map.110
  23.1 0.6 shard_map.111
  23.7 0.9 reshape.45
  24.6 8.0 %all-to-all-start.1 = ((bf16[128,2,640]{2,1,0:T(2,128)(2,1)}), bf16[128,2,640]{2,1,0:T(2,128)(2,1)}, u32[]{:S(2)}, u32[]{:S(2)}) async-start(bf16[128,2,640]{2,1,0:T(2,128)(2,1)} %reshape.45), calls=%async_computation.1 | async-start | bytes 655360 | tf_op jit(solution)/shard_map/all_to_all | solution.py:289
  32.7 0.5 collective-permute-start.1
  33.3 0.4 collective-permute-start.3
  33.8 1.6 collective-permute-done.4.refs_9_
  35.4 0.8 shard_map.113
  36.3 1.1 collective-permute-start.5
  37.3 3.2 %collective-permute-start.6 = (bf16[64,2176]{1,0:T(8,128)(2,1)S(1)}, bf16[64,2176]{1,0:T(8,128)(2,1)S(1)}, u32[]{:S(2)}, u32[]{:S(2)}) collective-permute-start(bf16[64,2176]{1,0:T(8,128)(2,1)S(1)} %get-tuple-element.81), channel_id=1, source_target_pairs={{0,64},{16,80},{32,96},{48,112},{64,0},{80,16},{96,32},{112,48},{1... | collective-permute-start | bytes 835592 | tf_op jit(solution)/shard_map/ppermute | solution.py:357
  40.6 1.2 collective-permute-start.7
  41.8 2.0 %all-to-all-done.1 = bf16[128,2,640]{2,1,0:T(2,128)(2,1)} async-done(((bf16[128,2,640]{2,1,0:T(2,128)(2,1)}), bf16[128,2,640]{2,1,0:T(2,128)(2,1)}, u32[]{:S(2)}, u32[]{:S(2)}) %all-to-all-start.1) | async-done | bytes 327712 | tf_op jit(solution)/shard_map/all_to_all | solution.py:289
  43.8 1.3 convert_reduce_fusion.1
  45.2 3.6 %shard_map.114 = (bf16[2,16,512]{2,1,0:T(8,128)(2,1)S(1)}, f32[2,512]{1,0:T(2,128)S(1)}) custom-call(s32[2]{0:T(128)S(1)} %copy-done.8, f32[2,16,640]{2,1,0:T(8,128)S(1)} %bitcast.33, f32[2,512]{1,0:T(2,128)S(1)} %reshape.46.raw_ref, bf16[2,2048,256]{2,1,0:T(8,128)(2,1)} %refs_1_.3, bf16[2,2048,256]{2,1,0:T(8,128)(2,1)} %refs_2_.1), custom_call_target="tpu_custom_call" | custom-call | tf_op jit(solution)/shard_map/pallas_call | solution.py:39
  48.8 0.9 broadcast_in_dim.7
  49.7 6.2 %all-to-all-start.2 = ((bf16[128,2,512]{2,1,0:T(2,128)(2,1)}), bf16[128,2,512]{2,1,0:T(2,128)(2,1)}, u32[]{:S(2)}, u32[]{:S(2)}) async-start(bf16[128,2,512]{2,1,0:T(2,128)(2,1)} %bitcast.44), calls=%async_computation.2 | async-start | bytes 524288 | tf_op jit(solution)/shard_map/all_to_all | solution.py:289
  55.9 0.3 shard_map.115.refs_0_
  56.3 2.9 %collective-permute-start.10 = (bf16[64,1024]{1,0:T(8,128)(2,1)S(1)}, bf16[64,1024]{1,0:T(8,128)(2,1)S(1)}, u32[]{:S(2)}, u32[]{:S(2)}) collective-permute-start(bf16[64,1024]{1,0:T(8,128)(2,1)S(1)} %shard_map.115.refs_0_), channel_id=1, source_target_pairs={{0,64},{16,80},{32,96},{48,112},{64,0},{80,16},{96,32},{112,48},{1... | collective-permute-start | bytes 393224 | tf_op jit(solution)/shard_map/ppermute | solution.py:379
  59.3 0.9 collective-permute-start.11
  60.2 1.1 collective-permute-start.9
  61.3 5.1 %all-to-all-done.2 = bf16[128,2,512]{2,1,0:T(2,128)(2,1)} async-done(((bf16[128,2,512]{2,1,0:T(2,128)(2,1)}), bf16[128,2,512]{2,1,0:T(2,128)(2,1)}, u32[]{:S(2)}, u32[]{:S(2)}) %all-to-all-start.2) | async-done | bytes 262176 | tf_op jit(solution)/shard_map/all_to_all | solution.py:289
  66.4 1.1 reshape.48.heads_ref
  67.4 2.6 %shard_map.116 = (f32[256,1024]{1,0:T(8,128)S(1)}, bf16[2048,1024]{1,0:T(8,128)(2,1)S(1)}) custom-call(bf16[256,512]{1,0:T(8,128)(2,1)S(1)} %reshape.48.heads_ref, bf16[512,1024]{1,0:T(8,128)(2,1)} %wout_ref.3, bf16[2048,1024]{1,0:T(8,128)(2,1)} %down_ref.3), custom_call_target="tpu_custom_call" | custom-call | flops 10000000000 | tf_op jit(solution)/shard_map/pallas_call | solution.py:39
  70.2 0.5 collective-permute-start.13
  70.7 0.1 collective-permute-start.14
  70.8 1.3 shard_map.117.refs_4_
  72.2 1.3 shard_map.118
  73.5 16.1 %all_to_all.41.delta_ref = bf16[16,16,1024]{2,1,0:T(8,128)(2,1)S(1)} all-to-all(bf16[16,16,1024]{2,1,0:T(8,128)(2,1)S(1)} %bitcast.29), channel_id=1, replica_groups=mesh['gx'=8,'gy'=16] {'gy'}, dimensions={0} | all-to-all | bytes 1048576 | tf_op jit(solution)/shard_map/all_to_all | solution.py:289
  89.5 0.1 shard_map.119
  89.7 14.3 %all_to_all.42 = bf16[16,16,1024]{2,1,0:T(8,128)(2,1)S(1)} all-to-all(bf16[16,16,1024]{2,1,0:T(8,128)(2,1)S(1)} %get-tuple-element.98), channel_id=1, replica_groups=mesh['gx'=8,'gy'=16] {'gy'}, dimensions={0} | all-to-all | bytes 1048576 | tf_op jit(solution)/shard_map/all_to_all | solution.py:289
  104.0 1.3 shard_map.122
  105.3 0.7 copy-done.9
  106.0 1.3 shard_map.120
  107.2 0.6 shard_map.121
  107.8 0.9 reshape.51
  108.7 5.5 %all-to-all-start.5 = ((bf16[128,2,640]{2,1,0:T(2,128)(2,1)}), bf16[128,2,640]{2,1,0:T(2,128)(2,1)S(1)}, u32[]{:S(2)}, u32[]{:S(2)}) async-start(bf16[128,2,640]{2,1,0:T(2,128)(2,1)} %reshape.51), calls=%async_computation.5 | async-start | bytes 655360 | tf_op jit(solution)/shard_map/all_to_all | solution.py:289
  114.3 0.5 collective-permute-start.16
  114.9 0.4 collective-permute-start.18
  115.4 1.6 collective-permute-done.19.refs_9_
  117.1 0.8 shard_map.123
  117.9 1.1 collective-permute-start.20
  119.1 3.2 %collective-permute-start.21 = (bf16[64,2176]{1,0:T(8,128)(2,1)S(1)}, bf16[64,2176]{1,0:T(8,128)(2,1)S(1)}, u32[]{:S(2)}, u32[]{:S(2)}) collective-permute-start(bf16[64,2176]{1,0:T(8,128)(2,1)S(1)} %get-tuple-element.110), channel_id=1, source_target_pairs={{0,64},{16,80},{32,96},{48,112},{64,0},{80,16},{96,32},{112,48},{1... | collective-permute-start | bytes 835592 | tf_op jit(solution)/shard_map/ppermute | solution.py:357
  122.3 1.2 collective-permute-start.22
  123.5 2.3 %all-to-all-done.5 = bf16[128,2,640]{2,1,0:T(2,128)(2,1)S(1)} async-done(((bf16[128,2,640]{2,1,0:T(2,128)(2,1)}), bf16[128,2,640]{2,1,0:T(2,128)(2,1)S(1)}, u32[]{:S(2)}, u32[]{:S(2)}) %all-to-all-start.5) | async-done | bytes 327712 | tf_op jit(solution)/shard_map/all_to_all | solution.py:289
  125.8 0.3 convert_reduce_fusion
  126.2 3.7 %shard_map.124 = (bf16[2,16,512]{2,1,0:T(8,128)(2,1)S(1)}, f32[2,512]{1,0:T(2,128)}) custom-call(s32[2]{0:T(128)S(1)} %copy-done.8, f32[2,16,640]{2,1,0:T(8,128)S(1)} %bitcast.31, f32[2,512]{1,0:T(2,128)S(1)} %reshape.52.raw_ref, f32[2,512]{1,0:T(2,128)S(1)} %get-tuple-element.115.refs_0_, bf16[2,2048,256]{2,1,0:T(8,128)(2,1)} %refs_1_.3, ...), custom_call_target="tpu_custom_call" | custom-call | tf_op jit(solution)/shard_map/pallas_call | solution.py:39
  129.9 0.8 broadcast_in_dim.8
  130.8 5.4 %all-to-all-start.6 = ((bf16[128,2,512]{2,1,0:T(2,128)(2,1)}), bf16[128,2,512]{2,1,0:T(2,128)(2,1)S(1)}, u32[]{:S(2)}, u32[]{:S(2)}) async-start(bf16[128,2,512]{2,1,0:T(2,128)(2,1)} %bitcast.14), calls=%async_computation.6 | async-start | bytes 524288 | tf_op jit(solution)/shard_map/all_to_all | solution.py:289
  136.2 0.3 shard_map.125.refs_0_
  136.6 1.2 collective-permute-start.24
  137.8 3.2 %collective-permute-start.25 = (bf16[64,1024]{1,0:T(8,128)(2,1)S(1)}, bf16[64,1024]{1,0:T(8,128)(2,1)S(1)}, u32[]{:S(2)}, u32[]{:S(2)}) collective-permute-start(bf16[64,1024]{1,0:T(8,128)(2,1)S(1)} %shard_map.125.refs_0_), channel_id=1, source_target_pairs={{0,64},{16,80},{32,96},{48,112},{64,0},{80,16},{96,32},{112,48},{1... | collective-permute-start | bytes 393224 | tf_op jit(solution)/shard_map/ppermute | solution.py:379
  141.1 1.2 collective-permute-start.26
  142.3 4.8 %all-to-all-done.6 = bf16[128,2,512]{2,1,0:T(2,128)(2,1)S(1)} async-done(((bf16[128,2,512]{2,1,0:T(2,128)(2,1)}), bf16[128,2,512]{2,1,0:T(2,128)(2,1)S(1)}, u32[]{:S(2)}, u32[]{:S(2)}) %all-to-all-start.6) | async-done | bytes 262176 | tf_op jit(solution)/shard_map/all_to_all | solution.py:289
  147.1 0.1 reshape.54.heads_ref
  147.2 2.6 %shard_map.126 = (f32[256,1024]{1,0:T(8,128)S(1)}, bf16[2048,1024]{1,0:T(8,128)(2,1)S(1)}) custom-call(bf16[256,512]{1,0:T(8,128)(2,1)S(1)} %reshape.54.heads_ref, bf16[512,1024]{1,0:T(8,128)(2,1)} %wout_ref.3, bf16[2048,1024]{1,0:T(8,128)(2,1)} %down_ref.3), custom_call_target="tpu_custom_call" | custom-call | flops 10000000000 | tf_op jit(solution)/shard_map/pallas_call | solution.py:39
  150.0 0.5 collective-permute-start.28
  150.6 1.3 shard_map.127.refs_4_
  151.9 1.3 shard_map.128
  153.2 16.9 %all_to_all.43.delta_ref = bf16[16,16,1024]{2,1,0:T(8,128)(2,1)S(1)} all-to-all(bf16[16,16,1024]{2,1,0:T(8,128)(2,1)S(1)} %bitcast.28), channel_id=1, replica_groups=mesh['gx'=8,'gy'=16] {'gy'}, dimensions={0} | all-to-all | bytes 1048576 | tf_op jit(solution)/shard_map/all_to_all | solution.py:289
  170.0 0.7 shard_map.129
  (68 shorter events, 1.4 us)
Async XLA Ops:
  0.1 19.7 %copy-start = (bf16[1024,2048]{1,0:T(8,128)(2,1)S(1)}, bf16[1024,2048]{1,0:T(8,128)(2,1)}, u32[]{:S(2)}) copy-start(bf16[1024,2048]{1,0:T(8,128)(2,1)} %wg_ref.7) | copy-start | bytes 12582916
  0.1 19.7 %copy-start.2 = (bf16[1024,2048]{1,0:T(8,128)(2,1)S(1)}, bf16[1024,2048]{1,0:T(8,128)(2,1)}, u32[]{:S(2)}) copy-start(bf16[1024,2048]{1,0:T(8,128)(2,1)} %wu_ref.7) | copy-start | bytes 12582916
  21.1 0.7 copy-start.10
  21.8 1.3 copy-start.4
  21.8 1.3 copy-start.5
  21.8 1.3 copy-start.6
  23.1 22.1 %copy-start.8 = (s32[2]{0:T(128)S(1)}, s32[2]{0:T(128)}, u32[]{:S(2)}) copy-start(s32[2]{0:T(128)} %lengths_ref.3) | copy-start | bytes 28
  24.6 19.2 %all-to-all-start.1 = ((bf16[128,2,640]{2,1,0:T(2,128)(2,1)}), bf16[128,2,640]{2,1,0:T(2,128)(2,1)}, u32[]{:S(2)}, u32[]{:S(2)}) async-start(bf16[128,2,640]{2,1,0:T(2,128)(2,1)} %reshape.45), calls=%async_computation.1 | async-start | bytes 655360 | tf_op jit(solution)/shard_map/all_to_all | solution.py:289
  32.6 2.8 %collective-permute-start = (bf16[256,512]{1,0:T(8,128)(2,1)}, bf16[256,512]{1,0:T(8,128)(2,1)S(1)}, u32[]{:S(2)}, u32[]{:S(2)}) collective-permute-start(bf16[256,512]{1,0:T(8,128)(2,1)} %copy-done.10), channel_id=1, source_target_pairs={{0,16},{16,0},{32,48},{48,32},{64,80},{80,64},{96,112},{112,96},{1... | collective-permute-start | bytes 786440 | tf_op jit(solution)/shard_map/ppermute | solution.py:342
  32.7 2.7 %collective-permute-start.1 = (bf16[256,512]{1,0:T(8,128)(2,1)S(1)}, bf16[256,512]{1,0:T(8,128)(2,1)S(1)}, u32[]{:S(2)}, u32[]{:S(2)}) collective-permute-start(bf16[256,512]{1,0:T(8,128)(2,1)S(1)} %get-tuple-element.76), channel_id=1, source_target_pairs={{0,16},{16,0},{32,48},{48,32},{64,80},{80,64},{96,112},{112,96},{1... | collective-permute-start | bytes 786440 | tf_op jit(solution)/shard_map/ppermute | solution.py:342
  33.2 2.3 %collective-permute-start.2 = (bf16[256,512]{1,0:T(8,128)(2,1)S(1)}, bf16[256,512]{1,0:T(8,128)(2,1)S(1)}, u32[]{:S(2)}, u32[]{:S(2)}) collective-permute-start(bf16[256,512]{1,0:T(8,128)(2,1)S(1)} %get-tuple-element.77), channel_id=1, source_target_pairs={{0,16},{16,0},{32,48},{48,32},{64,80},{80,64},{96,112},{112,96},{1... | collective-permute-start | bytes 786440 | tf_op jit(solution)/shard_map/ppermute | solution.py:342
  33.3 2.2 %collective-permute-start.3 = (bf16[256,512]{1,0:T(8,128)(2,1)S(1)}, bf16[256,512]{1,0:T(8,128)(2,1)S(1)}, u32[]{:S(2)}, u32[]{:S(2)}) collective-permute-start(bf16[256,512]{1,0:T(8,128)(2,1)S(1)} %get-tuple-element.78), channel_id=1, source_target_pairs={{0,16},{16,0},{32,48},{48,32},{64,80},{80,64},{96,112},{112,96},{1... | collective-permute-start | bytes 786440 | tf_op jit(solution)/shard_map/ppermute | solution.py:342
  33.7 1.7 %collective-permute-start.4 = (bf16[256,128]{1,0:T(8,128)(2,1)S(1)}, bf16[256,128]{1,0:T(8,128)(2,1)S(1)}, u32[]{:S(2)}, u32[]{:S(2)}) collective-permute-start(bf16[256,128]{1,0:T(8,128)(2,1)S(1)} %get-tuple-element.73.refs_4_), channel_id=1, source_target_pairs={{0,16},{16,0},{32,48},{48,32},{64,80},{80,64},{96,112},{112,96},{1... | collective-permute-start | bytes 196616 | tf_op jit(solution)/shard_map/ppermute | solution.py:342
  36.3 19.6 %collective-permute-start.5 = (bf16[64,2176]{1,0:T(8,128)(2,1)S(1)}, bf16[64,2176]{1,0:T(8,128)(2,1)S(1)}, u32[]{:S(2)}, u32[]{:S(2)}) collective-permute-start(bf16[64,2176]{1,0:T(8,128)(2,1)S(1)} %get-tuple-element.80), channel_id=1, source_target_pairs={{0,32},{16,48},{32,64},{48,80},{64,96},{80,112},{96,0},{112,16},{1... | collective-permute-start | bytes 835592 | tf_op jit(solution)/shard_map/ppermute | solution.py:357
  37.3 18.6 %collective-permute-start.6 = (bf16[64,2176]{1,0:T(8,128)(2,1)S(1)}, bf16[64,2176]{1,0:T(8,128)(2,1)S(1)}, u32[]{:S(2)}, u32[]{:S(2)}) collective-permute-start(bf16[64,2176]{1,0:T(8,128)(2,1)S(1)} %get-tuple-element.81), channel_id=1, source_target_pairs={{0,64},{16,80},{32,96},{48,112},{64,0},{80,16},{96,32},{112,48},{1... | collective-permute-start | bytes 835592 | tf_op jit(solution)/shard_map/ppermute | solution.py:357
  40.6 15.4 %collective-permute-start.7 = (bf16[64,2176]{1,0:T(8,128)(2,1)S(1)}, bf16[64,2176]{1,0:T(8,128)(2,1)S(1)}, u32[]{:S(2)}, u32[]{:S(2)}) collective-permute-start(bf16[64,2176]{1,0:T(8,128)(2,1)S(1)} %get-tuple-element.82), channel_id=1, source_target_pairs={{0,96},{16,112},{32,0},{48,16},{64,32},{80,48},{96,64},{112,80},{1... | collective-permute-start | bytes 835592 | tf_op jit(solution)/shard_map/ppermute | solution.py:357
  49.7 16.7 %all-to-all-start.2 = ((bf16[128,2,512]{2,1,0:T(2,128)(2,1)}), bf16[128,2,512]{2,1,0:T(2,128)(2,1)}, u32[]{:S(2)}, u32[]{:S(2)}) async-start(bf16[128,2,512]{2,1,0:T(2,128)(2,1)} %bitcast.44), calls=%async_computation.2 | async-start | bytes 524288 | tf_op jit(solution)/shard_map/all_to_all | solution.py:289
  56.2 11.2 %collective-permute-start.8 = (bf16[64,1024]{1,0:T(8,128)(2,1)S(1)}, bf16[64,1024]{1,0:T(8,128)(2,1)S(1)}, u32[]{:S(2)}, u32[]{:S(2)}) collective-permute-start(bf16[64,1024]{1,0:T(8,128)(2,1)S(1)} %shard_map.115.refs_0_), channel_id=1, source_target_pairs={{0,16},{16,0},{32,48},{48,32},{64,80},{80,64},{96,112},{112,96},{1... | collective-permute-start | bytes 393224 | tf_op jit(solution)/shard_map/ppermute | solution.py:380
  56.3 13.8 %collective-permute-start.10 = (bf16[64,1024]{1,0:T(8,128)(2,1)S(1)}, bf16[64,1024]{1,0:T(8,128)(2,1)S(1)}, u32[]{:S(2)}, u32[]{:S(2)}) collective-permute-start(bf16[64,1024]{1,0:T(8,128)(2,1)S(1)} %shard_map.115.refs_0_), channel_id=1, source_target_pairs={{0,64},{16,80},{32,96},{48,112},{64,0},{80,16},{96,32},{112,48},{1... | collective-permute-start | bytes 393224 | tf_op jit(solution)/shard_map/ppermute | solution.py:379
  59.3 10.8 %collective-permute-start.11 = (bf16[64,1024]{1,0:T(8,128)(2,1)S(1)}, bf16[64,1024]{1,0:T(8,128)(2,1)S(1)}, u32[]{:S(2)}, u32[]{:S(2)}) collective-permute-start(bf16[64,1024]{1,0:T(8,128)(2,1)S(1)} %shard_map.115.refs_0_), channel_id=1, source_target_pairs={{0,96},{16,112},{32,0},{48,16},{64,32},{80,48},{96,64},{112,80},{1... | collective-permute-start | bytes 393224 | tf_op jit(solution)/shard_map/ppermute | solution.py:379
  60.2 9.9 %collective-permute-start.9 = (bf16[64,1024]{1,0:T(8,128)(2,1)S(1)}, bf16[64,1024]{1,0:T(8,128)(2,1)S(1)}, u32[]{:S(2)}, u32[]{:S(2)}) collective-permute-start(bf16[64,1024]{1,0:T(8,128)(2,1)S(1)} %shard_map.115.refs_0_), channel_id=1, source_target_pairs={{0,32},{16,48},{32,64},{48,80},{64,96},{80,112},{96,0},{112,16},{1... | collective-permute-start | bytes 393224 | tf_op jit(solution)/shard_map/ppermute | solution.py:379
  70.1 2.0 %collective-permute-start.12 = (bf16[64,1024]{1,0:T(8,128)(2,1)S(1)}, bf16[64,1024]{1,0:T(8,128)(2,1)S(1)}, u32[]{:S(2)}, u32[]{:S(2)}) collective-permute-start(bf16[64,1024]{1,0:T(8,128)(2,1)S(1)} %collective-permute-done.9.refs_1_), channel_id=1, source_target_pairs={{0,16},{16,0},{32,48},{48,32},{64,80},{80,64},{96,112},{112,96},{1... | collective-permute-start | bytes 393224 | tf_op jit(solution)/shard_map/ppermute | solution.py:384
  70.2 1.9 %collective-permute-start.13 = (bf16[64,1024]{1,0:T(8,128)(2,1)S(1)}, bf16[64,1024]{1,0:T(8,128)(2,1)S(1)}, u32[]{:S(2)}, u32[]{:S(2)}) collective-permute-start(bf16[64,1024]{1,0:T(8,128)(2,1)S(1)} %collective-permute-done.10.refs_2_), channel_id=1, source_target_pairs={{0,16},{16,0},{32,48},{48,32},{64,80},{80,64},{96,112},{112,96},{1... | collective-permute-start | bytes 393224 | tf_op jit(solution)/shard_map/ppermute | solution.py:384
  70.7 1.4 collective-permute-start.14
  70.8 18.8 %copy-start.7 = (f32[16,1024]{1,0:T(8,128)S(1)}, f32[16,1024]{1,0:T(8,128)}, u32[]{:S(2)}) copy-start(f32[16,1024]{1,0:T(8,128)} %x_ref.1) | copy-start | bytes 196612
  72.1 31.9 %copy-start.1 = (bf16[1024,2048]{1,0:T(8,128)(2,1)S(1)}, bf16[1024,2048]{1,0:T(8,128)(2,1)}, u32[]{:S(2)}) copy-start(bf16[1024,2048]{1,0:T(8,128)(2,1)} %wg_ref.7) | copy-start | bytes 12582916
  72.1 31.9 %copy-start.3 = (bf16[1024,2048]{1,0:T(8,128)(2,1)S(1)}, bf16[1024,2048]{1,0:T(8,128)(2,1)}, u32[]{:S(2)}) copy-start(bf16[1024,2048]{1,0:T(8,128)(2,1)} %wu_ref.7) | copy-start | bytes 12582916
  105.2 0.7 copy-start.9
  108.7 17.1 %all-to-all-start.5 = ((bf16[128,2,640]{2,1,0:T(2,128)(2,1)}), bf16[128,2,640]{2,1,0:T(2,128)(2,1)S(1)}, u32[]{:S(2)}, u32[]{:S(2)}) async-start(bf16[128,2,640]{2,1,0:T(2,128)(2,1)} %reshape.51), calls=%async_computation.5 | async-start | bytes 655360 | tf_op jit(solution)/shard_map/all_to_all | solution.py:289
  114.2 2.8 %collective-permute-start.15 = (bf16[256,512]{1,0:T(8,128)(2,1)}, bf16[256,512]{1,0:T(8,128)(2,1)S(1)}, u32[]{:S(2)}, u32[]{:S(2)}) collective-permute-start(bf16[256,512]{1,0:T(8,128)(2,1)} %copy-done.9), channel_id=1, source_target_pairs={{0,16},{16,0},{32,48},{48,32},{64,80},{80,64},{96,112},{112,96},{1... | collective-permute-start | bytes 786440 | tf_op jit(solution)/shard_map/ppermute | solution.py:342
  114.3 2.7 %collective-permute-start.16 = (bf16[256,512]{1,0:T(8,128)(2,1)S(1)}, bf16[256,512]{1,0:T(8,128)(2,1)S(1)}, u32[]{:S(2)}, u32[]{:S(2)}) collective-permute-start(bf16[256,512]{1,0:T(8,128)(2,1)S(1)} %get-tuple-element.105), channel_id=1, source_target_pairs={{0,16},{16,0},{32,48},{48,32},{64,80},{80,64},{96,112},{112,96},{1... | collective-permute-start | bytes 786440 | tf_op jit(solution)/shard_map/ppermute | solution.py:342
  114.8 2.3 %collective-permute-start.17 = (bf16[256,512]{1,0:T(8,128)(2,1)S(1)}, bf16[256,512]{1,0:T(8,128)(2,1)S(1)}, u32[]{:S(2)}, u32[]{:S(2)}) collective-permute-start(bf16[256,512]{1,0:T(8,128)(2,1)S(1)} %get-tuple-element.106), channel_id=1, source_target_pairs={{0,16},{16,0},{32,48},{48,32},{64,80},{80,64},{96,112},{112,96},{1... | collective-permute-start | bytes 786440 | tf_op jit(solution)/shard_map/ppermute | solution.py:342
  114.9 2.2 %collective-permute-start.18 = (bf16[256,512]{1,0:T(8,128)(2,1)S(1)}, bf16[256,512]{1,0:T(8,128)(2,1)S(1)}, u32[]{:S(2)}, u32[]{:S(2)}) collective-permute-start(bf16[256,512]{1,0:T(8,128)(2,1)S(1)} %get-tuple-element.107), channel_id=1, source_target_pairs={{0,16},{16,0},{32,48},{48,32},{64,80},{80,64},{96,112},{112,96},{1... | collective-permute-start | bytes 786440 | tf_op jit(solution)/shard_map/ppermute | solution.py:342
  115.3 1.7 %collective-permute-start.19 = (bf16[256,128]{1,0:T(8,128)(2,1)S(1)}, bf16[256,128]{1,0:T(8,128)(2,1)S(1)}, u32[]{:S(2)}, u32[]{:S(2)}) collective-permute-start(bf16[256,128]{1,0:T(8,128)(2,1)S(1)} %get-tuple-element.103.refs_4_), channel_id=1, source_target_pairs={{0,16},{16,0},{32,48},{48,32},{64,80},{80,64},{96,112},{112,96},{1... | collective-permute-start | bytes 196616 | tf_op jit(solution)/shard_map/ppermute | solution.py:342
  117.9 18.3 %collective-permute-start.20 = (bf16[64,2176]{1,0:T(8,128)(2,1)S(1)}, bf16[64,2176]{1,0:T(8,128)(2,1)S(1)}, u32[]{:S(2)}, u32[]{:S(2)}) collective-permute-start(bf16[64,2176]{1,0:T(8,128)(2,1)S(1)} %get-tuple-element.109), channel_id=1, source_target_pairs={{0,32},{16,48},{32,64},{48,80},{64,96},{80,112},{96,0},{112,16},{1... | collective-permute-start | bytes 835592 | tf_op jit(solution)/shard_map/ppermute | solution.py:357
  119.1 17.2 %collective-permute-start.21 = (bf16[64,2176]{1,0:T(8,128)(2,1)S(1)}, bf16[64,2176]{1,0:T(8,128)(2,1)S(1)}, u32[]{:S(2)}, u32[]{:S(2)}) collective-permute-start(bf16[64,2176]{1,0:T(8,128)(2,1)S(1)} %get-tuple-element.110), channel_id=1, source_target_pairs={{0,64},{16,80},{32,96},{48,112},{64,0},{80,16},{96,32},{112,48},{1... | collective-permute-start | bytes 835592 | tf_op jit(solution)/shard_map/ppermute | solution.py:357
  122.3 14.0 %collective-permute-start.22 = (bf16[64,2176]{1,0:T(8,128)(2,1)S(1)}, bf16[64,2176]{1,0:T(8,128)(2,1)S(1)}, u32[]{:S(2)}, u32[]{:S(2)}) collective-permute-start(bf16[64,2176]{1,0:T(8,128)(2,1)S(1)} %get-tuple-element.111), channel_id=1, source_target_pairs={{0,96},{16,112},{32,0},{48,16},{64,32},{80,48},{96,64},{112,80},{1... | collective-permute-start | bytes 835592 | tf_op jit(solution)/shard_map/ppermute | solution.py:357
  130.8 16.3 %all-to-all-start.6 = ((bf16[128,2,512]{2,1,0:T(2,128)(2,1)}), bf16[128,2,512]{2,1,0:T(2,128)(2,1)S(1)}, u32[]{:S(2)}, u32[]{:S(2)}) async-start(bf16[128,2,512]{2,1,0:T(2,128)(2,1)} %bitcast.14), calls=%async_computation.6 | async-start | bytes 524288 | tf_op jit(solution)/shard_map/all_to_all | solution.py:289
  136.5 10.7 %collective-permute-start.23 = (bf16[64,1024]{1,0:T(8,128)(2,1)S(1)}, bf16[64,1024]{1,0:T(8,128)(2,1)S(1)}, u32[]{:S(2)}, u32[]{:S(2)}) collective-permute-start(bf16[64,1024]{1,0:T(8,128)(2,1)S(1)} %shard_map.125.refs_0_), channel_id=1, source_target_pairs={{0,16},{16,0},{32,48},{48,32},{64,80},{80,64},{96,112},{112,96},{1... | collective-permute-start | bytes 393224 | tf_op jit(solution)/shard_map/ppermute | solution.py:380
  136.6 13.2 %collective-permute-start.24 = (bf16[64,1024]{1,0:T(8,128)(2,1)S(1)}, bf16[64,1024]{1,0:T(8,128)(2,1)S(1)}, u32[]{:S(2)}, u32[]{:S(2)}) collective-permute-start(bf16[64,1024]{1,0:T(8,128)(2,1)S(1)} %shard_map.125.refs_0_), channel_id=1, source_target_pairs={{0,32},{16,48},{32,64},{48,80},{64,96},{80,112},{96,0},{112,16},{1... | collective-permute-start | bytes 393224 | tf_op jit(solution)/shard_map/ppermute | solution.py:379
  137.8 12.0 %collective-permute-start.25 = (bf16[64,1024]{1,0:T(8,128)(2,1)S(1)}, bf16[64,1024]{1,0:T(8,128)(2,1)S(1)}, u32[]{:S(2)}, u32[]{:S(2)}) collective-permute-start(bf16[64,1024]{1,0:T(8,128)(2,1)S(1)} %shard_map.125.refs_0_), channel_id=1, source_target_pairs={{0,64},{16,80},{32,96},{48,112},{64,0},{80,16},{96,32},{112,48},{1... | collective-permute-start | bytes 393224 | tf_op jit(solution)/shard_map/ppermute | solution.py:379
  141.1 8.8 %collective-permute-start.26 = (bf16[64,1024]{1,0:T(8,128)(2,1)S(1)}, bf16[64,1024]{1,0:T(8,128)(2,1)S(1)}, u32[]{:S(2)}, u32[]{:S(2)}) collective-permute-start(bf16[64,1024]{1,0:T(8,128)(2,1)S(1)} %shard_map.125.refs_0_), channel_id=1, source_target_pairs={{0,96},{16,112},{32,0},{48,16},{64,32},{80,48},{96,64},{112,80},{1... | collective-permute-start | bytes 393224 | tf_op jit(solution)/shard_map/ppermute | solution.py:379
  149.9 2.0 %collective-permute-start.27 = (bf16[64,1024]{1,0:T(8,128)(2,1)S(1)}, bf16[64,1024]{1,0:T(8,128)(2,1)S(1)}, u32[]{:S(2)}, u32[]{:S(2)}) collective-permute-start(bf16[64,1024]{1,0:T(8,128)(2,1)S(1)} %collective-permute-done.24.refs_1_), channel_id=1, source_target_pairs={{0,16},{16,0},{32,48},{48,32},{64,80},{80,64},{96,112},{112,96},{1... | collective-permute-start | bytes 393224 | tf_op jit(solution)/shard_map/ppermute | solution.py:384
  150.0 1.9 %collective-permute-start.28 = (bf16[64,1024]{1,0:T(8,128)(2,1)S(1)}, bf16[64,1024]{1,0:T(8,128)(2,1)S(1)}, u32[]{:S(2)}, u32[]{:S(2)}) collective-permute-start(bf16[64,1024]{1,0:T(8,128)(2,1)S(1)} %collective-permute-done.25.refs_2_), channel_id=1, source_target_pairs={{0,16},{16,0},{32,48},{48,32},{64,80},{80,64},{96,112},{112,96},{1... | collective-permute-start | bytes 393224 | tf_op jit(solution)/shard_map/ppermute | solution.py:384
  150.5 1.4 collective-permute-start.29

commit v6 on v5

--- a/solution.py
+++ b/solution.py
@@ -55,12 +55,14 @@
     return copies
 
 
-def spread_kernel(x_ref, gain_ref, out_ref, x, gain, sems):
-    for copy in start_copies([(x_ref, x), (gain_ref, gain)], sems):
-        copy.wait()
+def spread_kernel(x_ref, gain_ref, wq_ref, out_ref, held_ref, x, gain, sems):
+    copies = start_copies([(x_ref, x), (gain_ref, gain), (wq_ref, held_ref)], sems)
+    copies[0].wait()
+    copies[1].wait()
     scaled = (x[...] * gain[...]).astype(BF16)
     for n in range(out_ref.shape[0]):
         out_ref[n] = scaled
+    copies[2].wait()
 
 
 def add_kernel(x_ref, delta_ref, gain_ref, new_ref, out_ref=None):
@@ -315,13 +317,17 @@
         )
         gain = norm_gain[None, :]
         news = []
-        spread = call(
+        spread, held_query = call(
             spread_kernel,
-            jax.ShapeDtypeStruct((gy, own_rows, width), BF16),
+            [
+                jax.ShapeDtypeStruct((gy, own_rows, width), BF16),
+                pltpu.VMEM(w_query.shape, w_query.dtype),
+            ],
             stream,
             gain,
-            far=2,
-            copies=2,
+            w_query,
+            far=3,
+            copies=3,
             buffers=[pltpu.VMEM(stream.shape, F32), pltpu.VMEM(gain.shape, F32)],
             cost=LATE,
         )
@@ -336,7 +342,7 @@
                 gathered,
                 gain,
                 w_keyval.T,
-                w_query,
+                held_query if step == 0 else w_query,
             )
             give = hidden_part(other_half, gathered, w_gate, w_up)
             other = [lax.ppermute(part, "gx", core_swap) for part in (*give, squares)]

time: 171 us -> 168 us (0.982)
  local copies, waits for them, and re-layouts: 6.29 us -> 3.87 us
  transfers between devices with their start and end apart: 34 -> 34, of which waited for: 6 -> 6; matrix products, arithmetic and copies ran while one was open for 3% -> 2% of each run, Pallas kernels for 10% -> 10%
where the time goes in v6:
time: 168 us
  blocking collectives  66.9 us (40%)
  starting transfers between devices  49.2 us (29%)
  Pallas kernels  28.4 us (17%)
  waiting for transfers between devices  18.2 us (11%)
  local copies, waits for them, and re-layouts  3.87 us (2%)
    all_to_all x4, blocking collectives, exchange(): return lax.all_to_all(parts, axis, split_axis=0, concat_axis=0, tiled=False)  66.9 us
    pallas_call x21, Pallas kernels, call(): pl.pallas_call(kernel, out_shape=out_shape, in_specs=[SMEM] * scalars + [...  28.4 us
    all_to_all x4, starting transfers between devices, exchange(): return lax.all_to_all(parts, axis, split_axis=0, concat_axis=0, tiled=False)  23.5 us
    all_to_all x4, waiting for transfers between devices, exchange(): return lax.all_to_all(parts, axis, split_axis=0, concat_axis=0, tiled=False)  14.9 us
    ppermute x6, starting transfers between devices, body(): lax.ppermute(pair[n], 'gx', z_shift(n))  11.1 us
    ppermute x6, starting transfers between devices, body(): lax.ppermute(hidden, 'gx', z_shift(n))  10.7 us
  transfers between devices with their start and end apart: 34, of which 6 were waited for; matrix products, arithmetic and copies ran while one was open for 2% of the time, Pallas kernels for 10%

profile of v6, /device:TPU:0, one launch (start us, length us, event | category | flops | bytes accessed | tf_op | source)
XLA Modules:
  0.0 167.9 jit_solution(15748619894765182379)
XLA Ops:
  0.1 1.4 shard_map.109
  1.5 18.7 %all_to_all.40 = bf16[16,16,1024]{2,1,0:T(8,128)(2,1)S(1)} all-to-all(bf16[16,16,1024]{2,1,0:T(8,128)(2,1)S(1)} %get-tuple-element.71), channel_id=1, replica_groups=mesh['gx'=8,'gy'=16] {'gy'}, dimensions={0} | all-to-all | bytes 1048576 | tf_op jit(solution)/shard_map/all_to_all | solution.py:291
  20.2 1.3 shard_map.112
  21.5 1.3 shard_map.110
  22.8 0.6 shard_map.111
  23.4 0.9 reshape.45
  24.3 7.5 %all-to-all-start.1 = ((bf16[128,2,640]{2,1,0:T(2,128)(2,1)}), bf16[128,2,640]{2,1,0:T(2,128)(2,1)S(1)}, u32[]{:S(2)}, u32[]{:S(2)}) async-start(bf16[128,2,640]{2,1,0:T(2,128)(2,1)} %reshape.45), calls=%async_computation.1 | async-start | bytes 655360 | tf_op jit(solution)/shard_map/all_to_all | solution.py:291
  31.9 0.5 collective-permute-start.1
  32.4 0.1 collective-permute-start.2
  32.5 0.4 collective-permute-start.3
  32.9 0.1 collective-permute-start.4
  33.0 1.6 collective-permute-done.4.refs_9_
  34.6 0.8 shard_map.113
  35.5 1.1 collective-permute-start.5
  36.6 3.2 %collective-permute-start.6 = (bf16[64,2176]{1,0:T(8,128)(2,1)S(1)}, bf16[64,2176]{1,0:T(8,128)(2,1)S(1)}, u32[]{:S(2)}, u32[]{:S(2)}) collective-permute-start(bf16[64,2176]{1,0:T(8,128)(2,1)S(1)} %get-tuple-element.85), channel_id=1, source_target_pairs={{0,64},{16,80},{32,96},{48,112},{64,0},{80,16},{96,32},{112,48},{1... | collective-permute-start | bytes 835592 | tf_op jit(solution)/shard_map/ppermute | solution.py:363
  39.9 1.2 collective-permute-start.7
  41.0 2.3 %all-to-all-done.1 = bf16[128,2,640]{2,1,0:T(2,128)(2,1)S(1)} async-done(((bf16[128,2,640]{2,1,0:T(2,128)(2,1)}), bf16[128,2,640]{2,1,0:T(2,128)(2,1)S(1)}, u32[]{:S(2)}, u32[]{:S(2)}) %all-to-all-start.1) | async-done | bytes 327712 | tf_op jit(solution)/shard_map/all_to_all | solution.py:291
  43.4 0.3 convert_reduce_fusion.1
  43.8 3.6 %shard_map.114 = (bf16[2,16,512]{2,1,0:T(8,128)(2,1)S(1)}, f32[2,512]{1,0:T(2,128)S(1)}) custom-call(s32[2]{0:T(128)S(1)} %copy-done.8, f32[2,16,640]{2,1,0:T(8,128)S(1)} %bitcast.33, f32[2,512]{1,0:T(2,128)S(1)} %reshape.46.raw_ref, bf16[2,2048,256]{2,1,0:T(8,128)(2,1)} %refs_1_.3, bf16[2,2048,256]{2,1,0:T(8,128)(2,1)} %refs_2_.1), custom_call_target="tpu_custom_call" | custom-call | tf_op jit(solution)/shard_map/pallas_call | solution.py:39
  47.4 0.8 broadcast_in_dim.7
  48.2 5.4 %all-to-all-start.2 = ((bf16[128,2,512]{2,1,0:T(2,128)(2,1)}), bf16[128,2,512]{2,1,0:T(2,128)(2,1)S(1)}, u32[]{:S(2)}, u32[]{:S(2)}) async-start(bf16[128,2,512]{2,1,0:T(2,128)(2,1)} %bitcast.8), calls=%async_computation.2 | async-start | bytes 524288 | tf_op jit(solution)/shard_map/all_to_all | solution.py:291
  53.7 0.3 shard_map.115.refs_0_
  54.1 3.0 %collective-permute-start.10 = (bf16[64,1024]{1,0:T(8,128)(2,1)S(1)}, bf16[64,1024]{1,0:T(8,128)(2,1)S(1)}, u32[]{:S(2)}, u32[]{:S(2)}) collective-permute-start(bf16[64,1024]{1,0:T(8,128)(2,1)S(1)} %shard_map.115.refs_0_), channel_id=1, source_target_pairs={{0,64},{16,80},{32,96},{48,112},{64,0},{80,16},{96,32},{112,48},{1... | collective-permute-start | bytes 393224 | tf_op jit(solution)/shard_map/ppermute | solution.py:385
  57.1 0.9 collective-permute-start.11
  58.0 1.1 collective-permute-start.9
  59.1 5.4 %all-to-all-done.2 = bf16[128,2,512]{2,1,0:T(2,128)(2,1)S(1)} async-done(((bf16[128,2,512]{2,1,0:T(2,128)(2,1)}), bf16[128,2,512]{2,1,0:T(2,128)(2,1)S(1)}, u32[]{:S(2)}, u32[]{:S(2)}) %all-to-all-start.2) | async-done | bytes 262176 | tf_op jit(solution)/shard_map/all_to_all | solution.py:291
  64.5 0.1 reshape.48.heads_ref
  64.7 2.6 %shard_map.116 = (f32[256,1024]{1,0:T(8,128)S(1)}, bf16[2048,1024]{1,0:T(8,128)(2,1)S(1)}) custom-call(bf16[256,512]{1,0:T(8,128)(2,1)S(1)} %reshape.48.heads_ref, bf16[512,1024]{1,0:T(8,128)(2,1)} %wout_ref.3, bf16[2048,1024]{1,0:T(8,128)(2,1)} %down_ref.3), custom_call_target="tpu_custom_call" | custom-call | flops 10000000000 | tf_op jit(solution)/shard_map/pallas_call | solution.py:39
  67.4 0.5 collective-permute-start.13
  67.9 0.1 collective-permute-start.14
  68.0 1.3 shard_map.117.refs_4_
  69.4 1.3 shard_map.118
  70.7 17.1 %all_to_all.41.delta_ref = bf16[16,16,1024]{2,1,0:T(8,128)(2,1)S(1)} all-to-all(bf16[16,16,1024]{2,1,0:T(8,128)(2,1)S(1)} %bitcast.29), channel_id=1, replica_groups=mesh['gx'=8,'gy'=16] {'gy'}, dimensions={0} | all-to-all | bytes 1048576 | tf_op jit(solution)/shard_map/all_to_all | solution.py:291
  87.7 0.1 shard_map.119
  87.8 14.3 %all_to_all.42 = bf16[16,16,1024]{2,1,0:T(8,128)(2,1)S(1)} all-to-all(bf16[16,16,1024]{2,1,0:T(8,128)(2,1)S(1)} %get-tuple-element.102), channel_id=1, replica_groups=mesh['gx'=8,'gy'=16] {'gy'}, dimensions={0} | all-to-all | bytes 1048576 | tf_op jit(solution)/shard_map/all_to_all | solution.py:291
  102.2 1.3 shard_map.122
  103.4 1.3 shard_map.120
  104.7 0.6 shard_map.121
  105.3 0.9 reshape.51
  106.2 5.1 %all-to-all-start.5 = ((bf16[128,2,640]{2,1,0:T(2,128)(2,1)}), bf16[128,2,640]{2,1,0:T(2,128)(2,1)S(1)}, u32[]{:S(2)}, u32[]{:S(2)}) async-start(bf16[128,2,640]{2,1,0:T(2,128)(2,1)} %reshape.51), calls=%async_computation.5 | async-start | bytes 655360 | tf_op jit(solution)/shard_map/all_to_all | solution.py:291
  111.4 0.5 collective-permute-start.16
  112.0 0.4 collective-permute-start.18
  112.5 1.6 collective-permute-done.19.refs_9_
  114.2 0.8 shard_map.123
  115.0 1.1 collective-permute-start.20
  116.2 3.2 %collective-permute-start.21 = (bf16[64,2176]{1,0:T(8,128)(2,1)S(1)}, bf16[64,2176]{1,0:T(8,128)(2,1)S(1)}, u32[]{:S(2)}, u32[]{:S(2)}) collective-permute-start(bf16[64,2176]{1,0:T(8,128)(2,1)S(1)} %get-tuple-element.114), channel_id=1, source_target_pairs={{0,64},{16,80},{32,96},{48,112},{64,0},{80,16},{96,32},{112,48},{1... | collective-permute-start | bytes 835592 | tf_op jit(solution)/shard_map/ppermute | solution.py:363
  119.4 1.2 collective-permute-start.22
  120.6 2.3 %all-to-all-done.5 = bf16[128,2,640]{2,1,0:T(2,128)(2,1)S(1)} async-done(((bf16[128,2,640]{2,1,0:T(2,128)(2,1)}), bf16[128,2,640]{2,1,0:T(2,128)(2,1)S(1)}, u32[]{:S(2)}, u32[]{:S(2)}) %all-to-all-start.5) | async-done | bytes 327712 | tf_op jit(solution)/shard_map/all_to_all | solution.py:291
  122.9 0.3 convert_reduce_fusion
  123.3 3.7 %shard_map.124 = (bf16[2,16,512]{2,1,0:T(8,128)(2,1)S(1)}, f32[2,512]{1,0:T(2,128)}) custom-call(s32[2]{0:T(128)S(1)} %copy-done.8, f32[2,16,640]{2,1,0:T(8,128)S(1)} %bitcast.31, f32[2,512]{1,0:T(2,128)S(1)} %reshape.52.raw_ref, f32[2,512]{1,0:T(2,128)S(1)} %get-tuple-element.119.refs_0_, bf16[2,2048,256]{2,1,0:T(8,128)(2,1)} %refs_1_.3, ...), custom_call_target="tpu_custom_call" | custom-call | tf_op jit(solution)/shard_map/pallas_call | solution.py:39
  127.0 0.8 broadcast_in_dim.8
  127.9 5.4 %all-to-all-start.6 = ((bf16[128,2,512]{2,1,0:T(2,128)(2,1)}), bf16[128,2,512]{2,1,0:T(2,128)(2,1)S(1)}, u32[]{:S(2)}, u32[]{:S(2)}) async-start(bf16[128,2,512]{2,1,0:T(2,128)(2,1)} %bitcast.14), calls=%async_computation.6 | async-start | bytes 524288 | tf_op jit(solution)/shard_map/all_to_all | solution.py:291
  133.3 0.3 shard_map.125.refs_0_
  133.7 1.2 collective-permute-start.24
  134.9 3.2 %collective-permute-start.25 = (bf16[64,1024]{1,0:T(8,128)(2,1)S(1)}, bf16[64,1024]{1,0:T(8,128)(2,1)S(1)}, u32[]{:S(2)}, u32[]{:S(2)}) collective-permute-start(bf16[64,1024]{1,0:T(8,128)(2,1)S(1)} %shard_map.125.refs_0_), channel_id=1, source_target_pairs={{0,64},{16,80},{32,96},{48,112},{64,0},{80,16},{96,32},{112,48},{1... | collective-permute-start | bytes 393224 | tf_op jit(solution)/shard_map/ppermute | solution.py:385
  138.2 1.2 collective-permute-start.26
  139.3 4.8 %all-to-all-done.6 = bf16[128,2,512]{2,1,0:T(2,128)(2,1)S(1)} async-done(((bf16[128,2,512]{2,1,0:T(2,128)(2,1)}), bf16[128,2,512]{2,1,0:T(2,128)(2,1)S(1)}, u32[]{:S(2)}, u32[]{:S(2)}) %all-to-all-start.6) | async-done | bytes 262176 | tf_op jit(solution)/shard_map/all_to_all | solution.py:291
  144.2 0.1 reshape.54.heads_ref
  144.3 2.6 %shard_map.126 = (f32[256,1024]{1,0:T(8,128)S(1)}, bf16[2048,1024]{1,0:T(8,128)(2,1)S(1)}) custom-call(bf16[256,512]{1,0:T(8,128)(2,1)S(1)} %reshape.54.heads_ref, bf16[512,1024]{1,0:T(8,128)(2,1)} %wout_ref.3, bf16[2048,1024]{1,0:T(8,128)(2,1)} %down_ref.3), custom_call_target="tpu_custom_call" | custom-call | flops 10000000000 | tf_op jit(solution)/shard_map/pallas_call | solution.py:39
  147.1 0.5 collective-permute-start.28
  147.7 1.3 shard_map.127.refs_4_
  149.0 1.3 shard_map.128
  150.3 16.9 %all_to_all.43.delta_ref = bf16[16,16,1024]{2,1,0:T(8,128)(2,1)S(1)} all-to-all(bf16[16,16,1024]{2,1,0:T(8,128)(2,1)S(1)} %bitcast.28), channel_id=1, replica_groups=mesh['gx'=8,'gy'=16] {'gy'}, dimensions={0} | all-to-all | bytes 1048576 | tf_op jit(solution)/shard_map/all_to_all | solution.py:291
  167.1 0.7 shard_map.129
  (64 shorter events, 1.2 us)
Async XLA Ops:
  0.1 20.1 %copy-start = (bf16[1024,2048]{1,0:T(8,128)(2,1)S(1)}, bf16[1024,2048]{1,0:T(8,128)(2,1)}, u32[]{:S(2)}) copy-start(bf16[1024,2048]{1,0:T(8,128)(2,1)} %wg_ref.7) | copy-start | bytes 12582916
  0.1 20.1 %copy-start.2 = (bf16[1024,2048]{1,0:T(8,128)(2,1)S(1)}, bf16[1024,2048]{1,0:T(8,128)(2,1)}, u32[]{:S(2)}) copy-start(bf16[1024,2048]{1,0:T(8,128)(2,1)} %wu_ref.7) | copy-start | bytes 12582916
  21.5 1.3 copy-start.5
  21.5 1.3 copy-start.6
  22.8 21.0 %copy-start.8 = (s32[2]{0:T(128)S(1)}, s32[2]{0:T(128)}, u32[]{:S(2)}) copy-start(s32[2]{0:T(128)} %lengths_ref.3) | copy-start | bytes 28
  24.3 19.1 %all-to-all-start.1 = ((bf16[128,2,640]{2,1,0:T(2,128)(2,1)}), bf16[128,2,640]{2,1,0:T(2,128)(2,1)S(1)}, u32[]{:S(2)}, u32[]{:S(2)}) async-start(bf16[128,2,640]{2,1,0:T(2,128)(2,1)} %reshape.45), calls=%async_computation.1 | async-start | bytes 655360 | tf_op jit(solution)/shard_map/all_to_all | solution.py:291
  31.8 2.8 %collective-permute-start = (bf16[256,512]{1,0:T(8,128)(2,1)S(1)}, bf16[256,512]{1,0:T(8,128)(2,1)S(1)}, u32[]{:S(2)}, u32[]{:S(2)}) collective-permute-start(bf16[256,512]{1,0:T(8,128)(2,1)S(1)} %get-tuple-element.79), channel_id=1, source_target_pairs={{0,16},{16,0},{32,48},{48,32},{64,80},{80,64},{96,112},{112,96},{1... | collective-permute-start | bytes 786440 | tf_op jit(solution)/shard_map/ppermute | solution.py:348
  31.9 2.7 %collective-permute-start.1 = (bf16[256,512]{1,0:T(8,128)(2,1)S(1)}, bf16[256,512]{1,0:T(8,128)(2,1)S(1)}, u32[]{:S(2)}, u32[]{:S(2)}) collective-permute-start(bf16[256,512]{1,0:T(8,128)(2,1)S(1)} %get-tuple-element.80), channel_id=1, source_target_pairs={{0,16},{16,0},{32,48},{48,32},{64,80},{80,64},{96,112},{112,96},{1... | collective-permute-start | bytes 786440 | tf_op jit(solution)/shard_map/ppermute | solution.py:348
  32.4 2.3 %collective-permute-start.2 = (bf16[256,512]{1,0:T(8,128)(2,1)S(1)}, bf16[256,512]{1,0:T(8,128)(2,1)S(1)}, u32[]{:S(2)}, u32[]{:S(2)}) collective-permute-start(bf16[256,512]{1,0:T(8,128)(2,1)S(1)} %get-tuple-element.81), channel_id=1, source_target_pairs={{0,16},{16,0},{32,48},{48,32},{64,80},{80,64},{96,112},{112,96},{1... | collective-permute-start | bytes 786440 | tf_op jit(solution)/shard_map/ppermute | solution.py:348
  32.5 2.2 %collective-permute-start.3 = (bf16[256,512]{1,0:T(8,128)(2,1)S(1)}, bf16[256,512]{1,0:T(8,128)(2,1)S(1)}, u32[]{:S(2)}, u32[]{:S(2)}) collective-permute-start(bf16[256,512]{1,0:T(8,128)(2,1)S(1)} %get-tuple-element.82), channel_id=1, source_target_pairs={{0,16},{16,0},{32,48},{48,32},{64,80},{80,64},{96,112},{112,96},{1... | collective-permute-start | bytes 786440 | tf_op jit(solution)/shard_map/ppermute | solution.py:348
  32.9 1.7 %collective-permute-start.4 = (bf16[256,128]{1,0:T(8,128)(2,1)S(1)}, bf16[256,128]{1,0:T(8,128)(2,1)S(1)}, u32[]{:S(2)}, u32[]{:S(2)}) collective-permute-start(bf16[256,128]{1,0:T(8,128)(2,1)S(1)} %get-tuple-element.77.refs_4_), channel_id=1, source_target_pairs={{0,16},{16,0},{32,48},{48,32},{64,80},{80,64},{96,112},{112,96},{1... | collective-permute-start | bytes 196616 | tf_op jit(solution)/shard_map/ppermute | solution.py:348
  35.5 18.2 %collective-permute-start.5 = (bf16[64,2176]{1,0:T(8,128)(2,1)S(1)}, bf16[64,2176]{1,0:T(8,128)(2,1)S(1)}, u32[]{:S(2)}, u32[]{:S(2)}) collective-permute-start(bf16[64,2176]{1,0:T(8,128)(2,1)S(1)} %get-tuple-element.84), channel_id=1, source_target_pairs={{0,32},{16,48},{32,64},{48,80},{64,96},{80,112},{96,0},{112,16},{1... | collective-permute-start | bytes 835592 | tf_op jit(solution)/shard_map/ppermute | solution.py:363
  36.6 17.0 %collective-permute-start.6 = (bf16[64,2176]{1,0:T(8,128)(2,1)S(1)}, bf16[64,2176]{1,0:T(8,128)(2,1)S(1)}, u32[]{:S(2)}, u32[]{:S(2)}) collective-permute-start(bf16[64,2176]{1,0:T(8,128)(2,1)S(1)} %get-tuple-element.85), channel_id=1, source_target_pairs={{0,64},{16,80},{32,96},{48,112},{64,0},{80,16},{96,32},{112,48},{1... | collective-permute-start | bytes 835592 | tf_op jit(solution)/shard_map/ppermute | solution.py:363
  39.9 13.8 %collective-permute-start.7 = (bf16[64,2176]{1,0:T(8,128)(2,1)S(1)}, bf16[64,2176]{1,0:T(8,128)(2,1)S(1)}, u32[]{:S(2)}, u32[]{:S(2)}) collective-permute-start(bf16[64,2176]{1,0:T(8,128)(2,1)S(1)} %get-tuple-element.86), channel_id=1, source_target_pairs={{0,96},{16,112},{32,0},{48,16},{64,32},{80,48},{96,64},{112,80},{1... | collective-permute-start | bytes 835592 | tf_op jit(solution)/shard_map/ppermute | solution.py:363
  48.2 16.3 %all-to-all-start.2 = ((bf16[128,2,512]{2,1,0:T(2,128)(2,1)}), bf16[128,2,512]{2,1,0:T(2,128)(2,1)S(1)}, u32[]{:S(2)}, u32[]{:S(2)}) async-start(bf16[128,2,512]{2,1,0:T(2,128)(2,1)} %bitcast.8), calls=%async_computation.2 | async-start | bytes 524288 | tf_op jit(solution)/shard_map/all_to_all | solution.py:291
  54.0 10.7 %collective-permute-start.8 = (bf16[64,1024]{1,0:T(8,128)(2,1)S(1)}, bf16[64,1024]{1,0:T(8,128)(2,1)S(1)}, u32[]{:S(2)}, u32[]{:S(2)}) collective-permute-start(bf16[64,1024]{1,0:T(8,128)(2,1)S(1)} %shard_map.115.refs_0_), channel_id=1, source_target_pairs={{0,16},{16,0},{32,48},{48,32},{64,80},{80,64},{96,112},{112,96},{1... | collective-permute-start | bytes 393224 | tf_op jit(solution)/shard_map/ppermute | solution.py:386
  54.1 13.2 %collective-permute-start.10 = (bf16[64,1024]{1,0:T(8,128)(2,1)S(1)}, bf16[64,1024]{1,0:T(8,128)(2,1)S(1)}, u32[]{:S(2)}, u32[]{:S(2)}) collective-permute-start(bf16[64,1024]{1,0:T(8,128)(2,1)S(1)} %shard_map.115.refs_0_), channel_id=1, source_target_pairs={{0,64},{16,80},{32,96},{48,112},{64,0},{80,16},{96,32},{112,48},{1... | collective-permute-start | bytes 393224 | tf_op jit(solution)/shard_map/ppermute | solution.py:385
  57.1 10.2 %collective-permute-start.11 = (bf16[64,1024]{1,0:T(8,128)(2,1)S(1)}, bf16[64,1024]{1,0:T(8,128)(2,1)S(1)}, u32[]{:S(2)}, u32[]{:S(2)}) collective-permute-start(bf16[64,1024]{1,0:T(8,128)(2,1)S(1)} %shard_map.115.refs_0_), channel_id=1, source_target_pairs={{0,96},{16,112},{32,0},{48,16},{64,32},{80,48},{96,64},{112,80},{1... | collective-permute-start | bytes 393224 | tf_op jit(solution)/shard_map/ppermute | solution.py:385
  58.0 9.4 %collective-permute-start.9 = (bf16[64,1024]{1,0:T(8,128)(2,1)S(1)}, bf16[64,1024]{1,0:T(8,128)(2,1)S(1)}, u32[]{:S(2)}, u32[]{:S(2)}) collective-permute-start(bf16[64,1024]{1,0:T(8,128)(2,1)S(1)} %shard_map.115.refs_0_), channel_id=1, source_target_pairs={{0,32},{16,48},{32,64},{48,80},{64,96},{80,112},{96,0},{112,16},{1... | collective-permute-start | bytes 393224 | tf_op jit(solution)/shard_map/ppermute | solution.py:385
  67.3 2.0 %collective-permute-start.12 = (bf16[64,1024]{1,0:T(8,128)(2,1)S(1)}, bf16[64,1024]{1,0:T(8,128)(2,1)S(1)}, u32[]{:S(2)}, u32[]{:S(2)}) collective-permute-start(bf16[64,1024]{1,0:T(8,128)(2,1)S(1)} %collective-permute-done.9.refs_1_), channel_id=1, source_target_pairs={{0,16},{16,0},{32,48},{48,32},{64,80},{80,64},{96,112},{112,96},{1... | collective-permute-start | bytes 393224 | tf_op jit(solution)/shard_map/ppermute | solution.py:390
  67.4 1.9 %collective-permute-start.13 = (bf16[64,1024]{1,0:T(8,128)(2,1)S(1)}, bf16[64,1024]{1,0:T(8,128)(2,1)S(1)}, u32[]{:S(2)}, u32[]{:S(2)}) collective-permute-start(bf16[64,1024]{1,0:T(8,128)(2,1)S(1)} %collective-permute-done.10.refs_2_), channel_id=1, source_target_pairs={{0,16},{16,0},{32,48},{48,32},{64,80},{80,64},{96,112},{112,96},{1... | collective-permute-start | bytes 393224 | tf_op jit(solution)/shard_map/ppermute | solution.py:390
  67.9 1.4 collective-permute-start.14
  68.0 19.7 %copy-start.7 = (f32[16,1024]{1,0:T(8,128)S(1)}, f32[16,1024]{1,0:T(8,128)}, u32[]{:S(2)}) copy-start(f32[16,1024]{1,0:T(8,128)} %x_ref.1) | copy-start | bytes 196612
  69.3 32.8 %copy-start.1 = (bf16[1024,2048]{1,0:T(8,128)(2,1)S(1)}, bf16[1024,2048]{1,0:T(8,128)(2,1)}, u32[]{:S(2)}) copy-start(bf16[1024,2048]{1,0:T(8,128)(2,1)} %wg_ref.7) | copy-start | bytes 12582916
  69.3 32.8 %copy-start.3 = (bf16[1024,2048]{1,0:T(8,128)(2,1)S(1)}, bf16[1024,2048]{1,0:T(8,128)(2,1)}, u32[]{:S(2)}) copy-start(bf16[1024,2048]{1,0:T(8,128)(2,1)} %wu_ref.7) | copy-start | bytes 12582916
  103.4 1.3 copy-start.4
  106.2 16.7 %all-to-all-start.5 = ((bf16[128,2,640]{2,1,0:T(2,128)(2,1)}), bf16[128,2,640]{2,1,0:T(2,128)(2,1)S(1)}, u32[]{:S(2)}, u32[]{:S(2)}) async-start(bf16[128,2,640]{2,1,0:T(2,128)(2,1)} %reshape.51), calls=%async_computation.5 | async-start | bytes 655360 | tf_op jit(solution)/shard_map/all_to_all | solution.py:291
  111.3 2.8 %collective-permute-start.15 = (bf16[256,512]{1,0:T(8,128)(2,1)S(1)}, bf16[256,512]{1,0:T(8,128)(2,1)S(1)}, u32[]{:S(2)}, u32[]{:S(2)}) collective-permute-start(bf16[256,512]{1,0:T(8,128)(2,1)S(1)} %get-tuple-element.108), channel_id=1, source_target_pairs={{0,16},{16,0},{32,48},{48,32},{64,80},{80,64},{96,112},{112,96},{1... | collective-permute-start | bytes 786440 | tf_op jit(solution)/shard_map/ppermute | solution.py:348
  111.4 2.7 %collective-permute-start.16 = (bf16[256,512]{1,0:T(8,128)(2,1)S(1)}, bf16[256,512]{1,0:T(8,128)(2,1)S(1)}, u32[]{:S(2)}, u32[]{:S(2)}) collective-permute-start(bf16[256,512]{1,0:T(8,128)(2,1)S(1)} %get-tuple-element.109), channel_id=1, source_target_pairs={{0,16},{16,0},{32,48},{48,32},{64,80},{80,64},{96,112},{112,96},{1... | collective-permute-start | bytes 786440 | tf_op jit(solution)/shard_map/ppermute | solution.py:348
  111.9 2.3 %collective-permute-start.17 = (bf16[256,512]{1,0:T(8,128)(2,1)S(1)}, bf16[256,512]{1,0:T(8,128)(2,1)S(1)}, u32[]{:S(2)}, u32[]{:S(2)}) collective-permute-start(bf16[256,512]{1,0:T(8,128)(2,1)S(1)} %get-tuple-element.110), channel_id=1, source_target_pairs={{0,16},{16,0},{32,48},{48,32},{64,80},{80,64},{96,112},{112,96},{1... | collective-permute-start | bytes 786440 | tf_op jit(solution)/shard_map/ppermute | solution.py:348
  112.0 2.2 %collective-permute-start.18 = (bf16[256,512]{1,0:T(8,128)(2,1)S(1)}, bf16[256,512]{1,0:T(8,128)(2,1)S(1)}, u32[]{:S(2)}, u32[]{:S(2)}) collective-permute-start(bf16[256,512]{1,0:T(8,128)(2,1)S(1)} %get-tuple-element.111), channel_id=1, source_target_pairs={{0,16},{16,0},{32,48},{48,32},{64,80},{80,64},{96,112},{112,96},{1... | collective-permute-start | bytes 786440 | tf_op jit(solution)/shard_map/ppermute | solution.py:348
  112.4 1.7 %collective-permute-start.19 = (bf16[256,128]{1,0:T(8,128)(2,1)S(1)}, bf16[256,128]{1,0:T(8,128)(2,1)S(1)}, u32[]{:S(2)}, u32[]{:S(2)}) collective-permute-start(bf16[256,128]{1,0:T(8,128)(2,1)S(1)} %get-tuple-element.107.refs_4_), channel_id=1, source_target_pairs={{0,16},{16,0},{32,48},{48,32},{64,80},{80,64},{96,112},{112,96},{1... | collective-permute-start | bytes 196616 | tf_op jit(solution)/shard_map/ppermute | solution.py:348
  115.0 18.3 %collective-permute-start.20 = (bf16[64,2176]{1,0:T(8,128)(2,1)S(1)}, bf16[64,2176]{1,0:T(8,128)(2,1)S(1)}, u32[]{:S(2)}, u32[]{:S(2)}) collective-permute-start(bf16[64,2176]{1,0:T(8,128)(2,1)S(1)} %get-tuple-element.113), channel_id=1, source_target_pairs={{0,32},{16,48},{32,64},{48,80},{64,96},{80,112},{96,0},{112,16},{1... | collective-permute-start | bytes 835592 | tf_op jit(solution)/shard_map/ppermute | solution.py:363
  116.2 17.1 %collective-permute-start.21 = (bf16[64,2176]{1,0:T(8,128)(2,1)S(1)}, bf16[64,2176]{1,0:T(8,128)(2,1)S(1)}, u32[]{:S(2)}, u32[]{:S(2)}) collective-permute-start(bf16[64,2176]{1,0:T(8,128)(2,1)S(1)} %get-tuple-element.114), channel_id=1, source_target_pairs={{0,64},{16,80},{32,96},{48,112},{64,0},{80,16},{96,32},{112,48},{1... | collective-permute-start | bytes 835592 | tf_op jit(solution)/shard_map/ppermute | solution.py:363
  119.4 13.9 %collective-permute-start.22 = (bf16[64,2176]{1,0:T(8,128)(2,1)S(1)}, bf16[64,2176]{1,0:T(8,128)(2,1)S(1)}, u32[]{:S(2)}, u32[]{:S(2)}) collective-permute-start(bf16[64,2176]{1,0:T(8,128)(2,1)S(1)} %get-tuple-element.115), channel_id=1, source_target_pairs={{0,96},{16,112},{32,0},{48,16},{64,32},{80,48},{96,64},{112,80},{1... | collective-permute-start | bytes 835592 | tf_op jit(solution)/shard_map/ppermute | solution.py:363
  127.9 16.3 %all-to-all-start.6 = ((bf16[128,2,512]{2,1,0:T(2,128)(2,1)}), bf16[128,2,512]{2,1,0:T(2,128)(2,1)S(1)}, u32[]{:S(2)}, u32[]{:S(2)}) async-start(bf16[128,2,512]{2,1,0:T(2,128)(2,1)} %bitcast.14), calls=%async_computation.6 | async-start | bytes 524288 | tf_op jit(solution)/shard_map/all_to_all | solution.py:291
  133.6 10.7 %collective-permute-start.23 = (bf16[64,1024]{1,0:T(8,128)(2,1)S(1)}, bf16[64,1024]{1,0:T(8,128)(2,1)S(1)}, u32[]{:S(2)}, u32[]{:S(2)}) collective-permute-start(bf16[64,1024]{1,0:T(8,128)(2,1)S(1)} %shard_map.125.refs_0_), channel_id=1, source_target_pairs={{0,16},{16,0},{32,48},{48,32},{64,80},{80,64},{96,112},{112,96},{1... | collective-permute-start | bytes 393224 | tf_op jit(solution)/shard_map/ppermute | solution.py:386
  133.7 13.2 %collective-permute-start.24 = (bf16[64,1024]{1,0:T(8,128)(2,1)S(1)}, bf16[64,1024]{1,0:T(8,128)(2,1)S(1)}, u32[]{:S(2)}, u32[]{:S(2)}) collective-permute-start(bf16[64,1024]{1,0:T(8,128)(2,1)S(1)} %shard_map.125.refs_0_), channel_id=1, source_target_pairs={{0,32},{16,48},{32,64},{48,80},{64,96},{80,112},{96,0},{112,16},{1... | collective-permute-start | bytes 393224 | tf_op jit(solution)/shard_map/ppermute | solution.py:385
  134.9 12.0 %collective-permute-start.25 = (bf16[64,1024]{1,0:T(8,128)(2,1)S(1)}, bf16[64,1024]{1,0:T(8,128)(2,1)S(1)}, u32[]{:S(2)}, u32[]{:S(2)}) collective-permute-start(bf16[64,1024]{1,0:T(8,128)(2,1)S(1)} %shard_map.125.refs_0_), channel_id=1, source_target_pairs={{0,64},{16,80},{32,96},{48,112},{64,0},{80,16},{96,32},{112,48},{1... | collective-permute-start | bytes 393224 | tf_op jit(solution)/shard_map/ppermute | solution.py:385
  138.2 8.8 %collective-permute-start.26 = (bf16[64,1024]{1,0:T(8,128)(2,1)S(1)}, bf16[64,1024]{1,0:T(8,128)(2,1)S(1)}, u32[]{:S(2)}, u32[]{:S(2)}) collective-permute-start(bf16[64,1024]{1,0:T(8,128)(2,1)S(1)} %shard_map.125.refs_0_), channel_id=1, source_target_pairs={{0,96},{16,112},{32,0},{48,16},{64,32},{80,48},{96,64},{112,80},{1... | collective-permute-start | bytes 393224 | tf_op jit(solution)/shard_map/ppermute | solution.py:385
  147.0 2.0 %collective-permute-start.27 = (bf16[64,1024]{1,0:T(8,128)(2,1)S(1)}, bf16[64,1024]{1,0:T(8,128)(2,1)S(1)}, u32[]{:S(2)}, u32[]{:S(2)}) collective-permute-start(bf16[64,1024]{1,0:T(8,128)(2,1)S(1)} %collective-permute-done.24.refs_1_), channel_id=1, source_target_pairs={{0,16},{16,0},{32,48},{48,32},{64,80},{80,64},{96,112},{112,96},{1... | collective-permute-start | bytes 393224 | tf_op jit(solution)/shard_map/ppermute | solution.py:390
  147.1 1.9 %collective-permute-start.28 = (bf16[64,1024]{1,0:T(8,128)(2,1)S(1)}, bf16[64,1024]{1,0:T(8,128)(2,1)S(1)}, u32[]{:S(2)}, u32[]{:S(2)}) collective-permute-start(bf16[64,1024]{1,0:T(8,128)(2,1)S(1)} %collective-permute-done.25.refs_2_), channel_id=1, source_target_pairs={{0,16},{16,0},{32,48},{48,32},{64,80},{80,64},{96,112},{112,96},{1... | collective-permute-start | bytes 393224 | tf_op jit(solution)/shard_map/ppermute | solution.py:390
  147.6 1.4 collective-permute-start.29

commit v7 on v5

--- a/solution.py
+++ b/solution.py
@@ -99,10 +99,26 @@
         outs[2 * n + 1][...] = dot32(x_ref[...], wu_ref[:, here]).astype(BF16)
 
 
-def hidden_part(half_index, x, w_gate, w_up, blocks=2):
+def hidden_part_and_fetch_kernel(half_ref, x_ref, wg_ref, wu_ref, far_ref, *refs):
+    outs, (held_ref, sems) = refs[:-2], refs[-2:]
+    (copy,) = start_copies([(far_ref, held_ref)], sems)
+    hidden_part_kernel(half_ref, x_ref, wg_ref, wu_ref, *outs)
+    copy.wait()
+
+
+def hidden_part(half_index, x, w_gate, w_up, fetch=None, blocks=2):
     part = jax.ShapeDtypeStruct((x.shape[0], w_gate.shape[1] // 2 // blocks), BF16)
+    args = (half_index, x, w_gate, w_up)
+    if fetch is None:
+        return call(hidden_part_kernel, [part] * (2 * blocks), *args, scalars=1)
     return call(
-        hidden_part_kernel, [part] * (2 * blocks), half_index, x, w_gate, w_up, scalars=1
+        hidden_part_and_fetch_kernel,
+        [part] * (2 * blocks) + [pltpu.VMEM(fetch.shape, fetch.dtype)],
+        *args,
+        fetch,
+        scalars=1,
+        far=1,
+        copies=1,
     )
 
 
@@ -327,6 +343,10 @@
         )
         for step in range(STEPS):
             gathered = exchange(spread, "gy").reshape(rows, width)
+            near_query = w_query
+            give = hidden_part(other_half, gathered, w_gate, w_up, w_query if step == 0 else None)
+            if step == 0:
+                *give, near_query = give
             packed, squares = call(
                 query_kernel,
                 (
@@ -336,9 +356,8 @@
                 gathered,
                 gain,
                 w_keyval.T,
-                w_query,
+                near_query,
             )
-            give = hidden_part(other_half, gathered, w_gate, w_up)
             other = [lax.ppermute(part, "gx", core_swap) for part in (*give, squares)]
             keep = hidden_part(mine_half, gathered, w_gate, w_up)
             packed = lax.optimization_barrier((packed, give, keep))[0]
@@ -380,7 +399,7 @@
             own_other = lax.ppermute(hidden, "gx", core_swap)
             heads_all = lax.optimization_barrier((heads_all, own_other))[0]
             heads_part, held_down = heads_output(heads_all, w_out, w_down)
-            late = lax.optimization_barrier((pieces[1:], heads_part))[0]
+            late = [lax.optimization_barrier((piece, heads_part))[0] for piece in pieces[1:]]
             others = [own_other] + [lax.ppermute(piece, "gx", core_swap) for piece in late]
             part = output_part(place, pieces, heads_part, held_down, False, F32)
             delta = output_part(place, others, part, held_down, True, BF16)

time: 171 us -> 167 us (0.977)
  local copies, waits for them, and re-layouts: 6.29 us -> 3.87 us
  transfers between devices with their start and end apart: 34 -> 34, of which waited for: 6 -> 6; matrix products, arithmetic and copies ran while one was open for 3% -> 2% of each run, Pallas kernels for 10% -> 10%
where the time goes in v7:
time: 167 us
  blocking collectives  65.8 us (39%)
  starting transfers between devices  49.6 us (30%)
  Pallas kernels  28.1 us (17%)
  waiting for transfers between devices  18.2 us (11%)
  local copies, waits for them, and re-layouts  3.87 us (2%)
    all_to_all x4, blocking collectives, exchange(): return lax.all_to_all(parts, axis, split_axis=0, concat_axis=0, tiled=False)  65.8 us
    pallas_call x21, Pallas kernels, call(): pl.pallas_call(kernel, out_shape=out_shape, in_specs=[SMEM] * scalars + [...  28.1 us
    all_to_all x4, starting transfers between devices, exchange(): return lax.all_to_all(parts, axis, split_axis=0, concat_axis=0, tiled=False)  23.7 us
    all_to_all x4, waiting for transfers between devices, exchange(): return lax.all_to_all(parts, axis, split_axis=0, concat_axis=0, tiled=False)  14.9 us
    ppermute x6, starting transfers between devices, body(): lax.ppermute(pair[n], 'gx', z_shift(n))  11.1 us
    ppermute x6, starting transfers between devices, body(): lax.ppermute(hidden, 'gx', z_shift(n))  10.7 us
  transfers between devices with their start and end apart: 34, of which 6 were waited for; matrix products, arithmetic and copies ran while one was open for 2% of the time, Pallas kernels for 10%

profile of v7, /device:TPU:0, one launch (start us, length us, event | category | flops | bytes accessed | tf_op | source)
XLA Modules:
  0.0 166.7 jit_solution(248239391079103754)
XLA Ops:
  0.1 1.1 shard_map.109
  1.1 18.7 %all_to_all.40 = bf16[16,16,1024]{2,1,0:T(8,128)(2,1)S(1)} all-to-all(bf16[16,16,1024]{2,1,0:T(8,128)(2,1)S(1)} %shard_map.109), channel_id=1, replica_groups=mesh['gx'=8,'gy'=16] {'gy'}, dimensions={0} | all-to-all | bytes 1048576 | tf_op jit(solution)/shard_map/all_to_all | solution.py:305
  19.8 1.3 shard_map.110
  21.1 1.3 shard_map.111
  22.4 0.6 shard_map.112
  23.0 0.8 reshape.45
  23.9 7.5 %all-to-all-start.1 = ((bf16[128,2,640]{2,1,0:T(2,128)(2,1)}), bf16[128,2,640]{2,1,0:T(2,128)(2,1)S(1)}, u32[]{:S(2)}, u32[]{:S(2)}) async-start(bf16[128,2,640]{2,1,0:T(2,128)(2,1)} %reshape.45), calls=%async_computation.1 | async-start | bytes 655360 | tf_op jit(solution)/shard_map/all_to_all | solution.py:305
  31.5 0.5 collective-permute-start.1
  32.0 0.1 collective-permute-start.2
  32.1 0.4 collective-permute-start.3
  32.6 1.6 collective-permute-done.4.refs_9_
  34.3 0.8 shard_map.113
  35.1 1.1 collective-permute-start.5
  36.3 3.2 %collective-permute-start.6 = (bf16[64,2176]{1,0:T(8,128)(2,1)S(1)}, bf16[64,2176]{1,0:T(8,128)(2,1)S(1)}, u32[]{:S(2)}, u32[]{:S(2)}) collective-permute-start(bf16[64,2176]{1,0:T(8,128)(2,1)S(1)} %get-tuple-element.83), channel_id=1, source_target_pairs={{0,64},{16,80},{32,96},{48,112},{64,0},{80,16},{96,32},{112,48},{1... | collective-permute-start | bytes 835592 | tf_op jit(solution)/shard_map/ppermute | solution.py:376
  39.5 1.2 collective-permute-start.7
  40.7 2.3 %all-to-all-done.1 = bf16[128,2,640]{2,1,0:T(2,128)(2,1)S(1)} async-done(((bf16[128,2,640]{2,1,0:T(2,128)(2,1)}), bf16[128,2,640]{2,1,0:T(2,128)(2,1)S(1)}, u32[]{:S(2)}, u32[]{:S(2)}) %all-to-all-start.1) | async-done | bytes 327712 | tf_op jit(solution)/shard_map/all_to_all | solution.py:305
  43.0 0.3 convert_reduce_fusion.1
  43.4 3.6 %shard_map.114 = (bf16[2,16,512]{2,1,0:T(8,128)(2,1)S(1)}, f32[2,512]{1,0:T(2,128)S(1)}) custom-call(s32[2]{0:T(128)S(1)} %copy-done.8, f32[2,16,640]{2,1,0:T(8,128)S(1)} %bitcast.33, f32[2,512]{1,0:T(2,128)S(1)} %reshape.46.raw_ref, bf16[2,2048,256]{2,1,0:T(8,128)(2,1)} %refs_1_.3, bf16[2,2048,256]{2,1,0:T(8,128)(2,1)} %refs_2_.1), custom_call_target="tpu_custom_call" | custom-call | tf_op jit(solution)/shard_map/pallas_call | solution.py:39
  47.0 0.8 broadcast_in_dim.7
  47.8 5.4 %all-to-all-start.2 = ((bf16[128,2,512]{2,1,0:T(2,128)(2,1)}), bf16[128,2,512]{2,1,0:T(2,128)(2,1)S(1)}, u32[]{:S(2)}, u32[]{:S(2)}) async-start(bf16[128,2,512]{2,1,0:T(2,128)(2,1)} %bitcast.8), calls=%async_computation.2 | async-start | bytes 524288 | tf_op jit(solution)/shard_map/all_to_all | solution.py:305
  53.3 0.3 shard_map.115.refs_0_
  53.7 3.0 %collective-permute-start.11 = (bf16[64,1024]{1,0:T(8,128)(2,1)S(1)}, bf16[64,1024]{1,0:T(8,128)(2,1)S(1)}, u32[]{:S(2)}, u32[]{:S(2)}) collective-permute-start(bf16[64,1024]{1,0:T(8,128)(2,1)S(1)} %shard_map.115.refs_0_), channel_id=1, source_target_pairs={{0,64},{16,80},{32,96},{48,112},{64,0},{80,16},{96,32},{112,48},{1... | collective-permute-start | bytes 393224 | tf_op jit(solution)/shard_map/ppermute | solution.py:398
  56.7 0.9 collective-permute-start.13
  57.6 1.1 collective-permute-start.9
  58.7 5.4 %all-to-all-done.2 = bf16[128,2,512]{2,1,0:T(2,128)(2,1)S(1)} async-done(((bf16[128,2,512]{2,1,0:T(2,128)(2,1)}), bf16[128,2,512]{2,1,0:T(2,128)(2,1)S(1)}, u32[]{:S(2)}, u32[]{:S(2)}) %all-to-all-start.2) | async-done | bytes 262176 | tf_op jit(solution)/shard_map/all_to_all | solution.py:305
  64.2 0.1 reshape.48.heads_ref
  64.3 2.6 %shard_map.116 = (f32[256,1024]{1,0:T(8,128)S(1)}, bf16[2048,1024]{1,0:T(8,128)(2,1)S(1)}) custom-call(bf16[256,512]{1,0:T(8,128)(2,1)S(1)} %reshape.48.heads_ref, bf16[512,1024]{1,0:T(8,128)(2,1)} %wout_ref.3, bf16[2048,1024]{1,0:T(8,128)(2,1)} %down_ref.3), custom_call_target="tpu_custom_call" | custom-call | flops 10000000000 | tf_op jit(solution)/shard_map/pallas_call | solution.py:39
  67.0 0.5 collective-permute-start.12
  67.5 0.3 collective-permute-start.10
  67.8 1.3 shard_map.117.refs_4_
  69.1 1.3 shard_map.118
  70.4 16.4 %all_to_all.41.delta_ref = bf16[16,16,1024]{2,1,0:T(8,128)(2,1)S(1)} all-to-all(bf16[16,16,1024]{2,1,0:T(8,128)(2,1)S(1)} %bitcast.29), channel_id=1, replica_groups=mesh['gx'=8,'gy'=16] {'gy'}, dimensions={0} | all-to-all | bytes 1048576 | tf_op jit(solution)/shard_map/all_to_all | solution.py:305
  86.8 0.1 shard_map.119
  87.0 14.3 %all_to_all.42 = bf16[16,16,1024]{2,1,0:T(8,128)(2,1)S(1)} all-to-all(bf16[16,16,1024]{2,1,0:T(8,128)(2,1)S(1)} %get-tuple-element.100), channel_id=1, replica_groups=mesh['gx'=8,'gy'=16] {'gy'}, dimensions={0} | all-to-all | bytes 1048576 | tf_op jit(solution)/shard_map/all_to_all | solution.py:305
  101.3 1.3 shard_map.122
  102.6 1.3 shard_map.120
  103.8 0.6 shard_map.121
  104.4 0.8 reshape.51
  105.3 5.4 %all-to-all-start.5 = ((bf16[128,2,640]{2,1,0:T(2,128)(2,1)}), bf16[128,2,640]{2,1,0:T(2,128)(2,1)S(1)}, u32[]{:S(2)}, u32[]{:S(2)}) async-start(bf16[128,2,640]{2,1,0:T(2,128)(2,1)} %reshape.51), calls=%async_computation.5 | async-start | bytes 655360 | tf_op jit(solution)/shard_map/all_to_all | solution.py:305
  110.7 0.5 collective-permute-start.16
  111.3 0.4 collective-permute-start.18
  111.8 1.6 collective-permute-done.19.refs_9_
  113.5 0.8 shard_map.123
  114.3 1.1 collective-permute-start.20
  115.5 3.2 %collective-permute-start.21 = (bf16[64,2176]{1,0:T(8,128)(2,1)S(1)}, bf16[64,2176]{1,0:T(8,128)(2,1)S(1)}, u32[]{:S(2)}, u32[]{:S(2)}) collective-permute-start(bf16[64,2176]{1,0:T(8,128)(2,1)S(1)} %get-tuple-element.112), channel_id=1, source_target_pairs={{0,64},{16,80},{32,96},{48,112},{64,0},{80,16},{96,32},{112,48},{1... | collective-permute-start | bytes 835592 | tf_op jit(solution)/shard_map/ppermute | solution.py:376
  118.7 1.2 collective-permute-start.22
  119.9 2.3 %all-to-all-done.5 = bf16[128,2,640]{2,1,0:T(2,128)(2,1)S(1)} async-done(((bf16[128,2,640]{2,1,0:T(2,128)(2,1)}), bf16[128,2,640]{2,1,0:T(2,128)(2,1)S(1)}, u32[]{:S(2)}, u32[]{:S(2)}) %all-to-all-start.5) | async-done | bytes 327712 | tf_op jit(solution)/shard_map/all_to_all | solution.py:305
  122.2 0.3 convert_reduce_fusion
  122.6 3.7 %shard_map.124 = (bf16[2,16,512]{2,1,0:T(8,128)(2,1)S(1)}, f32[2,512]{1,0:T(2,128)}) custom-call(s32[2]{0:T(128)S(1)} %copy-done.8, f32[2,16,640]{2,1,0:T(8,128)S(1)} %bitcast.31, f32[2,512]{1,0:T(2,128)S(1)} %reshape.52.raw_ref, f32[2,512]{1,0:T(2,128)S(1)} %get-tuple-element.117.refs_0_, bf16[2,2048,256]{2,1,0:T(8,128)(2,1)} %refs_1_.3, ...), custom_call_target="tpu_custom_call" | custom-call | tf_op jit(solution)/shard_map/pallas_call | solution.py:39
  126.3 0.8 broadcast_in_dim.8
  127.2 5.4 %all-to-all-start.6 = ((bf16[128,2,512]{2,1,0:T(2,128)(2,1)}), bf16[128,2,512]{2,1,0:T(2,128)(2,1)S(1)}, u32[]{:S(2)}, u32[]{:S(2)}) async-start(bf16[128,2,512]{2,1,0:T(2,128)(2,1)} %bitcast.14), calls=%async_computation.6 | async-start | bytes 524288 | tf_op jit(solution)/shard_map/all_to_all | solution.py:305
  132.7 0.3 shard_map.125.refs_0_
  133.0 1.2 collective-permute-start.24
  134.3 3.2 %collective-permute-start.26 = (bf16[64,1024]{1,0:T(8,128)(2,1)S(1)}, bf16[64,1024]{1,0:T(8,128)(2,1)S(1)}, u32[]{:S(2)}, u32[]{:S(2)}) collective-permute-start(bf16[64,1024]{1,0:T(8,128)(2,1)S(1)} %shard_map.125.refs_0_), channel_id=1, source_target_pairs={{0,64},{16,80},{32,96},{48,112},{64,0},{80,16},{96,32},{112,48},{1... | collective-permute-start | bytes 393224 | tf_op jit(solution)/shard_map/ppermute | solution.py:398
  137.5 1.2 collective-permute-start.28
  138.7 4.8 %all-to-all-done.6 = bf16[128,2,512]{2,1,0:T(2,128)(2,1)S(1)} async-done(((bf16[128,2,512]{2,1,0:T(2,128)(2,1)}), bf16[128,2,512]{2,1,0:T(2,128)(2,1)S(1)}, u32[]{:S(2)}, u32[]{:S(2)}) %all-to-all-start.6) | async-done | bytes 262176 | tf_op jit(solution)/shard_map/all_to_all | solution.py:305
  143.5 0.1 reshape.54.heads_ref
  143.6 2.6 %shard_map.126 = (f32[256,1024]{1,0:T(8,128)S(1)}, bf16[2048,1024]{1,0:T(8,128)(2,1)S(1)}) custom-call(bf16[256,512]{1,0:T(8,128)(2,1)S(1)} %reshape.54.heads_ref, bf16[512,1024]{1,0:T(8,128)(2,1)} %wout_ref.3, bf16[2048,1024]{1,0:T(8,128)(2,1)} %down_ref.3), custom_call_target="tpu_custom_call" | custom-call | flops 10000000000 | tf_op jit(solution)/shard_map/pallas_call | solution.py:39
  146.4 0.5 collective-permute-start.27
  146.9 0.1 collective-permute-start.25
  147.0 1.3 shard_map.127.refs_4_
  148.3 1.3 shard_map.128
  149.6 16.4 %all_to_all.43.delta_ref = bf16[16,16,1024]{2,1,0:T(8,128)(2,1)S(1)} all-to-all(bf16[16,16,1024]{2,1,0:T(8,128)(2,1)S(1)} %bitcast.28), channel_id=1, replica_groups=mesh['gx'=8,'gy'=16] {'gy'}, dimensions={0} | all-to-all | bytes 1048576 | tf_op jit(solution)/shard_map/all_to_all | solution.py:305
  166.0 0.7 shard_map.129
  (64 shorter events, 1.2 us)
Async XLA Ops:
  0.1 19.7 %copy-start = (bf16[1024,2048]{1,0:T(8,128)(2,1)S(1)}, bf16[1024,2048]{1,0:T(8,128)(2,1)}, u32[]{:S(2)}) copy-start(bf16[1024,2048]{1,0:T(8,128)(2,1)} %wg_ref.7) | copy-start | bytes 12582916
  0.1 19.7 %copy-start.2 = (bf16[1024,2048]{1,0:T(8,128)(2,1)S(1)}, bf16[1024,2048]{1,0:T(8,128)(2,1)}, u32[]{:S(2)}) copy-start(bf16[1024,2048]{1,0:T(8,128)(2,1)} %wu_ref.7) | copy-start | bytes 12582916
  21.1 1.3 copy-start.5
  21.1 1.3 copy-start.6
  22.4 21.0 %copy-start.8 = (s32[2]{0:T(128)S(1)}, s32[2]{0:T(128)}, u32[]{:S(2)}) copy-start(s32[2]{0:T(128)} %lengths_ref.3) | copy-start | bytes 28
  23.9 19.1 %all-to-all-start.1 = ((bf16[128,2,640]{2,1,0:T(2,128)(2,1)}), bf16[128,2,640]{2,1,0:T(2,128)(2,1)S(1)}, u32[]{:S(2)}, u32[]{:S(2)}) async-start(bf16[128,2,640]{2,1,0:T(2,128)(2,1)} %reshape.45), calls=%async_computation.1 | async-start | bytes 655360 | tf_op jit(solution)/shard_map/all_to_all | solution.py:305
  31.4 2.8 %collective-permute-start = (bf16[256,512]{1,0:T(8,128)(2,1)S(1)}, bf16[256,512]{1,0:T(8,128)(2,1)S(1)}, u32[]{:S(2)}, u32[]{:S(2)}) collective-permute-start(bf16[256,512]{1,0:T(8,128)(2,1)S(1)} %get-tuple-element.77), channel_id=1, source_target_pairs={{0,16},{16,0},{32,48},{48,32},{64,80},{80,64},{96,112},{112,96},{1... | collective-permute-start | bytes 786440 | tf_op jit(solution)/shard_map/ppermute | solution.py:361
  31.5 2.7 %collective-permute-start.1 = (bf16[256,512]{1,0:T(8,128)(2,1)S(1)}, bf16[256,512]{1,0:T(8,128)(2,1)S(1)}, u32[]{:S(2)}, u32[]{:S(2)}) collective-permute-start(bf16[256,512]{1,0:T(8,128)(2,1)S(1)} %get-tuple-element.78), channel_id=1, source_target_pairs={{0,16},{16,0},{32,48},{48,32},{64,80},{80,64},{96,112},{112,96},{1... | collective-permute-start | bytes 786440 | tf_op jit(solution)/shard_map/ppermute | solution.py:361
  32.0 2.3 %collective-permute-start.2 = (bf16[256,512]{1,0:T(8,128)(2,1)S(1)}, bf16[256,512]{1,0:T(8,128)(2,1)S(1)}, u32[]{:S(2)}, u32[]{:S(2)}) collective-permute-start(bf16[256,512]{1,0:T(8,128)(2,1)S(1)} %get-tuple-element.79), channel_id=1, source_target_pairs={{0,16},{16,0},{32,48},{48,32},{64,80},{80,64},{96,112},{112,96},{1... | collective-permute-start | bytes 786440 | tf_op jit(solution)/shard_map/ppermute | solution.py:361
  32.1 2.2 %collective-permute-start.3 = (bf16[256,512]{1,0:T(8,128)(2,1)S(1)}, bf16[256,512]{1,0:T(8,128)(2,1)S(1)}, u32[]{:S(2)}, u32[]{:S(2)}) collective-permute-start(bf16[256,512]{1,0:T(8,128)(2,1)S(1)} %get-tuple-element.80), channel_id=1, source_target_pairs={{0,16},{16,0},{32,48},{48,32},{64,80},{80,64},{96,112},{112,96},{1... | collective-permute-start | bytes 786440 | tf_op jit(solution)/shard_map/ppermute | solution.py:361
  32.5 1.7 %collective-permute-start.4 = (bf16[256,128]{1,0:T(8,128)(2,1)S(1)}, bf16[256,128]{1,0:T(8,128)(2,1)S(1)}, u32[]{:S(2)}, u32[]{:S(2)}) collective-permute-start(bf16[256,128]{1,0:T(8,128)(2,1)S(1)} %get-tuple-element.76.refs_4_), channel_id=1, source_target_pairs={{0,16},{16,0},{32,48},{48,32},{64,80},{80,64},{96,112},{112,96},{1... | collective-permute-start | bytes 196616 | tf_op jit(solution)/shard_map/ppermute | solution.py:361
  35.1 18.2 %collective-permute-start.5 = (bf16[64,2176]{1,0:T(8,128)(2,1)S(1)}, bf16[64,2176]{1,0:T(8,128)(2,1)S(1)}, u32[]{:S(2)}, u32[]{:S(2)}) collective-permute-start(bf16[64,2176]{1,0:T(8,128)(2,1)S(1)} %get-tuple-element.82), channel_id=1, source_target_pairs={{0,32},{16,48},{32,64},{48,80},{64,96},{80,112},{96,0},{112,16},{1... | collective-permute-start | bytes 835592 | tf_op jit(solution)/shard_map/ppermute | solution.py:376
  36.3 17.0 %collective-permute-start.6 = (bf16[64,2176]{1,0:T(8,128)(2,1)S(1)}, bf16[64,2176]{1,0:T(8,128)(2,1)S(1)}, u32[]{:S(2)}, u32[]{:S(2)}) collective-permute-start(bf16[64,2176]{1,0:T(8,128)(2,1)S(1)} %get-tuple-element.83), channel_id=1, source_target_pairs={{0,64},{16,80},{32,96},{48,112},{64,0},{80,16},{96,32},{112,48},{1... | collective-permute-start | bytes 835592 | tf_op jit(solution)/shard_map/ppermute | solution.py:376
  39.5 13.8 %collective-permute-start.7 = (bf16[64,2176]{1,0:T(8,128)(2,1)S(1)}, bf16[64,2176]{1,0:T(8,128)(2,1)S(1)}, u32[]{:S(2)}, u32[]{:S(2)}) collective-permute-start(bf16[64,2176]{1,0:T(8,128)(2,1)S(1)} %get-tuple-element.84), channel_id=1, source_target_pairs={{0,96},{16,112},{32,0},{48,16},{64,32},{80,48},{96,64},{112,80},{1... | collective-permute-start | bytes 835592 | tf_op jit(solution)/shard_map/ppermute | solution.py:376
  47.8 16.3 %all-to-all-start.2 = ((bf16[128,2,512]{2,1,0:T(2,128)(2,1)}), bf16[128,2,512]{2,1,0:T(2,128)(2,1)S(1)}, u32[]{:S(2)}, u32[]{:S(2)}) async-start(bf16[128,2,512]{2,1,0:T(2,128)(2,1)} %bitcast.8), calls=%async_computation.2 | async-start | bytes 524288 | tf_op jit(solution)/shard_map/all_to_all | solution.py:305
  53.6 10.7 %collective-permute-start.8 = (bf16[64,1024]{1,0:T(8,128)(2,1)S(1)}, bf16[64,1024]{1,0:T(8,128)(2,1)S(1)}, u32[]{:S(2)}, u32[]{:S(2)}) collective-permute-start(bf16[64,1024]{1,0:T(8,128)(2,1)S(1)} %shard_map.115.refs_0_), channel_id=1, source_target_pairs={{0,16},{16,0},{32,48},{48,32},{64,80},{80,64},{96,112},{112,96},{1... | collective-permute-start | bytes 393224 | tf_op jit(solution)/shard_map/ppermute | solution.py:399
  53.7 13.3 %collective-permute-start.11 = (bf16[64,1024]{1,0:T(8,128)(2,1)S(1)}, bf16[64,1024]{1,0:T(8,128)(2,1)S(1)}, u32[]{:S(2)}, u32[]{:S(2)}) collective-permute-start(bf16[64,1024]{1,0:T(8,128)(2,1)S(1)} %shard_map.115.refs_0_), channel_id=1, source_target_pairs={{0,64},{16,80},{32,96},{48,112},{64,0},{80,16},{96,32},{112,48},{1... | collective-permute-start | bytes 393224 | tf_op jit(solution)/shard_map/ppermute | solution.py:398
  56.7 10.2 %collective-permute-start.13 = (bf16[64,1024]{1,0:T(8,128)(2,1)S(1)}, bf16[64,1024]{1,0:T(8,128)(2,1)S(1)}, u32[]{:S(2)}, u32[]{:S(2)}) collective-permute-start(bf16[64,1024]{1,0:T(8,128)(2,1)S(1)} %shard_map.115.refs_0_), channel_id=1, source_target_pairs={{0,96},{16,112},{32,0},{48,16},{64,32},{80,48},{96,64},{112,80},{1... | collective-permute-start | bytes 393224 | tf_op jit(solution)/shard_map/ppermute | solution.py:398
  57.6 9.9 %collective-permute-start.9 = (bf16[64,1024]{1,0:T(8,128)(2,1)S(1)}, bf16[64,1024]{1,0:T(8,128)(2,1)S(1)}, u32[]{:S(2)}, u32[]{:S(2)}) collective-permute-start(bf16[64,1024]{1,0:T(8,128)(2,1)S(1)} %shard_map.115.refs_0_), channel_id=1, source_target_pairs={{0,32},{16,48},{32,64},{48,80},{64,96},{80,112},{96,0},{112,16},{1... | collective-permute-start | bytes 393224 | tf_op jit(solution)/shard_map/ppermute | solution.py:398
  66.9 2.2 %collective-permute-start.14 = (bf16[64,1024]{1,0:T(8,128)(2,1)S(1)}, bf16[64,1024]{1,0:T(8,128)(2,1)S(1)}, u32[]{:S(2)}, u32[]{:S(2)}) collective-permute-start(bf16[64,1024]{1,0:T(8,128)(2,1)S(1)} %collective-permute-done.13.refs_3_), channel_id=1, source_target_pairs={{0,16},{16,0},{32,48},{48,32},{64,80},{80,64},{96,112},{112,96},{1... | collective-permute-start | bytes 393224 | tf_op jit(solution)/shard_map/ppermute | solution.py:403
  67.0 2.1 %collective-permute-start.12 = (bf16[64,1024]{1,0:T(8,128)(2,1)S(1)}, bf16[64,1024]{1,0:T(8,128)(2,1)S(1)}, u32[]{:S(2)}, u32[]{:S(2)}) collective-permute-start(bf16[64,1024]{1,0:T(8,128)(2,1)S(1)} %collective-permute-done.11.refs_2_), channel_id=1, source_target_pairs={{0,16},{16,0},{32,48},{48,32},{64,80},{80,64},{96,112},{112,96},{1... | collective-permute-start | bytes 393224 | tf_op jit(solution)/shard_map/ppermute | solution.py:403
  67.5 1.6 collective-permute-start.10
  67.8 19.1 %copy-start.7 = (f32[16,1024]{1,0:T(8,128)S(1)}, f32[16,1024]{1,0:T(8,128)}, u32[]{:S(2)}) copy-start(f32[16,1024]{1,0:T(8,128)} %x_ref.1) | copy-start | bytes 196612
  69.1 32.2 %copy-start.1 = (bf16[1024,2048]{1,0:T(8,128)(2,1)S(1)}, bf16[1024,2048]{1,0:T(8,128)(2,1)}, u32[]{:S(2)}) copy-start(bf16[1024,2048]{1,0:T(8,128)(2,1)} %wg_ref.7) | copy-start | bytes 12582916
  69.1 32.2 %copy-start.3 = (bf16[1024,2048]{1,0:T(8,128)(2,1)S(1)}, bf16[1024,2048]{1,0:T(8,128)(2,1)}, u32[]{:S(2)}) copy-start(bf16[1024,2048]{1,0:T(8,128)(2,1)} %wu_ref.7) | copy-start | bytes 12582916
  102.5 1.3 copy-start.4
  105.3 16.9 %all-to-all-start.5 = ((bf16[128,2,640]{2,1,0:T(2,128)(2,1)}), bf16[128,2,640]{2,1,0:T(2,128)(2,1)S(1)}, u32[]{:S(2)}, u32[]{:S(2)}) async-start(bf16[128,2,640]{2,1,0:T(2,128)(2,1)} %reshape.51), calls=%async_computation.5 | async-start | bytes 655360 | tf_op jit(solution)/shard_map/all_to_all | solution.py:305
  110.6 2.8 %collective-permute-start.15 = (bf16[256,512]{1,0:T(8,128)(2,1)S(1)}, bf16[256,512]{1,0:T(8,128)(2,1)S(1)}, u32[]{:S(2)}, u32[]{:S(2)}) collective-permute-start(bf16[256,512]{1,0:T(8,128)(2,1)S(1)} %get-tuple-element.106), channel_id=1, source_target_pairs={{0,16},{16,0},{32,48},{48,32},{64,80},{80,64},{96,112},{112,96},{1... | collective-permute-start | bytes 786440 | tf_op jit(solution)/shard_map/ppermute | solution.py:361
  110.7 2.7 %collective-permute-start.16 = (bf16[256,512]{1,0:T(8,128)(2,1)S(1)}, bf16[256,512]{1,0:T(8,128)(2,1)S(1)}, u32[]{:S(2)}, u32[]{:S(2)}) collective-permute-start(bf16[256,512]{1,0:T(8,128)(2,1)S(1)} %get-tuple-element.107), channel_id=1, source_target_pairs={{0,16},{16,0},{32,48},{48,32},{64,80},{80,64},{96,112},{112,96},{1... | collective-permute-start | bytes 786440 | tf_op jit(solution)/shard_map/ppermute | solution.py:361
  111.2 2.3 %collective-permute-start.17 = (bf16[256,512]{1,0:T(8,128)(2,1)S(1)}, bf16[256,512]{1,0:T(8,128)(2,1)S(1)}, u32[]{:S(2)}, u32[]{:S(2)}) collective-permute-start(bf16[256,512]{1,0:T(8,128)(2,1)S(1)} %get-tuple-element.108), channel_id=1, source_target_pairs={{0,16},{16,0},{32,48},{48,32},{64,80},{80,64},{96,112},{112,96},{1... | collective-permute-start | bytes 786440 | tf_op jit(solution)/shard_map/ppermute | solution.py:361
  111.3 2.2 %collective-permute-start.18 = (bf16[256,512]{1,0:T(8,128)(2,1)S(1)}, bf16[256,512]{1,0:T(8,128)(2,1)S(1)}, u32[]{:S(2)}, u32[]{:S(2)}) collective-permute-start(bf16[256,512]{1,0:T(8,128)(2,1)S(1)} %get-tuple-element.109), channel_id=1, source_target_pairs={{0,16},{16,0},{32,48},{48,32},{64,80},{80,64},{96,112},{112,96},{1... | collective-permute-start | bytes 786440 | tf_op jit(solution)/shard_map/ppermute | solution.py:361
  111.7 1.7 %collective-permute-start.19 = (bf16[256,128]{1,0:T(8,128)(2,1)S(1)}, bf16[256,128]{1,0:T(8,128)(2,1)S(1)}, u32[]{:S(2)}, u32[]{:S(2)}) collective-permute-start(bf16[256,128]{1,0:T(8,128)(2,1)S(1)} %get-tuple-element.105.refs_4_), channel_id=1, source_target_pairs={{0,16},{16,0},{32,48},{48,32},{64,80},{80,64},{96,112},{112,96},{1... | collective-permute-start | bytes 196616 | tf_op jit(solution)/shard_map/ppermute | solution.py:361
  114.3 18.3 %collective-permute-start.20 = (bf16[64,2176]{1,0:T(8,128)(2,1)S(1)}, bf16[64,2176]{1,0:T(8,128)(2,1)S(1)}, u32[]{:S(2)}, u32[]{:S(2)}) collective-permute-start(bf16[64,2176]{1,0:T(8,128)(2,1)S(1)} %get-tuple-element.111), channel_id=1, source_target_pairs={{0,32},{16,48},{32,64},{48,80},{64,96},{80,112},{96,0},{112,16},{1... | collective-permute-start | bytes 835592 | tf_op jit(solution)/shard_map/ppermute | solution.py:376
  115.5 17.1 %collective-permute-start.21 = (bf16[64,2176]{1,0:T(8,128)(2,1)S(1)}, bf16[64,2176]{1,0:T(8,128)(2,1)S(1)}, u32[]{:S(2)}, u32[]{:S(2)}) collective-permute-start(bf16[64,2176]{1,0:T(8,128)(2,1)S(1)} %get-tuple-element.112), channel_id=1, source_target_pairs={{0,64},{16,80},{32,96},{48,112},{64,0},{80,16},{96,32},{112,48},{1... | collective-permute-start | bytes 835592 | tf_op jit(solution)/shard_map/ppermute | solution.py:376
  118.7 13.9 %collective-permute-start.22 = (bf16[64,2176]{1,0:T(8,128)(2,1)S(1)}, bf16[64,2176]{1,0:T(8,128)(2,1)S(1)}, u32[]{:S(2)}, u32[]{:S(2)}) collective-permute-start(bf16[64,2176]{1,0:T(8,128)(2,1)S(1)} %get-tuple-element.113), channel_id=1, source_target_pairs={{0,96},{16,112},{32,0},{48,16},{64,32},{80,48},{96,64},{112,80},{1... | collective-permute-start | bytes 835592 | tf_op jit(solution)/shard_map/ppermute | solution.py:376
  127.2 16.3 %all-to-all-start.6 = ((bf16[128,2,512]{2,1,0:T(2,128)(2,1)}), bf16[128,2,512]{2,1,0:T(2,128)(2,1)S(1)}, u32[]{:S(2)}, u32[]{:S(2)}) async-start(bf16[128,2,512]{2,1,0:T(2,128)(2,1)} %bitcast.14), calls=%async_computation.6 | async-start | bytes 524288 | tf_op jit(solution)/shard_map/all_to_all | solution.py:305
  132.9 10.7 %collective-permute-start.23 = (bf16[64,1024]{1,0:T(8,128)(2,1)S(1)}, bf16[64,1024]{1,0:T(8,128)(2,1)S(1)}, u32[]{:S(2)}, u32[]{:S(2)}) collective-permute-start(bf16[64,1024]{1,0:T(8,128)(2,1)S(1)} %shard_map.125.refs_0_), channel_id=1, source_target_pairs={{0,16},{16,0},{32,48},{48,32},{64,80},{80,64},{96,112},{112,96},{1... | collective-permute-start | bytes 393224 | tf_op jit(solution)/shard_map/ppermute | solution.py:399
  133.0 13.8 %collective-permute-start.24 = (bf16[64,1024]{1,0:T(8,128)(2,1)S(1)}, bf16[64,1024]{1,0:T(8,128)(2,1)S(1)}, u32[]{:S(2)}, u32[]{:S(2)}) collective-permute-start(bf16[64,1024]{1,0:T(8,128)(2,1)S(1)} %shard_map.125.refs_0_), channel_id=1, source_target_pairs={{0,32},{16,48},{32,64},{48,80},{64,96},{80,112},{96,0},{112,16},{1... | collective-permute-start | bytes 393224 | tf_op jit(solution)/shard_map/ppermute | solution.py:398
  134.3 12.1 %collective-permute-start.26 = (bf16[64,1024]{1,0:T(8,128)(2,1)S(1)}, bf16[64,1024]{1,0:T(8,128)(2,1)S(1)}, u32[]{:S(2)}, u32[]{:S(2)}) collective-permute-start(bf16[64,1024]{1,0:T(8,128)(2,1)S(1)} %shard_map.125.refs_0_), channel_id=1, source_target_pairs={{0,64},{16,80},{32,96},{48,112},{64,0},{80,16},{96,32},{112,48},{1... | collective-permute-start | bytes 393224 | tf_op jit(solution)/shard_map/ppermute | solution.py:398
  137.5 8.8 %collective-permute-start.28 = (bf16[64,1024]{1,0:T(8,128)(2,1)S(1)}, bf16[64,1024]{1,0:T(8,128)(2,1)S(1)}, u32[]{:S(2)}, u32[]{:S(2)}) collective-permute-start(bf16[64,1024]{1,0:T(8,128)(2,1)S(1)} %shard_map.125.refs_0_), channel_id=1, source_target_pairs={{0,96},{16,112},{32,0},{48,16},{64,32},{80,48},{96,64},{112,80},{1... | collective-permute-start | bytes 393224 | tf_op jit(solution)/shard_map/ppermute | solution.py:398
  146.3 2.0 %collective-permute-start.29 = (bf16[64,1024]{1,0:T(8,128)(2,1)S(1)}, bf16[64,1024]{1,0:T(8,128)(2,1)S(1)}, u32[]{:S(2)}, u32[]{:S(2)}) collective-permute-start(bf16[64,1024]{1,0:T(8,128)(2,1)S(1)} %collective-permute-done.28.refs_3_), channel_id=1, source_target_pairs={{0,16},{16,0},{32,48},{48,32},{64,80},{80,64},{96,112},{112,96},{1... | collective-permute-start | bytes 393224 | tf_op jit(solution)/shard_map/ppermute | solution.py:403
  146.4 1.9 %collective-permute-start.27 = (bf16[64,1024]{1,0:T(8,128)(2,1)S(1)}, bf16[64,1024]{1,0:T(8,128)(2,1)S(1)}, u32[]{:S(2)}, u32[]{:S(2)}) collective-permute-start(bf16[64,1024]{1,0:T(8,128)(2,1)S(1)} %collective-permute-done.26.refs_2_), channel_id=1, source_target_pairs={{0,16},{16,0},{32,48},{48,32},{64,80},{80,64},{96,112},{112,96},{1... | collective-permute-start | bytes 393224 | tf_op jit(solution)/shard_map/ppermute | solution.py:403
  146.9 1.4 collective-permute-start.25

commit v8 on v7

--- a/solution.py
+++ b/solution.py
@@ -182,9 +182,8 @@
             [jnp.sum(heads32 * line[:, :DH], axis=1, keepdims=True) * scale for line in lines]
         )
         new_values.append([line[:, DH:] for line in lines])
-    for copy in key_copies[1:]:
-        copy.wait()
     for row in range(rows):
+        key_copies[row + 1].wait()
         old_s = lax.dot_general(
             heads[row], keys[row], (((1,), (1,)), ((), ())), preferred_element_type=F32
         )
@@ -202,9 +201,8 @@
             total = total + e
         share = 1.0 / total
         weights.append(((old_e * share).astype(BF16), [(e * share).astype(BF16) for e in new_e]))
-    for copy in value_copies:
-        copy.wait()
     for row in range(rows):
+        value_copies[row].wait()
         old_w, new_w = weights[row]
         result = dot32(old_w, values[row])
         for w, v in zip(new_w, new_values[row]):

time: 167 us -> 168 us (level)
  transfers between devices with their start and end apart: 34 -> 34, of which waited for: 6 -> 6; matrix products, arithmetic and copies ran while one was open for 2% -> 2% of each run, Pallas kernels for 10% -> 11%
where the time goes in v8:
time: 168 us; the launch traced here: 167 us
  blocking collectives  65.8 us (39%)
  starting transfers between devices  49.6 us (30%)
  Pallas kernels  28.4 us (17%)
  waiting for transfers between devices  18.2 us (11%)
  local copies, waits for them, and re-layouts  3.87 us (2%)
    all_to_all x4, blocking collectives, exchange(): return lax.all_to_all(parts, axis, split_axis=0, concat_axis=0, tiled=False)  65.8 us
    pallas_call x21, Pallas kernels, call(): pl.pallas_call(kernel, out_shape=out_shape, in_specs=[SMEM] * scalars + [...  28.4 us
    all_to_all x4, starting transfers between devices, exchange(): return lax.all_to_all(parts, axis, split_axis=0, concat_axis=0, tiled=False)  23.7 us
    all_to_all x4, waiting for transfers between devices, exchange(): return lax.all_to_all(parts, axis, split_axis=0, concat_axis=0, tiled=False)  14.9 us
    ppermute x6, starting transfers between devices, body(): lax.ppermute(pair[n], 'gx', z_shift(n))  11.1 us
    ppermute x6, starting transfers between devices, body(): lax.ppermute(hidden, 'gx', z_shift(n))  10.7 us
  transfers between devices with their start and end apart: 34, of which 6 were waited for; matrix products, arithmetic and copies ran while one was open for 2% of the time, Pallas kernels for 11%

profile of v8, /device:TPU:0, one launch (start us, length us, event | category | flops | bytes accessed | tf_op | source)
XLA Modules:
  0.0 167.0 jit_solution(2973651704465847698)
XLA Ops:
  0.1 1.1 shard_map.109
  1.1 18.7 %all_to_all.40 = bf16[16,16,1024]{2,1,0:T(8,128)(2,1)S(1)} all-to-all(bf16[16,16,1024]{2,1,0:T(8,128)(2,1)S(1)} %shard_map.109), channel_id=1, replica_groups=mesh['gx'=8,'gy'=16] {'gy'}, dimensions={0} | all-to-all | bytes 1048576 | tf_op jit(solution)/shard_map/all_to_all | solution.py:303
  19.8 1.3 shard_map.110
  21.1 1.3 shard_map.111
  22.4 0.6 shard_map.112
  23.0 0.8 reshape.45
  23.9 7.5 %all-to-all-start.1 = ((bf16[128,2,640]{2,1,0:T(2,128)(2,1)}), bf16[128,2,640]{2,1,0:T(2,128)(2,1)S(1)}, u32[]{:S(2)}, u32[]{:S(2)}) async-start(bf16[128,2,640]{2,1,0:T(2,128)(2,1)} %reshape.45), calls=%async_computation.1 | async-start | bytes 655360 | tf_op jit(solution)/shard_map/all_to_all | solution.py:303
  31.5 0.5 collective-permute-start.1
  32.0 0.1 collective-permute-start.2
  32.1 0.4 collective-permute-start.3
  32.6 1.6 collective-permute-done.4.refs_9_
  34.3 0.8 shard_map.113
  35.1 1.1 collective-permute-start.5
  36.3 3.2 %collective-permute-start.6 = (bf16[64,2176]{1,0:T(8,128)(2,1)S(1)}, bf16[64,2176]{1,0:T(8,128)(2,1)S(1)}, u32[]{:S(2)}, u32[]{:S(2)}) collective-permute-start(bf16[64,2176]{1,0:T(8,128)(2,1)S(1)} %get-tuple-element.83), channel_id=1, source_target_pairs={{0,64},{16,80},{32,96},{48,112},{64,0},{80,16},{96,32},{112,48},{1... | collective-permute-start | bytes 835592 | tf_op jit(solution)/shard_map/ppermute | solution.py:374
  39.5 1.2 collective-permute-start.7
  40.7 2.3 %all-to-all-done.1 = bf16[128,2,640]{2,1,0:T(2,128)(2,1)S(1)} async-done(((bf16[128,2,640]{2,1,0:T(2,128)(2,1)}), bf16[128,2,640]{2,1,0:T(2,128)(2,1)S(1)}, u32[]{:S(2)}, u32[]{:S(2)}) %all-to-all-start.1) | async-done | bytes 327712 | tf_op jit(solution)/shard_map/all_to_all | solution.py:303
  43.0 0.3 convert_reduce_fusion.1
  43.4 3.7 %shard_map.114 = (bf16[2,16,512]{2,1,0:T(8,128)(2,1)S(1)}, f32[2,512]{1,0:T(2,128)S(1)}) custom-call(s32[2]{0:T(128)S(1)} %copy-done.8, f32[2,16,640]{2,1,0:T(8,128)S(1)} %bitcast.33, f32[2,512]{1,0:T(2,128)S(1)} %reshape.46.raw_ref, bf16[2,2048,256]{2,1,0:T(8,128)(2,1)} %refs_1_.3, bf16[2,2048,256]{2,1,0:T(8,128)(2,1)} %refs_2_.1), custom_call_target="tpu_custom_call" | custom-call | tf_op jit(solution)/shard_map/pallas_call | solution.py:39
  47.1 0.8 broadcast_in_dim.7
  48.0 5.4 %all-to-all-start.2 = ((bf16[128,2,512]{2,1,0:T(2,128)(2,1)}), bf16[128,2,512]{2,1,0:T(2,128)(2,1)S(1)}, u32[]{:S(2)}, u32[]{:S(2)}) async-start(bf16[128,2,512]{2,1,0:T(2,128)(2,1)} %bitcast.8), calls=%async_computation.2 | async-start | bytes 524288 | tf_op jit(solution)/shard_map/all_to_all | solution.py:303
  53.4 0.3 shard_map.115.refs_0_
  53.8 3.0 %collective-permute-start.11 = (bf16[64,1024]{1,0:T(8,128)(2,1)S(1)}, bf16[64,1024]{1,0:T(8,128)(2,1)S(1)}, u32[]{:S(2)}, u32[]{:S(2)}) collective-permute-start(bf16[64,1024]{1,0:T(8,128)(2,1)S(1)} %shard_map.115.refs_0_), channel_id=1, source_target_pairs={{0,64},{16,80},{32,96},{48,112},{64,0},{80,16},{96,32},{112,48},{1... | collective-permute-start | bytes 393224 | tf_op jit(solution)/shard_map/ppermute | solution.py:396
  56.8 0.9 collective-permute-start.13
  57.7 1.1 collective-permute-start.9
  58.8 5.4 %all-to-all-done.2 = bf16[128,2,512]{2,1,0:T(2,128)(2,1)S(1)} async-done(((bf16[128,2,512]{2,1,0:T(2,128)(2,1)}), bf16[128,2,512]{2,1,0:T(2,128)(2,1)S(1)}, u32[]{:S(2)}, u32[]{:S(2)}) %all-to-all-start.2) | async-done | bytes 262176 | tf_op jit(solution)/shard_map/all_to_all | solution.py:303
  64.3 0.1 reshape.48.heads_ref
  64.4 2.6 %shard_map.116 = (f32[256,1024]{1,0:T(8,128)S(1)}, bf16[2048,1024]{1,0:T(8,128)(2,1)S(1)}) custom-call(bf16[256,512]{1,0:T(8,128)(2,1)S(1)} %reshape.48.heads_ref, bf16[512,1024]{1,0:T(8,128)(2,1)} %wout_ref.3, bf16[2048,1024]{1,0:T(8,128)(2,1)} %down_ref.3), custom_call_target="tpu_custom_call" | custom-call | flops 10000000000 | tf_op jit(solution)/shard_map/pallas_call | solution.py:39
  67.2 0.5 collective-permute-start.12
  67.6 0.3 collective-permute-start.10
  67.9 1.3 shard_map.117.refs_4_
  69.3 1.3 shard_map.118
  70.6 16.4 %all_to_all.41.delta_ref = bf16[16,16,1024]{2,1,0:T(8,128)(2,1)S(1)} all-to-all(bf16[16,16,1024]{2,1,0:T(8,128)(2,1)S(1)} %bitcast.29), channel_id=1, replica_groups=mesh['gx'=8,'gy'=16] {'gy'}, dimensions={0} | all-to-all | bytes 1048576 | tf_op jit(solution)/shard_map/all_to_all | solution.py:303
  87.0 0.1 shard_map.119
  87.1 14.3 %all_to_all.42 = bf16[16,16,1024]{2,1,0:T(8,128)(2,1)S(1)} all-to-all(bf16[16,16,1024]{2,1,0:T(8,128)(2,1)S(1)} %get-tuple-element.100), channel_id=1, replica_groups=mesh['gx'=8,'gy'=16] {'gy'}, dimensions={0} | all-to-all | bytes 1048576 | tf_op jit(solution)/shard_map/all_to_all | solution.py:303
  101.4 1.3 shard_map.122
  102.7 1.3 shard_map.120
  104.0 0.6 shard_map.121
  104.6 0.8 reshape.51
  105.4 5.3 %all-to-all-start.5 = ((bf16[128,2,640]{2,1,0:T(2,128)(2,1)}), bf16[128,2,640]{2,1,0:T(2,128)(2,1)S(1)}, u32[]{:S(2)}, u32[]{:S(2)}) async-start(bf16[128,2,640]{2,1,0:T(2,128)(2,1)} %reshape.51), calls=%async_computation.5 | async-start | bytes 655360 | tf_op jit(solution)/shard_map/all_to_all | solution.py:303
  110.9 0.5 collective-permute-start.16
  111.4 0.4 collective-permute-start.18
  112.0 1.6 collective-permute-done.19.refs_9_
  113.6 0.8 shard_map.123
  114.5 1.1 collective-permute-start.20
  115.6 3.2 %collective-permute-start.21 = (bf16[64,2176]{1,0:T(8,128)(2,1)S(1)}, bf16[64,2176]{1,0:T(8,128)(2,1)S(1)}, u32[]{:S(2)}, u32[]{:S(2)}) collective-permute-start(bf16[64,2176]{1,0:T(8,128)(2,1)S(1)} %get-tuple-element.112), channel_id=1, source_target_pairs={{0,64},{16,80},{32,96},{48,112},{64,0},{80,16},{96,32},{112,48},{1... | collective-permute-start | bytes 835592 | tf_op jit(solution)/shard_map/ppermute | solution.py:374
  118.8 1.2 collective-permute-start.22
  120.0 2.3 %all-to-all-done.5 = bf16[128,2,640]{2,1,0:T(2,128)(2,1)S(1)} async-done(((bf16[128,2,640]{2,1,0:T(2,128)(2,1)}), bf16[128,2,640]{2,1,0:T(2,128)(2,1)S(1)}, u32[]{:S(2)}, u32[]{:S(2)}) %all-to-all-start.5) | async-done | bytes 327712 | tf_op jit(solution)/shard_map/all_to_all | solution.py:303
  122.3 0.3 convert_reduce_fusion
  122.7 3.9 %shard_map.124 = (bf16[2,16,512]{2,1,0:T(8,128)(2,1)S(1)}, f32[2,512]{1,0:T(2,128)}) custom-call(s32[2]{0:T(128)S(1)} %copy-done.8, f32[2,16,640]{2,1,0:T(8,128)S(1)} %bitcast.31, f32[2,512]{1,0:T(2,128)S(1)} %reshape.52.raw_ref, f32[2,512]{1,0:T(2,128)S(1)} %get-tuple-element.117.refs_0_, bf16[2,2048,256]{2,1,0:T(8,128)(2,1)} %refs_1_.3, ...), custom_call_target="tpu_custom_call" | custom-call | tf_op jit(solution)/shard_map/pallas_call | solution.py:39
  126.7 0.8 broadcast_in_dim.8
  127.5 5.4 %all-to-all-start.6 = ((bf16[128,2,512]{2,1,0:T(2,128)(2,1)}), bf16[128,2,512]{2,1,0:T(2,128)(2,1)S(1)}, u32[]{:S(2)}, u32[]{:S(2)}) async-start(bf16[128,2,512]{2,1,0:T(2,128)(2,1)} %bitcast.14), calls=%async_computation.6 | async-start | bytes 524288 | tf_op jit(solution)/shard_map/all_to_all | solution.py:303
  133.0 0.3 shard_map.125.refs_0_
  133.4 1.2 collective-permute-start.24
  134.6 3.2 %collective-permute-start.26 = (bf16[64,1024]{1,0:T(8,128)(2,1)S(1)}, bf16[64,1024]{1,0:T(8,128)(2,1)S(1)}, u32[]{:S(2)}, u32[]{:S(2)}) collective-permute-start(bf16[64,1024]{1,0:T(8,128)(2,1)S(1)} %shard_map.125.refs_0_), channel_id=1, source_target_pairs={{0,64},{16,80},{32,96},{48,112},{64,0},{80,16},{96,32},{112,48},{1... | collective-permute-start | bytes 393224 | tf_op jit(solution)/shard_map/ppermute | solution.py:396
  137.8 1.2 collective-permute-start.28
  139.0 4.8 %all-to-all-done.6 = bf16[128,2,512]{2,1,0:T(2,128)(2,1)S(1)} async-done(((bf16[128,2,512]{2,1,0:T(2,128)(2,1)}), bf16[128,2,512]{2,1,0:T(2,128)(2,1)S(1)}, u32[]{:S(2)}, u32[]{:S(2)}) %all-to-all-start.6) | async-done | bytes 262176 | tf_op jit(solution)/shard_map/all_to_all | solution.py:303
  143.8 0.1 reshape.54.heads_ref
  143.9 2.6 %shard_map.126 = (f32[256,1024]{1,0:T(8,128)S(1)}, bf16[2048,1024]{1,0:T(8,128)(2,1)S(1)}) custom-call(bf16[256,512]{1,0:T(8,128)(2,1)S(1)} %reshape.54.heads_ref, bf16[512,1024]{1,0:T(8,128)(2,1)} %wout_ref.3, bf16[2048,1024]{1,0:T(8,128)(2,1)} %down_ref.3), custom_call_target="tpu_custom_call" | custom-call | flops 10000000000 | tf_op jit(solution)/shard_map/pallas_call | solution.py:39
  146.7 0.5 collective-permute-start.27
  147.2 0.1 collective-permute-start.25
  147.3 1.3 shard_map.127.refs_4_
  148.6 1.3 shard_map.128
  149.9 16.4 %all_to_all.43.delta_ref = bf16[16,16,1024]{2,1,0:T(8,128)(2,1)S(1)} all-to-all(bf16[16,16,1024]{2,1,0:T(8,128)(2,1)S(1)} %bitcast.28), channel_id=1, replica_groups=mesh['gx'=8,'gy'=16] {'gy'}, dimensions={0} | all-to-all | bytes 1048576 | tf_op jit(solution)/shard_map/all_to_all | solution.py:303
  166.3 0.7 shard_map.129
  (64 shorter events, 1.2 us)
Async XLA Ops:
  0.1 19.7 %copy-start = (bf16[1024,2048]{1,0:T(8,128)(2,1)S(1)}, bf16[1024,2048]{1,0:T(8,128)(2,1)}, u32[]{:S(2)}) copy-start(bf16[1024,2048]{1,0:T(8,128)(2,1)} %wg_ref.7) | copy-start | bytes 12582916
  0.1 19.7 %copy-start.2 = (bf16[1024,2048]{1,0:T(8,128)(2,1)S(1)}, bf16[1024,2048]{1,0:T(8,128)(2,1)}, u32[]{:S(2)}) copy-start(bf16[1024,2048]{1,0:T(8,128)(2,1)} %wu_ref.7) | copy-start | bytes 12582916
  21.1 1.3 copy-start.5
  21.1 1.3 copy-start.6
  22.4 21.0 %copy-start.8 = (s32[2]{0:T(128)S(1)}, s32[2]{0:T(128)}, u32[]{:S(2)}) copy-start(s32[2]{0:T(128)} %lengths_ref.3) | copy-start | bytes 28
  23.9 19.1 %all-to-all-start.1 = ((bf16[128,2,640]{2,1,0:T(2,128)(2,1)}), bf16[128,2,640]{2,1,0:T(2,128)(2,1)S(1)}, u32[]{:S(2)}, u32[]{:S(2)}) async-start(bf16[128,2,640]{2,1,0:T(2,128)(2,1)} %reshape.45), calls=%async_computation.1 | async-start | bytes 655360 | tf_op jit(solution)/shard_map/all_to_all | solution.py:303
  31.4 2.8 %collective-permute-start = (bf16[256,512]{1,0:T(8,128)(2,1)S(1)}, bf16[256,512]{1,0:T(8,128)(2,1)S(1)}, u32[]{:S(2)}, u32[]{:S(2)}) collective-permute-start(bf16[256,512]{1,0:T(8,128)(2,1)S(1)} %get-tuple-element.77), channel_id=1, source_target_pairs={{0,16},{16,0},{32,48},{48,32},{64,80},{80,64},{96,112},{112,96},{1... | collective-permute-start | bytes 786440 | tf_op jit(solution)/shard_map/ppermute | solution.py:359
  31.5 2.7 %collective-permute-start.1 = (bf16[256,512]{1,0:T(8,128)(2,1)S(1)}, bf16[256,512]{1,0:T(8,128)(2,1)S(1)}, u32[]{:S(2)}, u32[]{:S(2)}) collective-permute-start(bf16[256,512]{1,0:T(8,128)(2,1)S(1)} %get-tuple-element.78), channel_id=1, source_target_pairs={{0,16},{16,0},{32,48},{48,32},{64,80},{80,64},{96,112},{112,96},{1... | collective-permute-start | bytes 786440 | tf_op jit(solution)/shard_map/ppermute | solution.py:359
  32.0 2.3 %collective-permute-start.2 = (bf16[256,512]{1,0:T(8,128)(2,1)S(1)}, bf16[256,512]{1,0:T(8,128)(2,1)S(1)}, u32[]{:S(2)}, u32[]{:S(2)}) collective-permute-start(bf16[256,512]{1,0:T(8,128)(2,1)S(1)} %get-tuple-element.79), channel_id=1, source_target_pairs={{0,16},{16,0},{32,48},{48,32},{64,80},{80,64},{96,112},{112,96},{1... | collective-permute-start | bytes 786440 | tf_op jit(solution)/shard_map/ppermute | solution.py:359
  32.1 2.2 %collective-permute-start.3 = (bf16[256,512]{1,0:T(8,128)(2,1)S(1)}, bf16[256,512]{1,0:T(8,128)(2,1)S(1)}, u32[]{:S(2)}, u32[]{:S(2)}) collective-permute-start(bf16[256,512]{1,0:T(8,128)(2,1)S(1)} %get-tuple-element.80), channel_id=1, source_target_pairs={{0,16},{16,0},{32,48},{48,32},{64,80},{80,64},{96,112},{112,96},{1... | collective-permute-start | bytes 786440 | tf_op jit(solution)/shard_map/ppermute | solution.py:359
  32.5 1.7 %collective-permute-start.4 = (bf16[256,128]{1,0:T(8,128)(2,1)S(1)}, bf16[256,128]{1,0:T(8,128)(2,1)S(1)}, u32[]{:S(2)}, u32[]{:S(2)}) collective-permute-start(bf16[256,128]{1,0:T(8,128)(2,1)S(1)} %get-tuple-element.76.refs_4_), channel_id=1, source_target_pairs={{0,16},{16,0},{32,48},{48,32},{64,80},{80,64},{96,112},{112,96},{1... | collective-permute-start | bytes 196616 | tf_op jit(solution)/shard_map/ppermute | solution.py:359
  35.1 18.3 %collective-permute-start.5 = (bf16[64,2176]{1,0:T(8,128)(2,1)S(1)}, bf16[64,2176]{1,0:T(8,128)(2,1)S(1)}, u32[]{:S(2)}, u32[]{:S(2)}) collective-permute-start(bf16[64,2176]{1,0:T(8,128)(2,1)S(1)} %get-tuple-element.82), channel_id=1, source_target_pairs={{0,32},{16,48},{32,64},{48,80},{64,96},{80,112},{96,0},{112,16},{1... | collective-permute-start | bytes 835592 | tf_op jit(solution)/shard_map/ppermute | solution.py:374
  36.3 17.1 %collective-permute-start.6 = (bf16[64,2176]{1,0:T(8,128)(2,1)S(1)}, bf16[64,2176]{1,0:T(8,128)(2,1)S(1)}, u32[]{:S(2)}, u32[]{:S(2)}) collective-permute-start(bf16[64,2176]{1,0:T(8,128)(2,1)S(1)} %get-tuple-element.83), channel_id=1, source_target_pairs={{0,64},{16,80},{32,96},{48,112},{64,0},{80,16},{96,32},{112,48},{1... | collective-permute-start | bytes 835592 | tf_op jit(solution)/shard_map/ppermute | solution.py:374
  39.5 13.9 %collective-permute-start.7 = (bf16[64,2176]{1,0:T(8,128)(2,1)S(1)}, bf16[64,2176]{1,0:T(8,128)(2,1)S(1)}, u32[]{:S(2)}, u32[]{:S(2)}) collective-permute-start(bf16[64,2176]{1,0:T(8,128)(2,1)S(1)} %get-tuple-element.84), channel_id=1, source_target_pairs={{0,96},{16,112},{32,0},{48,16},{64,32},{80,48},{96,64},{112,80},{1... | collective-permute-start | bytes 835592 | tf_op jit(solution)/shard_map/ppermute | solution.py:374
  48.0 16.3 %all-to-all-start.2 = ((bf16[128,2,512]{2,1,0:T(2,128)(2,1)}), bf16[128,2,512]{2,1,0:T(2,128)(2,1)S(1)}, u32[]{:S(2)}, u32[]{:S(2)}) async-start(bf16[128,2,512]{2,1,0:T(2,128)(2,1)} %bitcast.8), calls=%async_computation.2 | async-start | bytes 524288 | tf_op jit(solution)/shard_map/all_to_all | solution.py:303
  53.7 10.7 %collective-permute-start.8 = (bf16[64,1024]{1,0:T(8,128)(2,1)S(1)}, bf16[64,1024]{1,0:T(8,128)(2,1)S(1)}, u32[]{:S(2)}, u32[]{:S(2)}) collective-permute-start(bf16[64,1024]{1,0:T(8,128)(2,1)S(1)} %shard_map.115.refs_0_), channel_id=1, source_target_pairs={{0,16},{16,0},{32,48},{48,32},{64,80},{80,64},{96,112},{112,96},{1... | collective-permute-start | bytes 393224 | tf_op jit(solution)/shard_map/ppermute | solution.py:397
  53.8 13.3 %collective-permute-start.11 = (bf16[64,1024]{1,0:T(8,128)(2,1)S(1)}, bf16[64,1024]{1,0:T(8,128)(2,1)S(1)}, u32[]{:S(2)}, u32[]{:S(2)}) collective-permute-start(bf16[64,1024]{1,0:T(8,128)(2,1)S(1)} %shard_map.115.refs_0_), channel_id=1, source_target_pairs={{0,64},{16,80},{32,96},{48,112},{64,0},{80,16},{96,32},{112,48},{1... | collective-permute-start | bytes 393224 | tf_op jit(solution)/shard_map/ppermute | solution.py:396
  56.8 10.2 %collective-permute-start.13 = (bf16[64,1024]{1,0:T(8,128)(2,1)S(1)}, bf16[64,1024]{1,0:T(8,128)(2,1)S(1)}, u32[]{:S(2)}, u32[]{:S(2)}) collective-permute-start(bf16[64,1024]{1,0:T(8,128)(2,1)S(1)} %shard_map.115.refs_0_), channel_id=1, source_target_pairs={{0,96},{16,112},{32,0},{48,16},{64,32},{80,48},{96,64},{112,80},{1... | collective-permute-start | bytes 393224 | tf_op jit(solution)/shard_map/ppermute | solution.py:396
  57.7 9.9 %collective-permute-start.9 = (bf16[64,1024]{1,0:T(8,128)(2,1)S(1)}, bf16[64,1024]{1,0:T(8,128)(2,1)S(1)}, u32[]{:S(2)}, u32[]{:S(2)}) collective-permute-start(bf16[64,1024]{1,0:T(8,128)(2,1)S(1)} %shard_map.115.refs_0_), channel_id=1, source_target_pairs={{0,32},{16,48},{32,64},{48,80},{64,96},{80,112},{96,0},{112,16},{1... | collective-permute-start | bytes 393224 | tf_op jit(solution)/shard_map/ppermute | solution.py:396
  67.0 2.2 %collective-permute-start.14 = (bf16[64,1024]{1,0:T(8,128)(2,1)S(1)}, bf16[64,1024]{1,0:T(8,128)(2,1)S(1)}, u32[]{:S(2)}, u32[]{:S(2)}) collective-permute-start(bf16[64,1024]{1,0:T(8,128)(2,1)S(1)} %collective-permute-done.13.refs_3_), channel_id=1, source_target_pairs={{0,16},{16,0},{32,48},{48,32},{64,80},{80,64},{96,112},{112,96},{1... | collective-permute-start | bytes 393224 | tf_op jit(solution)/shard_map/ppermute | solution.py:401
  67.2 2.1 %collective-permute-start.12 = (bf16[64,1024]{1,0:T(8,128)(2,1)S(1)}, bf16[64,1024]{1,0:T(8,128)(2,1)S(1)}, u32[]{:S(2)}, u32[]{:S(2)}) collective-permute-start(bf16[64,1024]{1,0:T(8,128)(2,1)S(1)} %collective-permute-done.11.refs_2_), channel_id=1, source_target_pairs={{0,16},{16,0},{32,48},{48,32},{64,80},{80,64},{96,112},{112,96},{1... | collective-permute-start | bytes 393224 | tf_op jit(solution)/shard_map/ppermute | solution.py:401
  67.6 1.6 collective-permute-start.10
  67.9 19.1 %copy-start.7 = (f32[16,1024]{1,0:T(8,128)S(1)}, f32[16,1024]{1,0:T(8,128)}, u32[]{:S(2)}) copy-start(f32[16,1024]{1,0:T(8,128)} %x_ref.1) | copy-start | bytes 196612
  69.2 32.2 %copy-start.1 = (bf16[1024,2048]{1,0:T(8,128)(2,1)S(1)}, bf16[1024,2048]{1,0:T(8,128)(2,1)}, u32[]{:S(2)}) copy-start(bf16[1024,2048]{1,0:T(8,128)(2,1)} %wg_ref.7) | copy-start | bytes 12582916
  69.2 32.2 %copy-start.3 = (bf16[1024,2048]{1,0:T(8,128)(2,1)S(1)}, bf16[1024,2048]{1,0:T(8,128)(2,1)}, u32[]{:S(2)}) copy-start(bf16[1024,2048]{1,0:T(8,128)(2,1)} %wu_ref.7) | copy-start | bytes 12582916
  102.7 1.3 copy-start.4
  105.4 16.9 %all-to-all-start.5 = ((bf16[128,2,640]{2,1,0:T(2,128)(2,1)}), bf16[128,2,640]{2,1,0:T(2,128)(2,1)S(1)}, u32[]{:S(2)}, u32[]{:S(2)}) async-start(bf16[128,2,640]{2,1,0:T(2,128)(2,1)} %reshape.51), calls=%async_computation.5 | async-start | bytes 655360 | tf_op jit(solution)/shard_map/all_to_all | solution.py:303
  110.8 2.8 %collective-permute-start.15 = (bf16[256,512]{1,0:T(8,128)(2,1)S(1)}, bf16[256,512]{1,0:T(8,128)(2,1)S(1)}, u32[]{:S(2)}, u32[]{:S(2)}) collective-permute-start(bf16[256,512]{1,0:T(8,128)(2,1)S(1)} %get-tuple-element.106), channel_id=1, source_target_pairs={{0,16},{16,0},{32,48},{48,32},{64,80},{80,64},{96,112},{112,96},{1... | collective-permute-start | bytes 786440 | tf_op jit(solution)/shard_map/ppermute | solution.py:359
  110.9 2.7 %collective-permute-start.16 = (bf16[256,512]{1,0:T(8,128)(2,1)S(1)}, bf16[256,512]{1,0:T(8,128)(2,1)S(1)}, u32[]{:S(2)}, u32[]{:S(2)}) collective-permute-start(bf16[256,512]{1,0:T(8,128)(2,1)S(1)} %get-tuple-element.107), channel_id=1, source_target_pairs={{0,16},{16,0},{32,48},{48,32},{64,80},{80,64},{96,112},{112,96},{1... | collective-permute-start | bytes 786440 | tf_op jit(solution)/shard_map/ppermute | solution.py:359
  111.4 2.3 %collective-permute-start.17 = (bf16[256,512]{1,0:T(8,128)(2,1)S(1)}, bf16[256,512]{1,0:T(8,128)(2,1)S(1)}, u32[]{:S(2)}, u32[]{:S(2)}) collective-permute-start(bf16[256,512]{1,0:T(8,128)(2,1)S(1)} %get-tuple-element.108), channel_id=1, source_target_pairs={{0,16},{16,0},{32,48},{48,32},{64,80},{80,64},{96,112},{112,96},{1... | collective-permute-start | bytes 786440 | tf_op jit(solution)/shard_map/ppermute | solution.py:359
  111.4 2.2 %collective-permute-start.18 = (bf16[256,512]{1,0:T(8,128)(2,1)S(1)}, bf16[256,512]{1,0:T(8,128)(2,1)S(1)}, u32[]{:S(2)}, u32[]{:S(2)}) collective-permute-start(bf16[256,512]{1,0:T(8,128)(2,1)S(1)} %get-tuple-element.109), channel_id=1, source_target_pairs={{0,16},{16,0},{32,48},{48,32},{64,80},{80,64},{96,112},{112,96},{1... | collective-permute-start | bytes 786440 | tf_op jit(solution)/shard_map/ppermute | solution.py:359
  111.9 1.7 %collective-permute-start.19 = (bf16[256,128]{1,0:T(8,128)(2,1)S(1)}, bf16[256,128]{1,0:T(8,128)(2,1)S(1)}, u32[]{:S(2)}, u32[]{:S(2)}) collective-permute-start(bf16[256,128]{1,0:T(8,128)(2,1)S(1)} %get-tuple-element.105.refs_4_), channel_id=1, source_target_pairs={{0,16},{16,0},{32,48},{48,32},{64,80},{80,64},{96,112},{112,96},{1... | collective-permute-start | bytes 196616 | tf_op jit(solution)/shard_map/ppermute | solution.py:359
  114.5 18.5 %collective-permute-start.20 = (bf16[64,2176]{1,0:T(8,128)(2,1)S(1)}, bf16[64,2176]{1,0:T(8,128)(2,1)S(1)}, u32[]{:S(2)}, u32[]{:S(2)}) collective-permute-start(bf16[64,2176]{1,0:T(8,128)(2,1)S(1)} %get-tuple-element.111), channel_id=1, source_target_pairs={{0,32},{16,48},{32,64},{48,80},{64,96},{80,112},{96,0},{112,16},{1... | collective-permute-start | bytes 835592 | tf_op jit(solution)/shard_map/ppermute | solution.py:374
  115.6 17.3 %collective-permute-start.21 = (bf16[64,2176]{1,0:T(8,128)(2,1)S(1)}, bf16[64,2176]{1,0:T(8,128)(2,1)S(1)}, u32[]{:S(2)}, u32[]{:S(2)}) collective-permute-start(bf16[64,2176]{1,0:T(8,128)(2,1)S(1)} %get-tuple-element.112), channel_id=1, source_target_pairs={{0,64},{16,80},{32,96},{48,112},{64,0},{80,16},{96,32},{112,48},{1... | collective-permute-start | bytes 835592 | tf_op jit(solution)/shard_map/ppermute | solution.py:374
  118.8 14.1 %collective-permute-start.22 = (bf16[64,2176]{1,0:T(8,128)(2,1)S(1)}, bf16[64,2176]{1,0:T(8,128)(2,1)S(1)}, u32[]{:S(2)}, u32[]{:S(2)}) collective-permute-start(bf16[64,2176]{1,0:T(8,128)(2,1)S(1)} %get-tuple-element.113), channel_id=1, source_target_pairs={{0,96},{16,112},{32,0},{48,16},{64,32},{80,48},{96,64},{112,80},{1... | collective-permute-start | bytes 835592 | tf_op jit(solution)/shard_map/ppermute | solution.py:374
  127.5 16.3 %all-to-all-start.6 = ((bf16[128,2,512]{2,1,0:T(2,128)(2,1)}), bf16[128,2,512]{2,1,0:T(2,128)(2,1)S(1)}, u32[]{:S(2)}, u32[]{:S(2)}) async-start(bf16[128,2,512]{2,1,0:T(2,128)(2,1)} %bitcast.14), calls=%async_computation.6 | async-start | bytes 524288 | tf_op jit(solution)/shard_map/all_to_all | solution.py:303
  133.3 10.7 %collective-permute-start.23 = (bf16[64,1024]{1,0:T(8,128)(2,1)S(1)}, bf16[64,1024]{1,0:T(8,128)(2,1)S(1)}, u32[]{:S(2)}, u32[]{:S(2)}) collective-permute-start(bf16[64,1024]{1,0:T(8,128)(2,1)S(1)} %shard_map.125.refs_0_), channel_id=1, source_target_pairs={{0,16},{16,0},{32,48},{48,32},{64,80},{80,64},{96,112},{112,96},{1... | collective-permute-start | bytes 393224 | tf_op jit(solution)/shard_map/ppermute | solution.py:397
  133.4 13.8 %collective-permute-start.24 = (bf16[64,1024]{1,0:T(8,128)(2,1)S(1)}, bf16[64,1024]{1,0:T(8,128)(2,1)S(1)}, u32[]{:S(2)}, u32[]{:S(2)}) collective-permute-start(bf16[64,1024]{1,0:T(8,128)(2,1)S(1)} %shard_map.125.refs_0_), channel_id=1, source_target_pairs={{0,32},{16,48},{32,64},{48,80},{64,96},{80,112},{96,0},{112,16},{1... | collective-permute-start | bytes 393224 | tf_op jit(solution)/shard_map/ppermute | solution.py:396
  134.6 12.1 %collective-permute-start.26 = (bf16[64,1024]{1,0:T(8,128)(2,1)S(1)}, bf16[64,1024]{1,0:T(8,128)(2,1)S(1)}, u32[]{:S(2)}, u32[]{:S(2)}) collective-permute-start(bf16[64,1024]{1,0:T(8,128)(2,1)S(1)} %shard_map.125.refs_0_), channel_id=1, source_target_pairs={{0,64},{16,80},{32,96},{48,112},{64,0},{80,16},{96,32},{112,48},{1... | collective-permute-start | bytes 393224 | tf_op jit(solution)/shard_map/ppermute | solution.py:396
  137.8 8.8 %collective-permute-start.28 = (bf16[64,1024]{1,0:T(8,128)(2,1)S(1)}, bf16[64,1024]{1,0:T(8,128)(2,1)S(1)}, u32[]{:S(2)}, u32[]{:S(2)}) collective-permute-start(bf16[64,1024]{1,0:T(8,128)(2,1)S(1)} %shard_map.125.refs_0_), channel_id=1, source_target_pairs={{0,96},{16,112},{32,0},{48,16},{64,32},{80,48},{96,64},{112,80},{1... | collective-permute-start | bytes 393224 | tf_op jit(solution)/shard_map/ppermute | solution.py:396
  146.6 2.0 %collective-permute-start.29 = (bf16[64,1024]{1,0:T(8,128)(2,1)S(1)}, bf16[64,1024]{1,0:T(8,128)(2,1)S(1)}, u32[]{:S(2)}, u32[]{:S(2)}) collective-permute-start(bf16[64,1024]{1,0:T(8,128)(2,1)S(1)} %collective-permute-done.28.refs_3_), channel_id=1, source_target_pairs={{0,16},{16,0},{32,48},{48,32},{64,80},{80,64},{96,112},{112,96},{1... | collective-permute-start | bytes 393224 | tf_op jit(solution)/shard_map/ppermute | solution.py:401
  146.7 1.9 %collective-permute-start.27 = (bf16[64,1024]{1,0:T(8,128)(2,1)S(1)}, bf16[64,1024]{1,0:T(8,128)(2,1)S(1)}, u32[]{:S(2)}, u32[]{:S(2)}) collective-permute-start(bf16[64,1024]{1,0:T(8,128)(2,1)S(1)} %collective-permute-done.26.refs_2_), channel_id=1, source_target_pairs={{0,16},{16,0},{32,48},{48,32},{64,80},{80,64},{96,112},{112,96},{1... | collective-permute-start | bytes 393224 | tf_op jit(solution)/shard_map/ppermute | solution.py:401
  147.2 1.4 collective-permute-start.25
